TPU v7x, 128 devices: a whole 4x4x4 slice. The times are simulated.
128 devices in a mesh: point: 8 (over x, core), cent: 16 (over z, y).
Axes of the slice: x: 4, y: 4, z: 4, core: 2. Of those that a mesh axis runs over, the one named last changes fastest.
Arguments:
- points: bfloat16 [262144, 1024], P(('point', 'cent')), may hold values from -200 to 200
- cluster_ids: int32 [262144], P(('point', 'cent')), may hold values from 0 to 31, as said below
- owner_slot: int32 [32], replicated, may hold values from 0 to 31, as said below
- centroids: bfloat16 [32, 256, 1024], P('point', 'cent'), may hold values from -0.8 to 0.8
Outputs:
- new_centroids: bfloat16 [32, 256, 1024], P('point', 'cent')
- centroid_mass: float32 [32, 256], P('point', 'cent')
Inputs may be any that keep to these rules, and one draw needn't show every extreme that they name: `cluster_ids`: cluster of each point. Among the 2048 points of one device at most 128 lie in any one level-one cluster, and in every draw, for each index of cent there is one owner (point index) such that each of that owner's 4 clusters receives exactly 128 points from every device with that cent index; every other cluster receives fewer than 128 from each device. Each block row once: a permutation. Cluster c belongs to point index owner_slot[c] // 4.
All inputs are finite; a program needn't handle non-finite values.
Results may differ from a plain program's by a relative error of at most 0.0063.
Values may be sent and summed in bfloat16 or wider, within the bound.
No kernel may reach another device: no remote copies, remote signals or barrier semaphores. Data moves between devices by JAX's collectives and lax.ppermute only.
A program may use at most 128 MiB of HBM per device.

v0:
```python
import jax
import jax.numpy as jnp
from jax import lax
from jax.sharding import PartitionSpec as P

ITERS = 2


score_scale = 0.25
prior_weight = 1.0


def responsibilities(received, present, full_blocks):
    squares = jnp.sum(jnp.square(full_blocks.astype(jnp.float32)), axis=-1)
    products = jnp.einsum(
        "pjcd,jkd->pjck", received, full_blocks, preferred_element_type=jnp.float32
    )
    scores = (products - 0.5 * squares[None, :, None, :]) * score_scale
    weights = jax.nn.softmax(scores, axis=-1) * present[..., None]
    totals = jnp.einsum(
        "pjck,pjcd->jkd", weights.astype(jnp.bfloat16), received, preferred_element_type=jnp.float32
    )
    masses = jnp.sum(weights, axis=(0, 2))
    return (totals, masses)


def refine(totals, masses, centers):
    updated = (totals + prior_weight * centers.astype(jnp.float32)) / (
        masses[..., None] + prior_weight
    )
    return updated.astype(jnp.bfloat16)


def shards(points, cluster_ids, owner_slot, centroids):
    point_count = lax.axis_size("point")
    local_rows, feature_width = points.shape
    cluster_total = owner_slot.shape[0]
    per_owner = cluster_total // point_count
    capacity = 2 * local_rows // cluster_total
    cluster_table = jnp.arange(cluster_total, dtype=jnp.int32)
    member_of = cluster_ids[:, None] == cluster_table[None, :]
    block_of = jnp.sum(jnp.where(member_of, owner_slot[None, :], 0), axis=1)
    one_hot = (block_of[:, None] == cluster_table[None, :]).astype(jnp.int32)
    before = jnp.cumsum(one_hot, axis=0) - one_hot
    position = jnp.sum(before * one_hot, axis=1)
    target = block_of * capacity + position
    outgoing = (
        jnp.zeros((cluster_total * capacity, feature_width), jnp.bfloat16).at[target].set(points)
    )
    occupied = (
        jnp.zeros((cluster_total * capacity,), jnp.bfloat16)
        .at[target]
        .set(jnp.ones((local_rows,), jnp.bfloat16))
    )
    outgoing = outgoing.reshape(point_count, per_owner * capacity, feature_width)
    occupied = occupied.reshape(point_count, per_owner * capacity)
    received, arrived = (
        lax.all_to_all(outgoing, "point", split_axis=0, concat_axis=0, tiled=True),
        lax.all_to_all(occupied, "point", split_axis=0, concat_axis=0, tiled=True),
    )
    received = received.reshape(point_count, per_owner, capacity, feature_width)
    present = arrived.reshape(point_count, per_owner, capacity).astype(jnp.float32)
    own_blocks = centroids
    part_masses = jnp.zeros(centroids.shape[:2], jnp.float32)
    for iteration in range(ITERS):
        full_blocks = lax.all_gather(own_blocks, "cent", axis=1, tiled=True)
        totals, masses = responsibilities(received, present, full_blocks)
        part_totals, part_masses = (
            lax.psum_scatter(totals, "cent", scatter_dimension=1, tiled=True),
            lax.psum_scatter(masses, "cent", scatter_dimension=1, tiled=True),
        )
        own_blocks = refine(part_totals, part_masses, own_blocks)
    return (own_blocks, part_masses)


def solution(mesh):
    return jax.shard_map(
        shards,
        mesh=mesh,
        in_specs=(P(("point", "cent"), None), P(("point", "cent")), P(), P("point", "cent", None)),
        out_specs=(P("point", "cent", None), P("point", "cent")),
        check_vma=False,
    )
```

profile of v0, /device:TPU:2, one launch (start us, length us, event | category | flops | bytes accessed | tf_op | source)
XLA Modules:
  0.0 401.5 jit_solution(8172812431339845163)
XLA Ops:
  7.2 0.8 select_reduce_fusion
  8.0 9.1 %reduce-window.6 = s32[32,16,128]{2,1,0:T(8,128)S(1)} reduce-window(s32[32,16,128]{2,1,0:T(8,128)S(1)} %fusion.39, s32[]{:T(128)} %constant.11.clone.1), window={size=1x1x128 pad=0_0x0_0x127_0}, to_apply=%region_1.2 | reduce-window | flops 8323072 | bytes 524292 | tf_op jit(solution)/shard_map/reduce-window
  17.1 0.1 slice.8
  17.2 0.2 copy.36
  17.5 0.2 reduce-window.9
  17.7 0.1 broadcast_add_fusion
  17.8 0.1 fusion.38
  18.0 14.6 %scatter_custom_fusion.1 = bf16[4096]{0:T(1024)(128)(2,1)S(1)} fusion(s32[2048]{0:T(1024)S(1)} %bitcast.77, bf16[2048]{0:T(1024)(128)(2,1)S(1)} %broadcast.86, bf16[]{:T(256)} %constant.10.clone.1), kind=kCustom, calls=%fused_computation.55 | custom fusion | bytes 8194 | tf_op jit(solution)/shard_map/scatter | solution.py:53
  32.6 0.5 broadcast.108
  33.1 0.7 reduce
  33.8 0.6 reshape.117
  34.4 4.8 %all-to-all-start.1 = ((bf16[8,2,256]{2,1,0:T(2,128)(2,1)}), bf16[8,2,256]{2,1,0:T(2,128)(2,1)S(1)}, u32[]{:S(2)}, u32[]{:S(2)}) async-start(bf16[8,2,256]{2,1,0:T(2,128)(2,1)} %reshape.117), calls=%async_computation.1 | async-start | bytes 16384 | tf_op jit(solution)/shard_map/all_to_all | solution.py:59
  39.2 15.2 %scatter_custom_fusion = bf16[4096,1024]{1,0:T(8,128)(2,1)} fusion(s32[2048]{0:T(1024)S(1)} %bitcast.78, bf16[2048,1024]{1,0:T(8,128)(2,1)} %param.4, bf16[]{:T(256)} %constant.10.clone.1), kind=kCustom, calls=%fused_computation.26 | custom fusion | bytes 8389120 | tf_op jit(solution)/shard_map/scatter | solution.py:48
  54.5 0.0 all-to-all-done.1
  54.5 4.9 %all-to-all-start = ((bf16[8,512,1024]{2,1,0:T(8,128)(2,1)}), bf16[8,512,1024]{2,1,0:T(8,128)(2,1)}, u32[]{:S(2)}, u32[]{:S(2)}) async-start(bf16[8,512,1024]{2,1,0:T(8,128)(2,1)} %bitcast.71), calls=%async_computation | async-start | bytes 16777216 | tf_op jit(solution)/shard_map/all_to_all | solution.py:58
  59.4 0.0 all-gather.3.cloned.1.call-start
  59.4 0.7 all-gather.3.cloned.1.call-update
  60.1 0.2 reduce-scatter.5.cloned.1.call-start
  60.4 49.6 %all-gather.3.cloned.1.call-done = bf16[4,256,1024]{2,1,0:T(8,128)(2,1)} async-done(((bf16[4,16,1024]{2,1,0:T(8,128)(2,1)}), bf16[4,256,1024]{2,1,0:T(8,128)(2,1)}) %all-gather.3.cloned.1.call-update) | async-done | bytes 2097168 | tf_op jit(solution)/shard_map/all_gather | solution.py:66
  110.0 2.1 multiply_reduce_fusion.1
  112.1 40.5 %all-to-all-done = bf16[8,512,1024]{2,1,0:T(8,128)(2,1)} async-done(((bf16[8,512,1024]{2,1,0:T(8,128)(2,1)}), bf16[8,512,1024]{2,1,0:T(8,128)(2,1)}, u32[]{:S(2)}, u32[]{:S(2)}) %all-to-all-start) | async-done | bytes 8388640 | tf_op jit(solution)/shard_map/all_to_all | solution.py:58
  152.6 6.3 %fusion.8 = f32[4,8,128,256]{3,2,1,0:T(8,128)S(1)} fusion(bf16[8,4,128,1024]{3,2,1,0:T(8,128)(2,1)} %bitcast.7, bf16[4,256,1024]{2,1,0:T(8,128)(2,1)} %all-gather.3.cloned.1.call-done), kind=kOutput, calls=%fused_computation.10 | convolution fusion | flops 2147483648 | bytes 14680064 | tf_op jit(solution)/shard_map/pjcd,jkd->pjck/dot_general | solution.py:15
  159.0 1.8 fusion.44
  160.8 0.0 copy-start
  160.8 1.9 copy-done
  162.7 7.1 %fusion.20 = f32[4,256,1024]{2,1,0:T(8,128)} fusion(bf16[8,4,128,1024]{3,2,1,0:T(8,128)(2,1)} %bitcast.7, f32[8,4,128,256]{3,2,0,1:T(8,128)S(1)} %get-tuple-element.5, f32[8,4,128]{2,0,1:T(8,128)S(1)} %bitcast_convert_fusion, f32[8,4,128]{2,0,1:T(8,128)S(1)} %get-tuple-element.4), kind=kOutput, calls=%fused_computation.28 | convolution fusion | flops 2150629376 | bytes 16809984 | tf_op jit(solution)/shard_map/pjck,pjcd->jkd/dot_general | solution.py:20
  169.8 0.0 copy-start.4
  169.8 0.0 copy-start.3
  169.8 0.0 reduce-scatter.5.cloned.1.call-update
  169.9 0.0 all-gather.5.cloned.1.call-start
  169.9 0.6 copy-done.4
  170.5 0.6 dynamic-slice
  171.7 2.9 fusion.34
  174.6 42.2 %all-reduce = f32[4,256]{1,0:T(4,128)S(1)} all-reduce(f32[4,256]{1,0:T(4,128)S(1)} %fusion.34), channel_id=3, replica_groups=mesh['point'=8,'cent'=16] {'cent'}, use_global_device_ids=true, to_apply=%region_11.12.clone | all-reduce | flops 1024 | bytes 8192
  216.8 0.1 dynamic-slice_add_fusion
  216.9 32.3 %reduce-scatter.5.cloned.1.call-done = f32[4,16,1024]{2,1,0:T(8,128)} async-done(((f32[4,256,1024]{2,1,0:T(8,128)}), f32[4,16,1024]{2,1,0:T(8,128)}) %reduce-scatter.5.cloned.1.call-update) | async-done | bytes 262160 | tf_op jit(solution)/shard_map/reduce_scatter | solution.py:69
  249.2 0.0 copy-done.3
  249.2 1.7 divide_convert_fusion.1
  250.9 0.0 all-gather.5.cloned.1.call-update
  251.0 0.0 reduce-scatter.7.cloned.1.call-start
  251.0 45.7 %all-gather.5.cloned.1.call-done = bf16[4,256,1024]{2,1,0:T(8,128)(2,1)} async-done(((bf16[4,16,1024]{2,1,0:T(8,128)(2,1)}), bf16[4,256,1024]{2,1,0:T(8,128)(2,1)}) %all-gather.5.cloned.1.call-update) | async-done | bytes 2097168 | tf_op jit(solution)/shard_map/all_gather | solution.py:66
  296.7 2.1 multiply_reduce_fusion
  298.8 6.4 %fusion.4 = f32[4,256,8,128]{1,3,2,0:T(8,128)S(1)} fusion(bf16[8,4,128,1024]{3,2,1,0:T(8,128)(2,1)} %bitcast.7, bf16[4,256,1024]{2,1,0:T(8,128)(2,1)} %all-gather.5.cloned.1.call-done), kind=kOutput, calls=%fused_computation.6 | convolution fusion | flops 2147483648 | bytes 14680064 | tf_op jit(solution)/shard_map/pjcd,jkd->pjck/dot_general | solution.py:15
  305.2 1.8 fusion.45
  307.0 0.0 copy-start.1
  307.0 1.9 copy-done.1
  309.0 7.1 %fusion.23 = f32[4,256,1024]{2,1,0:T(8,128)} fusion(bf16[8,4,128,1024]{3,2,1,0:T(8,128)(2,1)} %bitcast.7, f32[8,4,128,256]{3,2,0,1:T(8,128)S(1)} %get-tuple-element.7, f32[8,4,128]{2,0,1:T(8,128)S(1)} %get-tuple-element.6, f32[8,4,128]{2,0,1:T(8,128)S(1)} %bitcast_convert_fusion), kind=kOutput, calls=%fused_computation.29 | convolution fusion | flops 2150629376 | bytes 16809984 | tf_op jit(solution)/shard_map/pjck,pjcd->jkd/dot_general | solution.py:20
  316.1 0.0 copy-start.2
  316.1 0.0 reduce-scatter.7.cloned.1.call-update
  316.1 2.9 fusion.35
  319.0 38.5 %all-reduce.1 = f32[4,256]{1,0:T(4,128)S(1)} all-reduce(f32[4,256]{1,0:T(4,128)S(1)} %fusion.35), channel_id=5, replica_groups=mesh['point'=8,'cent'=16] {'cent'}, use_global_device_ids=true, to_apply=%region_17.18.clone | all-reduce | flops 1024 | bytes 8192
  357.4 0.7 broadcast_add_fusion.1
  358.1 35.2 %reduce-scatter.7.cloned.1.call-done = f32[4,16,1024]{2,1,0:T(8,128)} async-done(((f32[4,256,1024]{2,1,0:T(8,128)}), f32[4,16,1024]{2,1,0:T(8,128)}) %reduce-scatter.7.cloned.1.call-update) | async-done | bytes 262160 | tf_op jit(solution)/shard_map/reduce_scatter | solution.py:69
  393.3 0.0 copy-done.2
  393.3 1.7 divide_convert_fusion
  (9 shorter events, 0.1 us)
Async XLA Ops:
  34.4 20.1 %all-to-all-start.1 = ((bf16[8,2,256]{2,1,0:T(2,128)(2,1)}), bf16[8,2,256]{2,1,0:T(2,128)(2,1)S(1)}, u32[]{:S(2)}, u32[]{:S(2)}) async-start(bf16[8,2,256]{2,1,0:T(2,128)(2,1)} %reshape.117), calls=%async_computation.1 | async-start | bytes 16384 | tf_op jit(solution)/shard_map/all_to_all | solution.py:59
  54.5 98.1 %all-to-all-start = ((bf16[8,512,1024]{2,1,0:T(8,128)(2,1)}), bf16[8,512,1024]{2,1,0:T(8,128)(2,1)}, u32[]{:S(2)}, u32[]{:S(2)}) async-start(bf16[8,512,1024]{2,1,0:T(8,128)(2,1)} %bitcast.71), calls=%async_computation | async-start | bytes 16777216 | tf_op jit(solution)/shard_map/all_to_all | solution.py:58
  59.4 50.6 %all-gather.3.cloned.1.call-start = ((), (), s32[]{:S(2)}) async-start(), calls=%async_computation.4 | async-start | bytes 2228224 | tf_op jit(solution)/shard_map/all_gather | solution.py:66
  60.1 189.1 %reduce-scatter.5.cloned.1.call-start = ((), (), s32[]{:S(2)}) async-start(), calls=%async_computation.5 | async-start | bytes 4456448 | tf_op jit(solution)/shard_map/reduce_scatter | solution.py:69
  160.8 2.0 copy-start
  169.8 0.7 copy-start.4
  169.8 79.4 %copy-start.3 = (bf16[4,16,1024]{2,1,0:T(8,128)(2,1)S(1)}, bf16[4,16,1024]{2,1,0:T(8,128)(2,1)}, u32[]{:S(2)}) copy-start(bf16[4,16,1024]{2,1,0:T(8,128)(2,1)} %param.7) | copy-start | bytes 393220
  169.9 126.9 %all-gather.5.cloned.1.call-start = ((), (), s32[]{:S(2)}) async-start(), calls=%async_computation.6 | async-start | bytes 2228224 | tf_op jit(solution)/shard_map/all_gather | solution.py:66
  251.0 142.4 %reduce-scatter.7.cloned.1.call-start = ((), (), s32[]{:S(2)}) async-start(), calls=%async_computation.7 | async-start | bytes 4456448 | tf_op jit(solution)/shard_map/reduce_scatter | solution.py:69
  307.0 2.0 copy-start.1
  316.1 77.3 %copy-start.2 = (bf16[4,16,1024]{2,1,0:T(8,128)(2,1)S(1)}, bf16[4,16,1024]{2,1,0:T(8,128)(2,1)}, u32[]{:S(2)}) copy-start(bf16[4,16,1024]{2,1,0:T(8,128)(2,1)} %divide_convert_fusion.1) | copy-start | bytes 393220
Sparse Core Ops, SparseCore 0:
  62.4 47.6 all-gather.2
  170.0 79.2 reduce-scatter.4
  252.2 44.5 all-gather.4
  316.2 77.0 reduce-scatter.6
where the time goes:
time: 402 us
  waiting for transfers between devices  204 us (51%)
  blocking collectives  80.7 us (20%)
  local copies, waits for them, and re-layouts  36.4 us (9%)
  other arithmetic  28.6 us (7%)
  matrix products  27 us (7%)
  between operations  14.6 us (4%)
  starting transfers between devices  10.1 us (3%)
    all_gather x2, waiting for transfers between devices, shards(): full_blocks = lax.all_gather(own_blocks, 'cent', axis=1, tiled=True)  95.4 us
    unnamed x2, blocking collectives  80.7 us
    reduce_scatter x2, waiting for transfers between devices, shards(): lax.psum_scatter(totals, 'cent', scatter_dimension=1, tiled=True)  67.6 us
    all_to_all x1, waiting for transfers between devices, shards(): lax.all_to_all(outgoing, 'point', split_axis=0, concat_axis=0, tiled=True)  40.5 us
    scatter x1, local copies, waits for them, and re-layouts, shards(): jnp.zeros((cluster_total * capacity, feature_width), jnp.bfloat16)  15.2 us
    scatter x1, local copies, waits for them, and re-layouts, shards(): occupied = jnp.zeros((cluster_total * capacity,), jnp.bfloat16).at[target...  14.6 us
    dot_general x2, matrix products, responsibilities(): jnp.einsum('pjck,pjcd->jkd', weights.astype(jnp.bfloat16), received, pref...  14.2 us
    dot_general x2, matrix products, responsibilities(): jnp.einsum('pjcd,jkd->pjck', received, full_blocks, preferred_element_typ...  12.7 us
  transfers between devices with their start and end apart: 6, of which 5 were waited for; matrix products, arithmetic and copies ran while one was open for 6% of the time, Pallas kernels for 0%

commit v1 on v0

v1 whole, which is shorter than its diff:
```python
import functools

import jax
import jax.numpy as jnp
from jax import lax
from jax.experimental import pallas as pl
from jax.experimental.pallas import tpu as pltpu
from jax.sharding import PartitionSpec as P

ITERS = 2
SCORE_SCALE = 0.25
PRIOR_WEIGHT = 1.0
EXTRA = 128
MARK = 1024.0
MARK_LIMIT = 512.0
GROUP = 256
MIB = 1024 * 1024


def target_kernel(capacity, ids_ref, owner_ref, out_ref):
    clusters = owner_ref.shape[0]
    rows = ids_ref.shape[1]
    before = (
        lax.broadcasted_iota(jnp.int32, (GROUP, GROUP), 0)
        < lax.broadcasted_iota(jnp.int32, (GROUP, GROUP), 1)
    ).astype(jnp.float32).astype(jnp.bfloat16)
    table = lax.broadcasted_iota(jnp.int32, (clusters, GROUP), 0)
    base = (owner_ref[...] * capacity).astype(jnp.float32)
    for g in range(rows // GROUP):
        span = pl.ds(g * GROUP, GROUP)
        hit = (table == ids_ref[:, span]).astype(jnp.float32)
        place = jnp.dot(hit.astype(jnp.bfloat16), before, preferred_element_type=jnp.float32)
        out_ref[:, span] = jnp.sum(hit * (place + base), axis=0, keepdims=True).astype(jnp.int32)
        base = base + jnp.sum(hit, axis=1, keepdims=True)


def targets(cluster_ids, owner_slot, capacity):
    rows = cluster_ids.shape[0]
    return pl.pallas_call(
        functools.partial(target_kernel, capacity),
        out_shape=jax.ShapeDtypeStruct((1, rows), jnp.int32),
        name="targets",
    )(cluster_ids.reshape(1, rows), owner_slot.reshape(-1, 1))


def place_kernel(chunk, per_owner, capacity, owners_step, target_ref, points_ref, out_ref):
    rows = points_ref.shape[0]
    first = pl.program_id(0) * owners_step
    for o in range(owners_step):
        start = ((first + o) * per_owner + chunk) * capacity
        slot = lax.broadcasted_iota(jnp.int32, (capacity, rows), 0) + start
        pick = (slot == target_ref[...]).astype(jnp.float32)
        empty = 1.0 - jnp.sum(pick, axis=1, keepdims=True)
        lane = lax.broadcasted_iota(jnp.int32, (capacity, out_ref.shape[2]), 1)
        got = jnp.dot(pick.astype(jnp.bfloat16), points_ref[...], preferred_element_type=jnp.float32)
        out_ref[o] = (got + jnp.where(lane == 0, MARK * empty, 0.0)).astype(jnp.bfloat16)


def place(target, points, chunk, owners, per_owner, capacity):
    rows, width = points.shape
    step = 4
    return pl.pallas_call(
        functools.partial(place_kernel, chunk, per_owner, capacity, step),
        grid=(owners // step,),
        in_specs=[
            pl.BlockSpec((1, rows), lambda i: (0, 0)),
            pl.BlockSpec((rows, width), lambda i: (0, 0)),
        ],
        out_specs=pl.BlockSpec((step, capacity, width), lambda i: (i, 0, 0)),
        out_shape=jax.ShapeDtypeStruct((owners, capacity, width), jnp.bfloat16),
        compiler_params=pltpu.CompilerParams(vmem_limit_bytes=40 * MIB),
        cost_estimate=pl.CostEstimate(
            flops=2 * owners * capacity * rows * width,
            bytes_accessed=2 * width * (rows + owners * capacity),
            transcendentals=0,
        ),
        name="place",
    )(target, points)


def cluster_kernel(block_ref, rows_ref, out_ref, aug, total, mass, bias):
    step = pl.program_id(0)
    cents, width = block_ref.shape

    @pl.when(step == 0)
    def _():
        mu = block_ref[...]
        aug[:cents] = mu
        unit = lax.broadcasted_iota(jnp.int32, (aug.shape[0] - cents, width), 1) == 0
        aug[cents:] = unit.astype(jnp.float32).astype(jnp.bfloat16)
        wide = mu.astype(jnp.float32)
        bias[...] = 0.5 * jnp.sum(wide * wide, axis=1, keepdims=True)
        total[...] = jnp.zeros_like(total)
        mass[...] = jnp.zeros_like(mass)

    x = rows_ref[...].reshape(-1, width)
    raw = lax.dot_general(aug[...], x, (((1,), (1,)), ((), ())), preferred_element_type=jnp.float32)
    score = (raw[:cents] - bias[...]) * SCORE_SCALE
    present = (raw[cents : cents + 1] < MARK_LIMIT).astype(jnp.float32)
    e = jnp.exp(score - jnp.max(score, axis=0, keepdims=True))
    w = e * (present / jnp.sum(e, axis=0, keepdims=True))
    mass[...] += jnp.sum(w, axis=1, keepdims=True)
    total[...] += jnp.dot(w.astype(jnp.bfloat16), x, preferred_element_type=jnp.float32)

    @pl.when(step == pl.num_programs(0) - 1)
    def _():
        out_ref[:, :width] = total[...].astype(jnp.bfloat16)
        m = mass[...]
        hi = m.astype(jnp.bfloat16).astype(jnp.float32)
        mid = (m - hi).astype(jnp.bfloat16).astype(jnp.float32)
        low = m - hi - mid
        lane = lax.broadcasted_iota(jnp.int32, (cents, EXTRA), 1)
        terms = jnp.where(lane == 0, hi, jnp.where(lane == 1, mid, jnp.where(lane == 2, low, 0.0)))
        out_ref[:, width:] = terms.astype(jnp.bfloat16)


def cluster_sums(block, rows):
    cents, width = block.shape
    sources, capacity, _ = rows.shape
    step = 4
    return pl.pallas_call(
        cluster_kernel,
        grid=(sources // step,),
        in_specs=[
            pl.BlockSpec((cents, width), lambda i: (0, 0)),
            pl.BlockSpec((step, capacity, width), lambda i: (i, 0, 0)),
        ],
        out_specs=pl.BlockSpec((cents, width + EXTRA), lambda i: (0, 0)),
        out_shape=jax.ShapeDtypeStruct((cents, width + EXTRA), jnp.bfloat16),
        scratch_shapes=[
            pltpu.VMEM((cents + 16, width), jnp.bfloat16),
            pltpu.VMEM((cents, width), jnp.float32),
            pltpu.VMEM((cents, 1), jnp.float32),
            pltpu.VMEM((cents, 1), jnp.float32),
        ],
        compiler_params=pltpu.CompilerParams(vmem_limit_bytes=40 * MIB),
        cost_estimate=pl.CostEstimate(
            flops=4 * sources * capacity * cents * width,
            bytes_accessed=2 * width * (sources * capacity + 2 * cents),
            transcendentals=sources * capacity * cents,
        ),
        name="cluster_sums",
    )(block, rows)


def update_kernel(parts_ref, mu_ref, copies_ref, mass_ref):
    sources = parts_ref.shape[0]
    rows, width = mu_ref.shape
    total = parts_ref[0].astype(jnp.float32)
    for s in range(1, sources):
        total = total + parts_ref[s].astype(jnp.float32)
    mass = jnp.sum(total[:, width:], axis=1, keepdims=True)
    mu = mu_ref[...].astype(jnp.float32)
    new = ((total[:, :width] + PRIOR_WEIGHT * mu) / (mass + PRIOR_WEIGHT)).astype(jnp.bfloat16)
    for c in range(copies_ref.shape[0]):
        copies_ref[c] = new
    mass_ref[...] = jnp.broadcast_to(mass, mass_ref.shape)


def update(parts, mu, copies):
    rows, width = mu.shape
    return pl.pallas_call(
        update_kernel,
        out_shape=(
            jax.ShapeDtypeStruct((copies, rows, width), jnp.bfloat16),
            jax.ShapeDtypeStruct((rows, 128), jnp.float32),
        ),
        compiler_params=pltpu.CompilerParams(vmem_limit_bytes=16 * MIB),
        cost_estimate=pl.CostEstimate(
            flops=parts.size, bytes_accessed=2 * parts.size + 2 * copies * rows * width, transcendentals=0
        ),
        name="update",
    )(parts, mu)


def exchange(array, axis):
    return lax.all_to_all(array, axis, split_axis=0, concat_axis=0, tiled=True)


def shards(points, cluster_ids, owner_slot, centroids):
    owners = lax.axis_size("point")
    holders = lax.axis_size("cent")
    rows, width = points.shape
    per_owner, held, _ = centroids.shape
    capacity = 2 * rows // owner_slot.shape[0]

    blocks = lax.all_gather(centroids, "cent", axis=1, tiled=True)
    target = targets(cluster_ids, owner_slot, capacity)
    received = [
        exchange(place(target, points, j, owners, per_owner, capacity), "point")
        for j in range(per_owner)
    ]
    new, masses = [], []
    for j in range(per_owner):
        mine, block = centroids[j], blocks[j]
        for iteration in range(ITERS):
            last = iteration == ITERS - 1
            sums = cluster_sums(block, received[j])
            parts = exchange(sums.reshape(holders, held, width + EXTRA), "cent")
            copies, mass = update(parts, mine, 1 if last else holders)
            mine = copies[0]
            if not last:
                block = exchange(copies, "cent").reshape(holders * held, width)
        new.append(mine)
        masses.append(mass[:, 0])
    return jnp.stack(new), jnp.stack(masses)


def solution(mesh):
    return jax.shard_map(
        shards,
        mesh=mesh,
        in_specs=(P(("point", "cent"), None), P(("point", "cent")), P(), P("point", "cent", None)),
        out_specs=(P("point", "cent", None), P("point", "cent")),
        check_vma=False,
    )
```

time: 402 us -> 340 us (0.85)
  blocking collectives: 80.7 us -> 0 us
  starting transfers between devices: 10.1 us -> 68.3 us
  Pallas kernels: 0 us -> 54.9 us
  waiting for transfers between devices: 204 us -> 162 us
  other arithmetic: 28.6 us -> 1.27 us
  matrix products: 27 us -> 0 us
    all_to_all x2 -> x16, waiting for transfers between devices: 40.5 us -> 162 us  [exchange(): return lax.all_to_all(array, axis, split_axis=0, concat_axis=0, tiled=True)]
    all_gather x2 -> x1, waiting for transfers between devices: 95.4 us -> 0.01 us  [shards(): blocks = lax.all_gather(centroids, 'cent', axis=1, tiled=True)]
    unnamed x2 -> x0, blocking collectives: 80.7 us -> none
    reduce_scatter x2 -> x0, waiting for transfers between devices: 67.6 us -> none  [shards(): lax.psum_scatter(totals, 'cent', scatter_dimension=1, tiled=True)]
    all_to_all x2 -> x16, starting transfers between devices: 9.74 us -> 68.3 us  [exchange(): return lax.all_to_all(array, axis, split_axis=0, concat_axis=0, tiled=True)]
    pallas_call x0 -> x21, Pallas kernels: none -> 54.9 us  [the longest x8 27.8 us: cluster_sums(): pl.pallas_call(cluster_kernel, grid=(sources // step,), in_specs=[pl.Bloc...]
    scatter x2 -> x0, local copies, waits for them, and re-layouts: 29.8 us -> none  [the longest x1 15.2 us: shards(): jnp.zeros((cluster_total * capacity, feature_width), jnp.bfloat16)]
    dot_general x4 -> x0, matrix products: 27 us -> none  [the longest x2 14.2 us: responsibilities(): jnp.einsum('pjck,pjcd->jkd', weights.astype(jnp.bfloat16), received, pref...]
  transfers between devices with their start and end apart: 6 -> 17, of which waited for: 5 -> 16; matrix products, arithmetic and copies ran while one was open for 6% -> 2% of each run, Pallas kernels for 0% -> 14%
where the time goes in v1:
time: 340 us; the launch traced here: 337 us
  waiting for transfers between devices  162 us (48%)
  starting transfers between devices  68.3 us (20%)
  Pallas kernels  54.9 us (16%)
  local copies, waits for them, and re-layouts  35.8 us (11%)
  between operations  14.3 us (4%)
    all_to_all x16, waiting for transfers between devices, exchange(): return lax.all_to_all(array, axis, split_axis=0, concat_axis=0, tiled=True)  162 us
    all_to_all x16, starting transfers between devices, exchange(): return lax.all_to_all(array, axis, split_axis=0, concat_axis=0, tiled=True)  68.3 us
    unnamed x54, local copies, waits for them, and re-layouts  28.2 us
    pallas_call x8, Pallas kernels, cluster_sums(): pl.pallas_call(cluster_kernel, grid=(sources // step,), in_specs=[pl.Bloc...  27.8 us
    pallas_call x4, Pallas kernels, place(): pl.pallas_call(functools.partial(place_kernel, chunk, per_owner, capacity...  21.2 us
  transfers between devices with their start and end apart: 17, of which 16 were waited for; matrix products, arithmetic and copies ran while one was open for 2% of the time, Pallas kernels for 14%

profile of v1, /device:TPU:2, one launch (start us, length us, event | category | flops | bytes accessed | tf_op | source)
XLA Modules:
  0.0 337.0 jit_solution(15228448190117596198)
XLA Ops:
  7.2 1.3 copy.7.owner_ref
  8.5 1.7 targets.1.target_ref
  10.9 2.2 copy-done.22
  13.1 5.3 %place.4 = bf16[8,128,1024]{2,1,0:T(8,128)(2,1)S(1)} custom-call(s32[1,2048]{1,0:T(1,128)S(1)} %copy-done.20, bf16[2048,1024]{1,0:T(8,128)(2,1)S(1)} %copy-done.22), custom_call_target="tpu_custom_call" | custom-call | flops 4294967296 | bytes 6291456 | tf_op jit(solution)/shard_map/place/pallas_call | solution.py:62
  18.4 1.4 copy-done.12
  19.7 5.0 %all-to-all-start = ((bf16[8,128,1024]{2,1,0:T(8,128)(2,1)}), bf16[8,128,1024]{2,1,0:T(8,128)(2,1)S(1)}, u32[]{:S(2)}, u32[]{:S(2)}) async-start(bf16[8,128,1024]{2,1,0:T(8,128)(2,1)} %copy-done.12), calls=%async_computation | async-start | bytes 4194304 | tf_op jit(solution)/shard_map/all_to_all | solution.py:177
  24.7 2.2 copy-done.23
  26.9 5.3 %place.5 = bf16[8,128,1024]{2,1,0:T(8,128)(2,1)S(1)} custom-call(s32[1,2048]{1,0:T(1,128)S(1)} %copy-done.21, bf16[2048,1024]{1,0:T(8,128)(2,1)S(1)} %copy-done.23), custom_call_target="tpu_custom_call" | custom-call | flops 4294967296 | bytes 6291456 | tf_op jit(solution)/shard_map/place/pallas_call | solution.py:62
  32.2 1.3 copy-done.10
  33.6 16.9 %all-to-all-done.rows_ref = bf16[8,128,1024]{2,1,0:T(8,128)(2,1)S(1)} async-done(((bf16[8,128,1024]{2,1,0:T(8,128)(2,1)}), bf16[8,128,1024]{2,1,0:T(8,128)(2,1)S(1)}, u32[]{:S(2)}, u32[]{:S(2)}) %all-to-all-start) | async-done | bytes 2097184 | tf_op jit(solution)/shard_map/all_to_all | solution.py:177
  50.5 1.4 copy-done.6
  51.8 5.0 %all-to-all-start.4 = ((bf16[8,128,1024]{2,1,0:T(8,128)(2,1)}), bf16[8,128,1024]{2,1,0:T(8,128)(2,1)S(1)}, u32[]{:S(2)}, u32[]{:S(2)}) async-start(bf16[8,128,1024]{2,1,0:T(8,128)(2,1)} %copy-done.10), calls=%async_computation.4 | async-start | bytes 4194304 | tf_op jit(solution)/shard_map/all_to_all | solution.py:177
  57.5 2.2 copy-done.24
  59.7 5.3 %place.6 = bf16[8,128,1024]{2,1,0:T(8,128)(2,1)S(1)} custom-call(s32[1,2048]{1,0:T(1,128)S(1)} %copy-done.21, bf16[2048,1024]{1,0:T(8,128)(2,1)S(1)} %copy-done.24), custom_call_target="tpu_custom_call" | custom-call | flops 4294967296 | bytes 6291456 | tf_op jit(solution)/shard_map/place/pallas_call | solution.py:62
  65.0 1.4 copy-done.11
  66.4 16.1 %all-to-all-done.4.rows_ref = bf16[8,128,1024]{2,1,0:T(8,128)(2,1)S(1)} async-done(((bf16[8,128,1024]{2,1,0:T(8,128)(2,1)}), bf16[8,128,1024]{2,1,0:T(8,128)(2,1)S(1)}, u32[]{:S(2)}, u32[]{:S(2)}) %all-to-all-start.4) | async-done | bytes 2097184 | tf_op jit(solution)/shard_map/all_to_all | solution.py:177
  82.6 1.4 copy-done.3
  83.9 5.7 %all-to-all-start.8 = ((bf16[8,128,1024]{2,1,0:T(8,128)(2,1)}), bf16[8,128,1024]{2,1,0:T(8,128)(2,1)}, u32[]{:S(2)}, u32[]{:S(2)}) async-start(bf16[8,128,1024]{2,1,0:T(8,128)(2,1)} %copy-done.11), calls=%async_computation.8 | async-start | bytes 4194304 | tf_op jit(solution)/shard_map/all_to_all | solution.py:177
  89.6 2.2 copy-done.25
  91.8 5.3 %place.7 = bf16[8,128,1024]{2,1,0:T(8,128)(2,1)S(1)} custom-call(s32[1,2048]{1,0:T(1,128)S(1)} %copy-done.21, bf16[2048,1024]{1,0:T(8,128)(2,1)S(1)} %copy-done.25), custom_call_target="tpu_custom_call" | custom-call | flops 4294967296 | bytes 6291456 | tf_op jit(solution)/shard_map/place/pallas_call | solution.py:62
  97.1 1.3 copy-done.9
  98.4 17.0 %all-to-all-done.8.rows_ref = bf16[8,128,1024]{2,1,0:T(8,128)(2,1)} async-done(((bf16[8,128,1024]{2,1,0:T(8,128)(2,1)}), bf16[8,128,1024]{2,1,0:T(8,128)(2,1)}, u32[]{:S(2)}, u32[]{:S(2)}) %all-to-all-start.8) | async-done | bytes 2097184 | tf_op jit(solution)/shard_map/all_to_all | solution.py:177
  115.5 5.0 %all-to-all-start.12 = ((bf16[8,128,1024]{2,1,0:T(8,128)(2,1)}), bf16[8,128,1024]{2,1,0:T(8,128)(2,1)S(1)}, u32[]{:S(2)}, u32[]{:S(2)}) async-start(bf16[8,128,1024]{2,1,0:T(8,128)(2,1)} %copy-done.9), calls=%async_computation.12 | async-start | bytes 4194304 | tf_op jit(solution)/shard_map/all_to_all | solution.py:177
  120.5 2.7 slice_bitcast_fusion.3
  123.2 3.2 cluster_sums.8
  126.3 19.9 %all-to-all-done.12.rows_ref = bf16[8,128,1024]{2,1,0:T(8,128)(2,1)S(1)} async-done(((bf16[8,128,1024]{2,1,0:T(8,128)(2,1)}), bf16[8,128,1024]{2,1,0:T(8,128)(2,1)S(1)}, u32[]{:S(2)}, u32[]{:S(2)}) %all-to-all-start.12) | async-done | bytes 2097184 | tf_op jit(solution)/shard_map/all_to_all | solution.py:177
  146.2 1.4 copy-done
  147.6 8.0 %all-to-all-start.1 = ((bf16[16,16,1152]{2,1,0:T(8,128)(2,1)}), bf16[16,16,1152]{2,1,0:T(8,128)(2,1)S(1)}, u32[]{:S(2)}, u32[]{:S(2)}) async-start(bf16[16,16,1152]{2,1,0:T(8,128)(2,1)} %bitcast.3), calls=%async_computation.1 | async-start | bytes 1179648 | tf_op jit(solution)/shard_map/all_to_all | solution.py:177
  155.7 1.6 copy-done.4
  157.2 1.0 copy-done.19
  158.3 3.2 cluster_sums.10
  161.4 6.2 %all-to-all-done.1.parts_ref = bf16[16,16,1152]{2,1,0:T(8,128)(2,1)S(1)} async-done(((bf16[16,16,1152]{2,1,0:T(8,128)(2,1)}), bf16[16,16,1152]{2,1,0:T(8,128)(2,1)S(1)}, u32[]{:S(2)}, u32[]{:S(2)}) %all-to-all-start.1) | async-done | bytes 589856 | tf_op jit(solution)/shard_map/all_to_all | solution.py:177
  167.7 3.6 %all-to-all-start.5 = ((bf16[16,16,1152]{2,1,0:T(8,128)(2,1)}), bf16[16,16,1152]{2,1,0:T(8,128)(2,1)S(1)}, u32[]{:S(2)}, u32[]{:S(2)}) async-start(bf16[16,16,1152]{2,1,0:T(8,128)(2,1)} %bitcast.9), calls=%async_computation.5 | async-start | bytes 1179648 | tf_op jit(solution)/shard_map/all_to_all | solution.py:177
  171.3 4.4 %cluster_sums.12 = bf16[256,1152]{1,0:T(8,128)(2,1)} custom-call(bf16[256,1024]{1,0:T(8,128)(2,1)S(1)} %get-tuple-element.28.block_ref, bf16[8,128,1024]{2,1,0:T(8,128)(2,1)} %all-to-all-done.8.rows_ref), custom_call_target="tpu_custom_call" | custom-call | flops 1073741824 | bytes 3145728 | tf_op jit(solution)/shard_map/cluster_sums/pallas_call | solution.py:121
  175.7 6.7 %all-to-all-done.5.parts_ref = bf16[16,16,1152]{2,1,0:T(8,128)(2,1)S(1)} async-done(((bf16[16,16,1152]{2,1,0:T(8,128)(2,1)}), bf16[16,16,1152]{2,1,0:T(8,128)(2,1)S(1)}, u32[]{:S(2)}, u32[]{:S(2)}) %all-to-all-start.5) | async-done | bytes 589856 | tf_op jit(solution)/shard_map/all_to_all | solution.py:177
  182.4 3.6 %all-to-all-start.9 = ((bf16[16,16,1152]{2,1,0:T(8,128)(2,1)}), bf16[16,16,1152]{2,1,0:T(8,128)(2,1)S(1)}, u32[]{:S(2)}, u32[]{:S(2)}) async-start(bf16[16,16,1152]{2,1,0:T(8,128)(2,1)} %bitcast.15), calls=%async_computation.9 | async-start | bytes 1179648 | tf_op jit(solution)/shard_map/all_to_all | solution.py:177
  186.0 1.6 copy-done.1
  187.5 3.2 cluster_sums.14
  190.7 5.7 %all-to-all-done.9.parts_ref = bf16[16,16,1152]{2,1,0:T(8,128)(2,1)S(1)} async-done(((bf16[16,16,1152]{2,1,0:T(8,128)(2,1)}), bf16[16,16,1152]{2,1,0:T(8,128)(2,1)S(1)}, u32[]{:S(2)}, u32[]{:S(2)}) %all-to-all-start.9) | async-done | bytes 589856 | tf_op jit(solution)/shard_map/all_to_all | solution.py:177
  196.4 3.6 %all-to-all-start.13 = ((bf16[16,16,1152]{2,1,0:T(8,128)(2,1)}), bf16[16,16,1152]{2,1,0:T(8,128)(2,1)S(1)}, u32[]{:S(2)}, u32[]{:S(2)}) async-start(bf16[16,16,1152]{2,1,0:T(8,128)(2,1)} %bitcast.21), calls=%async_computation.13 | async-start | bytes 1179648 | tf_op jit(solution)/shard_map/all_to_all | solution.py:177
  200.9 9.5 %all-to-all-done.13.parts_ref = bf16[16,16,1152]{2,1,0:T(8,128)(2,1)S(1)} async-done(((bf16[16,16,1152]{2,1,0:T(8,128)(2,1)}), bf16[16,16,1152]{2,1,0:T(8,128)(2,1)S(1)}, u32[]{:S(2)}, u32[]{:S(2)}) %all-to-all-start.13) | async-done | bytes 589856 | tf_op jit(solution)/shard_map/all_to_all | solution.py:177
  210.4 3.6 %all-to-all-start.2 = ((bf16[16,16,1024]{2,1,0:T(8,128)(2,1)}), bf16[16,16,1024]{2,1,0:T(8,128)(2,1)S(1)}, u32[]{:S(2)}, u32[]{:S(2)}) async-start(bf16[16,16,1024]{2,1,0:T(8,128)(2,1)} %get-tuple-element.14), calls=%async_computation.2 | async-start | bytes 1048576 | tf_op jit(solution)/shard_map/all_to_all | solution.py:177
  214.9 9.2 %all-to-all-done.2 = bf16[16,16,1024]{2,1,0:T(8,128)(2,1)S(1)} async-done(((bf16[16,16,1024]{2,1,0:T(8,128)(2,1)}), bf16[16,16,1024]{2,1,0:T(8,128)(2,1)S(1)}, u32[]{:S(2)}, u32[]{:S(2)}) %all-to-all-start.2) | async-done | bytes 524320 | tf_op jit(solution)/shard_map/all_to_all | solution.py:177
  224.1 3.6 %all-to-all-start.6 = ((bf16[16,16,1024]{2,1,0:T(8,128)(2,1)}), bf16[16,16,1024]{2,1,0:T(8,128)(2,1)S(1)}, u32[]{:S(2)}, u32[]{:S(2)}) async-start(bf16[16,16,1024]{2,1,0:T(8,128)(2,1)} %get-tuple-element.16), calls=%async_computation.6 | async-start | bytes 1048576 | tf_op jit(solution)/shard_map/all_to_all | solution.py:177
  228.6 9.1 %all-to-all-done.6 = bf16[16,16,1024]{2,1,0:T(8,128)(2,1)S(1)} async-done(((bf16[16,16,1024]{2,1,0:T(8,128)(2,1)}), bf16[16,16,1024]{2,1,0:T(8,128)(2,1)S(1)}, u32[]{:S(2)}, u32[]{:S(2)}) %all-to-all-start.6) | async-done | bytes 524320 | tf_op jit(solution)/shard_map/all_to_all | solution.py:177
  237.8 3.6 %all-to-all-start.10 = ((bf16[16,16,1024]{2,1,0:T(8,128)(2,1)}), bf16[16,16,1024]{2,1,0:T(8,128)(2,1)S(1)}, u32[]{:S(2)}, u32[]{:S(2)}) async-start(bf16[16,16,1024]{2,1,0:T(8,128)(2,1)} %get-tuple-element.18), calls=%async_computation.10 | async-start | bytes 1048576 | tf_op jit(solution)/shard_map/all_to_all | solution.py:177
  242.3 9.2 %all-to-all-done.10 = bf16[16,16,1024]{2,1,0:T(8,128)(2,1)S(1)} async-done(((bf16[16,16,1024]{2,1,0:T(8,128)(2,1)}), bf16[16,16,1024]{2,1,0:T(8,128)(2,1)S(1)}, u32[]{:S(2)}, u32[]{:S(2)}) %all-to-all-start.10) | async-done | bytes 524320 | tf_op jit(solution)/shard_map/all_to_all | solution.py:177
  251.5 3.6 %all-to-all-start.14 = ((bf16[16,16,1024]{2,1,0:T(8,128)(2,1)}), bf16[16,16,1024]{2,1,0:T(8,128)(2,1)S(1)}, u32[]{:S(2)}, u32[]{:S(2)}) async-start(bf16[16,16,1024]{2,1,0:T(8,128)(2,1)} %get-tuple-element.20), calls=%async_computation.14 | async-start | bytes 1048576 | tf_op jit(solution)/shard_map/all_to_all | solution.py:177
  255.1 1.6 copy-done.8
  256.7 3.2 cluster_sums.9
  259.9 5.4 %all-to-all-done.14 = bf16[16,16,1024]{2,1,0:T(8,128)(2,1)S(1)} async-done(((bf16[16,16,1024]{2,1,0:T(8,128)(2,1)}), bf16[16,16,1024]{2,1,0:T(8,128)(2,1)S(1)}, u32[]{:S(2)}, u32[]{:S(2)}) %all-to-all-start.14) | async-done | bytes 524320 | tf_op jit(solution)/shard_map/all_to_all | solution.py:177
  266.1 3.6 %all-to-all-start.3 = ((bf16[16,16,1152]{2,1,0:T(8,128)(2,1)}), bf16[16,16,1152]{2,1,0:T(8,128)(2,1)S(1)}, u32[]{:S(2)}, u32[]{:S(2)}) async-start(bf16[16,16,1152]{2,1,0:T(8,128)(2,1)} %bitcast.6), calls=%async_computation.3 | async-start | bytes 1179648 | tf_op jit(solution)/shard_map/all_to_all | solution.py:177
  269.7 1.0 copy-done.14
  270.7 3.2 cluster_sums.11
  273.9 6.9 %all-to-all-done.3.parts_ref = bf16[16,16,1152]{2,1,0:T(8,128)(2,1)S(1)} async-done(((bf16[16,16,1152]{2,1,0:T(8,128)(2,1)}), bf16[16,16,1152]{2,1,0:T(8,128)(2,1)S(1)}, u32[]{:S(2)}, u32[]{:S(2)}) %all-to-all-start.3) | async-done | bytes 589856 | tf_op jit(solution)/shard_map/all_to_all | solution.py:177
  280.8 3.6 %all-to-all-start.7 = ((bf16[16,16,1152]{2,1,0:T(8,128)(2,1)}), bf16[16,16,1152]{2,1,0:T(8,128)(2,1)S(1)}, u32[]{:S(2)}, u32[]{:S(2)}) async-start(bf16[16,16,1152]{2,1,0:T(8,128)(2,1)} %bitcast.12), calls=%async_computation.7 | async-start | bytes 1179648 | tf_op jit(solution)/shard_map/all_to_all | solution.py:177
  284.4 4.5 %cluster_sums.13 = bf16[256,1152]{1,0:T(8,128)(2,1)} custom-call(bf16[256,1024]{1,0:T(8,128)(2,1)S(1)} %bitcast.45, bf16[8,128,1024]{2,1,0:T(8,128)(2,1)} %all-to-all-done.8.rows_ref), custom_call_target="tpu_custom_call" | custom-call | flops 1073741824 | bytes 3145728 | tf_op jit(solution)/shard_map/cluster_sums/pallas_call | solution.py:121
  288.9 7.7 %all-to-all-done.7.parts_ref = bf16[16,16,1152]{2,1,0:T(8,128)(2,1)S(1)} async-done(((bf16[16,16,1152]{2,1,0:T(8,128)(2,1)}), bf16[16,16,1152]{2,1,0:T(8,128)(2,1)S(1)}, u32[]{:S(2)}, u32[]{:S(2)}) %all-to-all-start.7) | async-done | bytes 589856 | tf_op jit(solution)/shard_map/all_to_all | solution.py:177
  296.5 3.8 %all-to-all-start.11 = ((bf16[16,16,1152]{2,1,0:T(8,128)(2,1)}), bf16[16,16,1152]{2,1,0:T(8,128)(2,1)S(1)}, u32[]{:S(2)}, u32[]{:S(2)}) async-start(bf16[16,16,1152]{2,1,0:T(8,128)(2,1)} %bitcast.18), calls=%async_computation.11 | async-start | bytes 1179648 | tf_op jit(solution)/shard_map/all_to_all | solution.py:177
  302.7 1.6 copy-done.2
  304.3 3.2 cluster_sums.15
  307.4 7.2 %all-to-all-done.11.parts_ref = bf16[16,16,1152]{2,1,0:T(8,128)(2,1)S(1)} async-done(((bf16[16,16,1152]{2,1,0:T(8,128)(2,1)}), bf16[16,16,1152]{2,1,0:T(8,128)(2,1)S(1)}, u32[]{:S(2)}, u32[]{:S(2)}) %all-to-all-start.11) | async-done | bytes 589856 | tf_op jit(solution)/shard_map/all_to_all | solution.py:177
  314.7 3.6 %all-to-all-start.15 = ((bf16[16,16,1152]{2,1,0:T(8,128)(2,1)}), bf16[16,16,1152]{2,1,0:T(8,128)(2,1)S(1)}, u32[]{:S(2)}, u32[]{:S(2)}) async-start(bf16[16,16,1152]{2,1,0:T(8,128)(2,1)} %bitcast.24), calls=%async_computation.15 | async-start | bytes 1179648 | tf_op jit(solution)/shard_map/all_to_all | solution.py:177
  319.7 9.0 %all-to-all-done.15.parts_ref = bf16[16,16,1152]{2,1,0:T(8,128)(2,1)S(1)} async-done(((bf16[16,16,1152]{2,1,0:T(8,128)(2,1)}), bf16[16,16,1152]{2,1,0:T(8,128)(2,1)S(1)}, u32[]{:S(2)}, u32[]{:S(2)}) %all-to-all-start.15) | async-done | bytes 589856 | tf_op jit(solution)/shard_map/all_to_all | solution.py:177
  (59 shorter events, 11.2 us)
Async XLA Ops:
  10.2 0.7 copy-start.20
  10.9 2.2 copy-start.22
  18.4 1.4 copy-start.12
  19.7 5.0 %copy-start.21 = (s32[1,2048]{1,0:T(1,128)S(1)}, s32[1,2048]{1,0:T(1,128)}, u32[]{:S(2)}) copy-start(s32[1,2048]{1,0:T(1,128)} %targets.1.target_ref) | copy-start | bytes 24580
  19.7 30.7 %all-to-all-start = ((bf16[8,128,1024]{2,1,0:T(8,128)(2,1)}), bf16[8,128,1024]{2,1,0:T(8,128)(2,1)S(1)}, u32[]{:S(2)}, u32[]{:S(2)}) async-start(bf16[8,128,1024]{2,1,0:T(8,128)(2,1)} %copy-done.12), calls=%async_computation | async-start | bytes 4194304 | tf_op jit(solution)/shard_map/all_to_all | solution.py:177
  24.7 2.2 copy-start.23
  32.2 1.4 copy-start.10
  50.5 1.4 copy-start.6
  51.8 30.7 %all-to-all-start.4 = ((bf16[8,128,1024]{2,1,0:T(8,128)(2,1)}), bf16[8,128,1024]{2,1,0:T(8,128)(2,1)S(1)}, u32[]{:S(2)}, u32[]{:S(2)}) async-start(bf16[8,128,1024]{2,1,0:T(8,128)(2,1)} %copy-done.10), calls=%async_computation.4 | async-start | bytes 4194304 | tf_op jit(solution)/shard_map/all_to_all | solution.py:177
  56.8 63.7 %all-gather.2.cloned.1.call-start = ((), (), s32[]{:S(2)}) async-start(), calls=%async_computation.16 | async-start | bytes 2228224 | tf_op jit(solution)/shard_map/all_gather | solution.py:187
  57.5 2.2 copy-start.24
  65.0 1.4 copy-start.11
  82.6 1.4 copy-start.3
  83.9 31.6 %all-to-all-start.8 = ((bf16[8,128,1024]{2,1,0:T(8,128)(2,1)}), bf16[8,128,1024]{2,1,0:T(8,128)(2,1)}, u32[]{:S(2)}, u32[]{:S(2)}) async-start(bf16[8,128,1024]{2,1,0:T(8,128)(2,1)} %copy-done.11), calls=%async_computation.8 | async-start | bytes 4194304 | tf_op jit(solution)/shard_map/all_to_all | solution.py:177
  89.6 2.2 copy-start.25
  97.1 1.3 copy-start.9
  115.5 30.7 %all-to-all-start.12 = ((bf16[8,128,1024]{2,1,0:T(8,128)(2,1)}), bf16[8,128,1024]{2,1,0:T(8,128)(2,1)S(1)}, u32[]{:S(2)}, u32[]{:S(2)}) async-start(bf16[8,128,1024]{2,1,0:T(8,128)(2,1)} %copy-done.9), calls=%async_computation.12 | async-start | bytes 4194304 | tf_op jit(solution)/shard_map/all_to_all | solution.py:177
  120.5 2.7 copy-start.7
  146.2 1.4 copy-start
  147.6 20.1 %all-to-all-start.1 = ((bf16[16,16,1152]{2,1,0:T(8,128)(2,1)}), bf16[16,16,1152]{2,1,0:T(8,128)(2,1)S(1)}, u32[]{:S(2)}, u32[]{:S(2)}) async-start(bf16[16,16,1152]{2,1,0:T(8,128)(2,1)} %bitcast.3), calls=%async_computation.1 | async-start | bytes 1179648 | tf_op jit(solution)/shard_map/all_to_all | solution.py:177
  155.6 1.6 copy-start.4
  157.2 1.0 copy-start.19
  167.7 14.7 %all-to-all-start.5 = ((bf16[16,16,1152]{2,1,0:T(8,128)(2,1)}), bf16[16,16,1152]{2,1,0:T(8,128)(2,1)S(1)}, u32[]{:S(2)}, u32[]{:S(2)}) async-start(bf16[16,16,1152]{2,1,0:T(8,128)(2,1)} %bitcast.9), calls=%async_computation.5 | async-start | bytes 1179648 | tf_op jit(solution)/shard_map/all_to_all | solution.py:177
  182.4 14.0 %all-to-all-start.9 = ((bf16[16,16,1152]{2,1,0:T(8,128)(2,1)}), bf16[16,16,1152]{2,1,0:T(8,128)(2,1)S(1)}, u32[]{:S(2)}, u32[]{:S(2)}) async-start(bf16[16,16,1152]{2,1,0:T(8,128)(2,1)} %bitcast.15), calls=%async_computation.9 | async-start | bytes 1179648 | tf_op jit(solution)/shard_map/all_to_all | solution.py:177
  186.0 1.6 copy-start.1
  187.5 12.4 %copy-start.26 = (bf16[4,16,1024]{2,1,0:T(8,128)(2,1)S(1)}, bf16[4,16,1024]{2,1,0:T(8,128)(2,1)}, u32[]{:S(2)}) copy-start(bf16[4,16,1024]{2,1,0:T(8,128)(2,1)} %param.7) | copy-start | bytes 393220
  196.4 14.0 %all-to-all-start.13 = ((bf16[16,16,1152]{2,1,0:T(8,128)(2,1)}), bf16[16,16,1152]{2,1,0:T(8,128)(2,1)S(1)}, u32[]{:S(2)}, u32[]{:S(2)}) async-start(bf16[16,16,1152]{2,1,0:T(8,128)(2,1)} %bitcast.21), calls=%async_computation.13 | async-start | bytes 1179648 | tf_op jit(solution)/shard_map/all_to_all | solution.py:177
  210.4 13.7 %all-to-all-start.2 = ((bf16[16,16,1024]{2,1,0:T(8,128)(2,1)}), bf16[16,16,1024]{2,1,0:T(8,128)(2,1)S(1)}, u32[]{:S(2)}, u32[]{:S(2)}) async-start(bf16[16,16,1024]{2,1,0:T(8,128)(2,1)} %get-tuple-element.14), calls=%async_computation.2 | async-start | bytes 1048576 | tf_op jit(solution)/shard_map/all_to_all | solution.py:177
  224.1 13.7 %all-to-all-start.6 = ((bf16[16,16,1024]{2,1,0:T(8,128)(2,1)}), bf16[16,16,1024]{2,1,0:T(8,128)(2,1)S(1)}, u32[]{:S(2)}, u32[]{:S(2)}) async-start(bf16[16,16,1024]{2,1,0:T(8,128)(2,1)} %get-tuple-element.16), calls=%async_computation.6 | async-start | bytes 1048576 | tf_op jit(solution)/shard_map/all_to_all | solution.py:177
  237.8 17.3 %copy-start.13 = (bf16[16,16,1024]{2,1,0:T(8,128)(2,1)}, bf16[16,16,1024]{2,1,0:T(8,128)(2,1)S(1)}, u32[]{:S(2)}) copy-start(bf16[16,16,1024]{2,1,0:T(8,128)(2,1)S(1)} %all-to-all-done.6) | copy-start | bytes 1572868
  237.8 13.7 %all-to-all-start.10 = ((bf16[16,16,1024]{2,1,0:T(8,128)(2,1)}), bf16[16,16,1024]{2,1,0:T(8,128)(2,1)S(1)}, u32[]{:S(2)}, u32[]{:S(2)}) async-start(bf16[16,16,1024]{2,1,0:T(8,128)(2,1)} %get-tuple-element.18), calls=%async_computation.10 | async-start | bytes 1048576 | tf_op jit(solution)/shard_map/all_to_all | solution.py:177
  251.5 3.6 %copy-start.17 = (bf16[16,16,1024]{2,1,0:T(8,128)(2,1)}, bf16[16,16,1024]{2,1,0:T(8,128)(2,1)S(1)}, u32[]{:S(2)}) copy-start(bf16[16,16,1024]{2,1,0:T(8,128)(2,1)S(1)} %all-to-all-done.10) | copy-start | bytes 1572868
  251.5 13.8 %all-to-all-start.14 = ((bf16[16,16,1024]{2,1,0:T(8,128)(2,1)}), bf16[16,16,1024]{2,1,0:T(8,128)(2,1)S(1)}, u32[]{:S(2)}, u32[]{:S(2)}) async-start(bf16[16,16,1024]{2,1,0:T(8,128)(2,1)} %get-tuple-element.20), calls=%async_computation.14 | async-start | bytes 1048576 | tf_op jit(solution)/shard_map/all_to_all | solution.py:177
  255.1 1.6 copy-start.8
  256.7 13.0 %copy-start.5 = (bf16[8,128,1024]{2,1,0:T(8,128)(2,1)S(1)}, bf16[8,128,1024]{2,1,0:T(8,128)(2,1)}, u32[]{:S(2)}) copy-start(bf16[8,128,1024]{2,1,0:T(8,128)(2,1)} %copy-done.3) | copy-start | bytes 6291460
  265.3 0.8 copy-start.15
  266.1 14.7 %all-to-all-start.3 = ((bf16[16,16,1152]{2,1,0:T(8,128)(2,1)}), bf16[16,16,1152]{2,1,0:T(8,128)(2,1)S(1)}, u32[]{:S(2)}, u32[]{:S(2)}) async-start(bf16[16,16,1152]{2,1,0:T(8,128)(2,1)} %bitcast.6), calls=%async_computation.3 | async-start | bytes 1179648 | tf_op jit(solution)/shard_map/all_to_all | solution.py:177
  269.7 1.0 copy-start.14
  270.7 13.6 %copy-start.18 = (bf16[16,16,1024]{2,1,0:T(8,128)(2,1)S(1)}, bf16[16,16,1024]{2,1,0:T(8,128)(2,1)}, u32[]{:S(2)}) copy-start(bf16[16,16,1024]{2,1,0:T(8,128)(2,1)} %copy-done.17) | copy-start | bytes 1572868
  280.8 15.8 %all-to-all-start.7 = ((bf16[16,16,1152]{2,1,0:T(8,128)(2,1)}), bf16[16,16,1152]{2,1,0:T(8,128)(2,1)S(1)}, u32[]{:S(2)}, u32[]{:S(2)}) async-start(bf16[16,16,1152]{2,1,0:T(8,128)(2,1)} %bitcast.12), calls=%async_computation.7 | async-start | bytes 1179648 | tf_op jit(solution)/shard_map/all_to_all | solution.py:177
  284.4 18.3 %copy-start.16 = (bf16[16,16,1024]{2,1,0:T(8,128)(2,1)S(1)}, bf16[16,16,1024]{2,1,0:T(8,128)(2,1)}, u32[]{:S(2)}) copy-start(bf16[16,16,1024]{2,1,0:T(8,128)(2,1)} %copy-done.15) | copy-start | bytes 1572868
  296.5 18.1 %all-to-all-start.11 = ((bf16[16,16,1152]{2,1,0:T(8,128)(2,1)}), bf16[16,16,1152]{2,1,0:T(8,128)(2,1)S(1)}, u32[]{:S(2)}, u32[]{:S(2)}) async-start(bf16[16,16,1152]{2,1,0:T(8,128)(2,1)} %bitcast.18), calls=%async_computation.11 | async-start | bytes 1179648 | tf_op jit(solution)/shard_map/all_to_all | solution.py:177
  302.7 1.6 copy-start.2
  314.7 14.0 %all-to-all-start.15 = ((bf16[16,16,1152]{2,1,0:T(8,128)(2,1)}), bf16[16,16,1152]{2,1,0:T(8,128)(2,1)S(1)}, u32[]{:S(2)}, u32[]{:S(2)}) async-start(bf16[16,16,1152]{2,1,0:T(8,128)(2,1)} %bitcast.24), calls=%async_computation.15 | async-start | bytes 1179648 | tf_op jit(solution)/shard_map/all_to_all | solution.py:177
Sparse Core Ops, SparseCore 0:
  59.8 47.6 all-gather.1

commit v2 on v1

v2 whole, which is shorter than its diff:
```python
import functools

import jax
import jax.numpy as jnp
from jax import lax
from jax.experimental import pallas as pl
from jax.experimental.pallas import tpu as pltpu
from jax.sharding import Mesh, PartitionSpec as P

ITERS = 2
SCORE_SCALE = 0.25
PRIOR_WEIGHT = 1.0
EXTRA = 128
MARK = 1024.0
MARK_LIMIT = 512.0
GROUP = 256
CHUNKS = 2
MIB = 1024 * 1024
VMEM = 60 * MIB


def target_kernel(capacity, ids_ref, owner_ref, out_ref):
    clusters = owner_ref.shape[0]
    rows = ids_ref.shape[1]
    before = (
        lax.broadcasted_iota(jnp.int32, (GROUP, GROUP), 0)
        < lax.broadcasted_iota(jnp.int32, (GROUP, GROUP), 1)
    ).astype(jnp.float32).astype(jnp.bfloat16)
    table = lax.broadcasted_iota(jnp.int32, (clusters, GROUP), 0)
    base = (owner_ref[...] * capacity).astype(jnp.float32)
    for g in range(rows // GROUP):
        span = pl.ds(g * GROUP, GROUP)
        hit = (table == ids_ref[:, span]).astype(jnp.float32)
        place = jnp.dot(hit.astype(jnp.bfloat16), before, preferred_element_type=jnp.float32)
        out_ref[:, span] = jnp.sum(hit * (place + base), axis=0, keepdims=True).astype(jnp.int32)
        base = base + jnp.sum(hit, axis=1, keepdims=True)


def targets(cluster_ids, owner_slot, capacity):
    rows = cluster_ids.shape[0]
    return pl.pallas_call(
        functools.partial(target_kernel, capacity),
        out_shape=jax.ShapeDtypeStruct((1, rows), jnp.int32),
        compiler_params=pltpu.CompilerParams(vmem_limit_bytes=VMEM),
        name="targets",
    )(cluster_ids.reshape(1, rows), owner_slot.reshape(-1, 1))


def place_kernel(first_slot, capacity, target_ref, points_ref, out_ref):
    rows = points_ref.shape[0]
    clusters, slots, width = out_ref.shape
    lane = lax.broadcasted_iota(jnp.int32, (slots, width), 1)
    local = lax.broadcasted_iota(jnp.int32, (slots, rows), 0)
    picks = []
    for c in range(clusters):
        start = (pl.program_id(0) * clusters + c) * capacity + first_slot
        picks.append((local + start == target_ref[...]).astype(jnp.float32))
    pick = jnp.concatenate(picks, axis=0)
    got = jnp.dot(pick.astype(jnp.bfloat16), points_ref[...], preferred_element_type=jnp.float32)
    for c in range(clusters):
        empty = 1.0 - jnp.sum(picks[c], axis=1, keepdims=True)
        part = got[c * slots : (c + 1) * slots]
        out_ref[c] = (part + jnp.where(lane == 0, MARK * empty, 0.0)).astype(jnp.bfloat16)


def place(target, points, clusters, capacity, chunk):
    rows, width = points.shape
    slots = capacity // CHUNKS
    step = 512 // slots
    return pl.pallas_call(
        functools.partial(place_kernel, chunk * slots, capacity),
        grid=(clusters // step,),
        in_specs=[
            pl.BlockSpec((1, rows), lambda i: (0, 0)),
            pl.BlockSpec((rows, width), lambda i: (0, 0)),
        ],
        out_specs=pl.BlockSpec((step, slots, width), lambda i: (i, 0, 0)),
        out_shape=jax.ShapeDtypeStruct((clusters, slots, width), jnp.bfloat16),
        compiler_params=pltpu.CompilerParams(vmem_limit_bytes=VMEM),
        cost_estimate=pl.CostEstimate(
            flops=2 * clusters * slots * rows * width,
            bytes_accessed=2 * width * (rows + clusters * slots),
            transcendentals=0,
        ),
        name="place",
    )(target, points)


def sums_kernel(groups, chunks, steps, carried, finish, *refs):
    blocks, refs = refs[:groups], refs[groups:]
    rows, refs = refs[:chunks], refs[chunks:]
    carry, refs = refs[: 2 * carried], refs[2 * carried :]
    outs, (aug, total, mass, bias) = refs[:-4], refs[-4:]
    step = pl.program_id(0)
    held, width = blocks[0].shape
    cents = groups * held

    @pl.when(step == 0)
    def _():
        for g in range(groups):
            mu = blocks[g][...]
            span = pl.ds(g * held, held)
            aug[span] = mu
            wide = mu.astype(jnp.float32)
            bias[span] = 0.5 * jnp.sum(wide * wide, axis=1, keepdims=True)
        unit = lax.broadcasted_iota(jnp.int32, (aug.shape[0] - cents, width), 1) == 0
        aug[cents:] = unit.astype(jnp.float32).astype(jnp.bfloat16)
        if carried:
            total[...] = carry[0][...]
            mass[...] = carry[1][...]
        else:
            total[...] = jnp.zeros_like(total)
            mass[...] = jnp.zeros_like(mass)

    def accumulate(rows_ref):
        x = rows_ref[...].reshape(-1, width)
        raw = lax.dot_general(
            aug[...], x, (((1,), (1,)), ((), ())), preferred_element_type=jnp.float32
        )
        score = (raw[:cents] - bias[...]) * SCORE_SCALE
        present = (raw[cents : cents + 1] < MARK_LIMIT).astype(jnp.float32)
        e = jnp.exp(score - jnp.max(score, axis=0, keepdims=True))
        w = e * (present / jnp.sum(e, axis=0, keepdims=True))
        mass[...] += jnp.sum(w, axis=1, keepdims=True)
        total[...] += jnp.dot(w.astype(jnp.bfloat16), x, preferred_element_type=jnp.float32)

    for c in range(chunks):
        if chunks == 1:
            accumulate(rows[c])
        else:
            pl.when(step // steps == c)(functools.partial(accumulate, rows[c]))

    @pl.when(step == chunks * steps - 1)
    def _():
        if not finish:
            outs[0][...] = total[...]
            outs[1][...] = mass[...]
            return
        lane = lax.broadcasted_iota(jnp.int32, (held, EXTRA), 1)
        for g in range(groups):
            span = pl.ds(g * held, held)
            outs[g][:, :width] = total[span].astype(jnp.bfloat16)
            outs[g][:, width:] = terms(mass[span], lane)


def terms(m, lane):
    hi = m.astype(jnp.bfloat16).astype(jnp.float32)
    mid = (m - hi).astype(jnp.bfloat16).astype(jnp.float32)
    low = m - hi - mid
    parts = jnp.where(lane == 0, hi, jnp.where(lane == 1, mid, jnp.where(lane == 2, low, 0.0)))
    return parts.astype(jnp.bfloat16)


def cluster_sums(blocks, rows, carry=(), finish=True):
    groups, chunks = len(blocks), len(rows)
    held, width = blocks[0].shape
    sources, slots, _ = rows[0].shape
    cents = groups * held
    step = max(1, 512 // slots)
    steps = sources // step

    def whole(shape):
        return pl.BlockSpec(shape, lambda i: (0,) * len(shape))

    def chunk_spec(c):
        return pl.BlockSpec(
            (step, slots, width), lambda i: (jnp.clip(i - c * steps, 0, steps - 1), 0, 0)
        )

    if finish:
        shapes = [jax.ShapeDtypeStruct((held, width + EXTRA), jnp.bfloat16)] * groups
    else:
        shapes = [
            jax.ShapeDtypeStruct((cents, width), jnp.float32),
            jax.ShapeDtypeStruct((cents, 1), jnp.float32),
        ]
    count = chunks * sources * slots
    return pl.pallas_call(
        functools.partial(sums_kernel, groups, chunks, steps, 1 if carry else 0, finish),
        grid=(chunks * steps,),
        in_specs=[whole((held, width))] * groups
        + [chunk_spec(c) for c in range(chunks)]
        + [whole(a.shape) for a in carry],
        out_specs=[whole(s.shape) for s in shapes],
        out_shape=shapes,
        scratch_shapes=[
            pltpu.VMEM((cents + 16, width), jnp.bfloat16),
            pltpu.VMEM((cents, width), jnp.float32),
            pltpu.VMEM((cents, 1), jnp.float32),
            pltpu.VMEM((cents, 1), jnp.float32),
        ],
        compiler_params=pltpu.CompilerParams(vmem_limit_bytes=VMEM),
        cost_estimate=pl.CostEstimate(
            flops=4 * count * cents * width,
            bytes_accessed=2 * width * (count + 2 * cents),
            transcendentals=count * cents,
        ),
        name="cluster_sums",
    )(*blocks, *rows, *carry)


def update_kernel(packed, count, *refs):
    parts, mu_ref, out_ref = refs[:count], refs[count], refs[count + 1]
    rows, width = mu_ref.shape
    total = parts[0][...].astype(jnp.float32)
    for s in range(1, count):
        total = total + parts[s][...].astype(jnp.float32)
    mass = jnp.sum(total[:, width:], axis=1, keepdims=True)
    mu = mu_ref[...].astype(jnp.float32)
    new = (total[:, :width] + PRIOR_WEIGHT * mu) / (mass + PRIOR_WEIGHT)
    out_ref[:, :width] = new.astype(jnp.bfloat16)
    if packed:
        out_ref[:, width:] = terms(mass, lax.broadcasted_iota(jnp.int32, (rows, EXTRA), 1))


def update(parts, mu, packed):
    rows, width = mu.shape
    return pl.pallas_call(
        functools.partial(update_kernel, packed, len(parts)),
        out_shape=jax.ShapeDtypeStruct((rows, width + (EXTRA if packed else 0)), jnp.bfloat16),
        compiler_params=pltpu.CompilerParams(vmem_limit_bytes=VMEM),
        cost_estimate=pl.CostEstimate(
            flops=len(parts) * rows * width,
            bytes_accessed=2 * (len(parts) + 2) * rows * width,
            transcendentals=0,
        ),
        name="update",
    )(*parts, mu)


def exchange(array, axis):
    return lax.all_to_all(array, axis, split_axis=0, concat_axis=0, tiled=True)


def shards(points, cluster_ids, owner_slot, centroids):
    rows, width = points.shape
    clusters = owner_slot.shape[0]
    capacity = 2 * rows // clusters
    per_owner, held, _ = centroids.shape
    ny, nz = lax.axis_size("y"), lax.axis_size("z")
    y = lax.axis_index("y")
    shifts = [[(i, (i + d) % ny) for i in range(ny)] for d in range(ny)]

    spread = jnp.broadcast_to(centroids[:, None], (nz, ny, held, width))
    gathered = exchange(spread.reshape(nz * ny, held, width), ("z", "y"))
    by_y = gathered.reshape(nz, ny, held, width).swapaxes(0, 1).reshape(ny, nz * held, width)
    blocks = [lax.dynamic_index_in_dim(by_y, (y + d) % ny, 0, keepdims=False) for d in range(ny)]
    mine = blocks[0]

    target = targets(cluster_ids, owner_slot, capacity)
    received = [
        exchange(place(target, points, clusters, capacity, c), ("x", "core", "z"))
        for c in range(CHUNKS)
    ]
    for iteration in range(ITERS):
        last = iteration == ITERS - 1
        if iteration == 0:
            carry = ()
            for c in range(CHUNKS - 1):
                carry = cluster_sums(blocks, received[c : c + 1], carry, finish=False)
            sums = cluster_sums(blocks, received[CHUNKS - 1 :], carry)
        else:
            sums = cluster_sums(blocks, received)
        parts = [sums[0]] + [lax.ppermute(sums[d], "y", shifts[d]) for d in range(1, ny)]
        mine = update(parts, mine, last)
        if not last:
            blocks = [mine] + [lax.ppermute(mine, "y", shifts[ny - d]) for d in range(1, ny)]
    final = exchange(mine.reshape(nz, held, width + EXTRA), "z")
    return final[..., :width], jnp.sum(final[..., width:].astype(jnp.float32), axis=-1)


def solution(mesh):
    fine = Mesh(mesh.devices.reshape(4, 2, 4, 4), ("x", "core", "z", "y"))
    point, cent = ("x", "core"), ("z", "y")
    return jax.shard_map(
        shards,
        mesh=fine,
        in_specs=(P(point + cent, None), P(point + cent), P(), P(point, cent, None)),
        out_specs=(P(point, cent, None), P(point, cent)),
        check_vma=False,
    )
```

time: 340 us -> 214 us (0.63)
  waiting for transfers between devices: 162 us -> 98.6 us
  starting transfers between devices: 68.3 us -> 37.4 us
  local copies, waits for them, and re-layouts: 35.8 us -> 6.65 us
  between operations: 14.3 us -> 0.75 us
  blocking collectives: 0 us -> 10.3 us
    all_to_all x16 -> x3, waiting for transfers between devices: 162 us -> 80.5 us  [exchange(): return lax.all_to_all(array, axis, split_axis=0, concat_axis=0, tiled=True)]
    all_to_all x16 -> x3, starting transfers between devices: 68.3 us -> 23.8 us  [exchange(): return lax.all_to_all(array, axis, split_axis=0, concat_axis=0, tiled=True)]
    unnamed x54 -> x18, local copies, waits for them, and re-layouts: 28.2 us -> 2.05 us
    ppermute x0 -> x9, waiting for transfers between devices: none -> 18.1 us  [the longest x6 11.1 us: shards(): lax.ppermute(sums[d], 'y', shifts[d])]
    ppermute x0 -> x9, starting transfers between devices: none -> 13.6 us  [the longest x6 9.57 us: shards(): lax.ppermute(sums[d], 'y', shifts[d])]
    all_to_all x0 -> x1, blocking collectives: none -> 10.3 us  [exchange(): return lax.all_to_all(array, axis, split_axis=0, concat_axis=0, tiled=True)]
    squeeze x6 -> x1, local copies, waits for them, and re-layouts: 5.78 us -> 0.79 us  [shards(): lax.dynamic_index_in_dim(by_y, (y + d) % ny, 0, keepdims=False)]
    pallas_call x20 -> x7, Pallas kernels: 53.3 us -> 55.3 us  [the longest x3 26.1 us: cluster_sums(): pl.pallas_call(functools.partial(sums_kernel, groups, chunks, steps, 1 if...]
  transfers between devices with their start and end apart: 17 -> 12, of which waited for: 16 -> 9; matrix products, arithmetic and copies ran while one was open for 2% -> 1% of each run, Pallas kernels for 14% -> 16%
where the time goes in v2:
time: 214 us; the launch traced here: 211 us
  waiting for transfers between devices  98.6 us (46%)
  Pallas kernels  57 us (27%)
  starting transfers between devices  37.4 us (17%)
  blocking collectives  10.3 us (5%)
  local copies, waits for them, and re-layouts  6.65 us (3%)
    all_to_all x3, waiting for transfers between devices, exchange(): return lax.all_to_all(array, axis, split_axis=0, concat_axis=0, tiled=True)  80.5 us
    pallas_call x3, Pallas kernels, cluster_sums(): pl.pallas_call(functools.partial(sums_kernel, groups, chunks, steps, 1 if...  26.1 us
    pallas_call x2, Pallas kernels, place(): pl.pallas_call(functools.partial(place_kernel, chunk * slots, capacity),...  25.3 us
    all_to_all x3, starting transfers between devices, exchange(): return lax.all_to_all(array, axis, split_axis=0, concat_axis=0, tiled=True)  23.8 us
    ppermute x6, waiting for transfers between devices, shards(): lax.ppermute(sums[d], 'y', shifts[d])  11.1 us
    all_to_all x1, blocking collectives, exchange(): return lax.all_to_all(array, axis, split_axis=0, concat_axis=0, tiled=True)  10.3 us
    ppermute x6, starting transfers between devices, shards(): lax.ppermute(sums[d], 'y', shifts[d])  9.57 us
    ppermute x3, waiting for transfers between devices, shards(): lax.ppermute(mine, 'y', shifts[ny - d])  7.01 us
  transfers between devices with their start and end apart: 12, of which 9 were waited for; matrix products, arithmetic and copies ran while one was open for 1% of the time, Pallas kernels for 16%

profile of v2, /device:TPU:2, one launch (start us, length us, event | category | flops | bytes accessed | tf_op | source)
XLA Modules:
  0.0 211.4 jit_solution(15752083850923987930)
XLA Ops:
  0.6 1.8 broadcast_in_dim.2
  2.4 8.0 %all-to-all-start = ((bf16[16,16,1024]{2,1,0:T(8,128)(2,1)}), bf16[16,16,1024]{2,1,0:T(8,128)(2,1)S(1)}, u32[]{:S(2)}, u32[]{:S(2)}) async-start(bf16[16,16,1024]{2,1,0:T(8,128)(2,1)} %bitcast), calls=%async_computation | async-start | bytes 1048576 | tf_op jit(solution)/shard_map/all_to_all | solution.py:232
  10.5 1.3 copy.9.owner_ref
  11.8 1.7 targets.1.target_ref
  13.5 12.7 %place.3 = bf16[32,64,1024]{2,1,0:T(8,128)(2,1)} custom-call(s32[1,2048]{1,0:T(1,128)} %targets.1.target_ref, bf16[2048,1024]{1,0:T(8,128)(2,1)} %points_ref.3), custom_call_target="tpu_custom_call" | custom-call | flops 8589934592 | bytes 8388608 | tf_op jit(solution)/shard_map/place/pallas_call | solution.py:70
  26.2 0.0 all-to-all-done
  26.2 7.9 %all-to-all-start.2 = ((bf16[32,64,1024]{2,1,0:T(8,128)(2,1)}), bf16[32,64,1024]{2,1,0:T(8,128)(2,1)}, u32[]{:S(2)}, u32[]{:S(2)}) async-start(bf16[32,64,1024]{2,1,0:T(8,128)(2,1)} %place.3), calls=%async_computation.2 | async-start | bytes 8388608 | tf_op jit(solution)/shard_map/all_to_all | solution.py:232
  34.1 12.6 %place.2 = bf16[32,64,1024]{2,1,0:T(8,128)(2,1)} custom-call(s32[1,2048]{1,0:T(1,128)} %targets.1.target_ref, bf16[2048,1024]{1,0:T(8,128)(2,1)} %points_ref.3), custom_call_target="tpu_custom_call" | custom-call | flops 8589934592 | bytes 8388608 | tf_op jit(solution)/shard_map/place/pallas_call | solution.py:70
  46.7 37.9 %all-to-all-done.2.refs_4_ = bf16[32,64,1024]{2,1,0:T(8,128)(2,1)} async-done(((bf16[32,64,1024]{2,1,0:T(8,128)(2,1)}), bf16[32,64,1024]{2,1,0:T(8,128)(2,1)}, u32[]{:S(2)}, u32[]{:S(2)}) %all-to-all-start.2) | async-done | bytes 4194336 | tf_op jit(solution)/shard_map/all_to_all | solution.py:232
  84.6 7.8 %all-to-all-start.1 = ((bf16[32,64,1024]{2,1,0:T(8,128)(2,1)}), bf16[32,64,1024]{2,1,0:T(8,128)(2,1)}, u32[]{:S(2)}, u32[]{:S(2)}) async-start(bf16[32,64,1024]{2,1,0:T(8,128)(2,1)} %place.2), calls=%async_computation.1 | async-start | bytes 8388608 | tf_op jit(solution)/shard_map/all_to_all | solution.py:232
  92.6 0.8 dynamic-slice_bitcast_fusion
  93.4 7.0 %cluster_sums.3 = (f32[256,1024]{1,0:T(8,128)}, f32[256,1]{1,0:T(8,128)}) custom-call(bf16[64,1024]{1,0:T(8,128)(2,1)} %get-tuple-element.25.refs_0_.refs_4_, bf16[64,1024]{1,0:T(8,128)(2,1)} %get-tuple-element.24.refs_1_, bf16[64,1024]{1,0:T(8,128)(2,1)} %get-tuple-element.23.refs_2_, bf16[64,1024]{1,0:T(8,128)(2,1)} %get-tuple-element.22.refs_3_, ...), custom_call_target="tpu_custom_call" | custom-call | flops 2147483648 | bytes 5242880 | tf_op jit(solution)/shard_map/cluster_sums/pallas_call | solution.py:178
  100.4 42.6 %all-to-all-done.1.refs_4_.refs_5_ = bf16[32,64,1024]{2,1,0:T(8,128)(2,1)} async-done(((bf16[32,64,1024]{2,1,0:T(8,128)(2,1)}), bf16[32,64,1024]{2,1,0:T(8,128)(2,1)}, u32[]{:S(2)}, u32[]{:S(2)}) %all-to-all-start.1) | async-done | bytes 4194336 | tf_op jit(solution)/shard_map/all_to_all | solution.py:232
  143.0 7.3 %cluster_sums.4 = (bf16[64,1152]{1,0:T(8,128)(2,1)}, bf16[64,1152]{1,0:T(8,128)(2,1)}, bf16[64,1152]{1,0:T(8,128)(2,1)}, bf16[64,1152]{1,0:T(8,128)(2,1)}) custom-call(bf16[64,1024]{1,0:T(8,128)(2,1)} %get-tuple-element.25.refs_0_.refs_4_, bf16[64,1024]{1,0:T(8,128)(2,1)} %get-tuple-element.24.refs_1_, bf16[64,1024]{1,0:T(8,128)(2,1)} %get-tuple-element.23.refs_2_, ...), custom_call_target="tpu_custom_call" | custom-call | flops 2147483648 | bytes 5242880 | tf_op jit(solution)/shard_map/cluster_sums/pallas_call | solution.py:178
  150.3 1.5 collective-permute-start
  151.7 2.7 %collective-permute-start.1 = (bf16[64,1152]{1,0:T(8,128)(2,1)}, bf16[64,1152]{1,0:T(8,128)(2,1)S(1)}, u32[]{:S(2)}, u32[]{:S(2)}) collective-permute-start(bf16[64,1152]{1,0:T(8,128)(2,1)} %get-tuple-element.16), channel_id=1, source_target_pairs={{0,2},{1,3},{2,0},{3,1},{4,6},{5,7},{6,4},{7,5},{8,10},{9,11},{10,... | collective-permute-start | bytes 442376 | tf_op jit(solution)/shard_map/ppermute | solution.py:264
  154.4 1.5 collective-permute-start.2
  155.9 1.7 collective-permute-done.refs_1_
  157.5 0.0 copy-start
  157.5 3.6 %collective-permute-done.1.refs_2_ = bf16[64,1152]{1,0:T(8,128)(2,1)S(1)} collective-permute-done((bf16[64,1152]{1,0:T(8,128)(2,1)}, bf16[64,1152]{1,0:T(8,128)(2,1)S(1)}, u32[]{:S(2)}, u32[]{:S(2)}) %collective-permute-start.1) | collective-permute-done | bytes 147488 | tf_op jit(solution)/shard_map/ppermute | solution.py:264
  161.1 0.0 copy-start.2
  161.1 0.0 collective-permute-done.2.refs_3_
  161.2 0.0 copy-start.4
  161.2 0.0 copy-done
  161.2 0.7 copy-done.2
  161.8 0.1 copy-done.4
  161.9 2.0 update.2.refs_0_.refs_4_
  163.8 2.3 %collective-permute-start.3 = (bf16[64,1024]{1,0:T(8,128)(2,1)}, bf16[64,1024]{1,0:T(8,128)(2,1)S(1)}, u32[]{:S(2)}, u32[]{:S(2)}) collective-permute-start(bf16[64,1024]{1,0:T(8,128)(2,1)} %update.2.refs_0_.refs_4_), channel_id=1, source_target_pairs={{0,3},{1,0},{2,1},{3,2},{4,7},{5,4},{6,5},{7,6},{8,11},{9,8},{10,9... | collective-permute-start | bytes 393224 | tf_op jit(solution)/shard_map/ppermute | solution.py:267
  166.1 1.1 collective-permute-start.4
  167.2 0.6 collective-permute-start.5
  167.9 3.4 %collective-permute-done.3.refs_1_ = bf16[64,1024]{1,0:T(8,128)(2,1)S(1)} collective-permute-done((bf16[64,1024]{1,0:T(8,128)(2,1)}, bf16[64,1024]{1,0:T(8,128)(2,1)S(1)}, u32[]{:S(2)}, u32[]{:S(2)}) %collective-permute-start.3) | collective-permute-done | bytes 131104 | tf_op jit(solution)/shard_map/ppermute | solution.py:267
  171.3 0.0 copy-start.6
  171.3 2.2 %collective-permute-done.4.refs_2_ = bf16[64,1024]{1,0:T(8,128)(2,1)S(1)} collective-permute-done((bf16[64,1024]{1,0:T(8,128)(2,1)}, bf16[64,1024]{1,0:T(8,128)(2,1)S(1)}, u32[]{:S(2)}, u32[]{:S(2)}) %collective-permute-start.4) | collective-permute-done | bytes 131104 | tf_op jit(solution)/shard_map/ppermute | solution.py:267
  173.5 0.0 copy-start.7
  173.5 1.3 collective-permute-done.5.refs_3_
  174.9 0.0 copy-done.6
  174.9 0.0 copy-done.7
  174.9 0.0 copy-start.8
  174.9 0.7 copy-done.8
  175.5 11.8 %cluster_sums.5 = (bf16[64,1152]{1,0:T(8,128)(2,1)}, bf16[64,1152]{1,0:T(8,128)(2,1)}, bf16[64,1152]{1,0:T(8,128)(2,1)}, bf16[64,1152]{1,0:T(8,128)(2,1)}) custom-call(bf16[64,1024]{1,0:T(8,128)(2,1)} %update.2.refs_0_.refs_4_, bf16[64,1024]{1,0:T(8,128)(2,1)} %copy-done.6, bf16[64,1024]{1,0:T(8,128)(2,1)} %copy-done.7, bf16[64,1024]{1,0:T(8,128)(2,1)} %copy-done.8, ...), custom_call_target="tpu_custom_call" | custom-call | flops 4294967296 | bytes 9437184 | tf_op jit(solution)/shard_map/cluster_sums/pallas_call | solution.py:178
  187.3 0.0 collective-permute-start.6
  187.3 2.2 %collective-permute-start.7 = (bf16[64,1152]{1,0:T(8,128)(2,1)}, bf16[64,1152]{1,0:T(8,128)(2,1)S(1)}, u32[]{:S(2)}, u32[]{:S(2)}) collective-permute-start(bf16[64,1152]{1,0:T(8,128)(2,1)} %get-tuple-element.20), channel_id=1, source_target_pairs={{0,2},{1,3},{2,0},{3,1},{4,6},{5,7},{6,4},{7,5},{8,10},{9,11},{10,... | collective-permute-start | bytes 442376 | tf_op jit(solution)/shard_map/ppermute | solution.py:264
  189.5 1.8 collective-permute-start.8
  191.3 5.2 %collective-permute-done.6.refs_1_ = bf16[64,1152]{1,0:T(8,128)(2,1)S(1)} collective-permute-done((bf16[64,1152]{1,0:T(8,128)(2,1)}, bf16[64,1152]{1,0:T(8,128)(2,1)S(1)}, u32[]{:S(2)}, u32[]{:S(2)}) %collective-permute-start.6) | collective-permute-done | bytes 147488 | tf_op jit(solution)/shard_map/ppermute | solution.py:264
  196.5 0.0 copy-start.1
  196.5 0.0 collective-permute-done.7.refs_2_
  196.5 0.0 copy-start.3
  196.5 0.6 collective-permute-done.8.refs_3_
  197.1 0.0 copy-start.5
  197.1 0.1 copy-done.1
  197.2 0.0 copy-done.3
  197.2 0.5 copy-done.5
  197.8 2.0 update.3
  199.7 10.3 %all_to_all.20 = bf16[4,16,1152]{2,1,0:T(8,128)(2,1)S(1)} all-to-all(bf16[4,16,1152]{2,1,0:T(8,128)(2,1)} %bitcast.18), channel_id=1, replica_groups=mesh['x'=4,'core'=2,'z'=4,'y'=4] {'z'}, dimensions={0} | all-to-all | bytes 294912 | tf_op jit(solution)/shard_map/all_to_all | solution.py:232
  210.0 0.7 slice.8
  210.7 0.7 convert_reduce_fusion
  (1 shorter events, 0.0 us)
Async XLA Ops:
  2.4 23.8 %all-to-all-start = ((bf16[16,16,1024]{2,1,0:T(8,128)(2,1)}), bf16[16,16,1024]{2,1,0:T(8,128)(2,1)S(1)}, u32[]{:S(2)}, u32[]{:S(2)}) async-start(bf16[16,16,1024]{2,1,0:T(8,128)(2,1)} %bitcast), calls=%async_computation | async-start | bytes 1048576 | tf_op jit(solution)/shard_map/all_to_all | solution.py:232
  26.2 58.5 %all-to-all-start.2 = ((bf16[32,64,1024]{2,1,0:T(8,128)(2,1)}), bf16[32,64,1024]{2,1,0:T(8,128)(2,1)}, u32[]{:S(2)}, u32[]{:S(2)}) async-start(bf16[32,64,1024]{2,1,0:T(8,128)(2,1)} %place.3), calls=%async_computation.2 | async-start | bytes 8388608 | tf_op jit(solution)/shard_map/all_to_all | solution.py:232
  84.6 58.4 %all-to-all-start.1 = ((bf16[32,64,1024]{2,1,0:T(8,128)(2,1)}), bf16[32,64,1024]{2,1,0:T(8,128)(2,1)}, u32[]{:S(2)}, u32[]{:S(2)}) async-start(bf16[32,64,1024]{2,1,0:T(8,128)(2,1)} %place.2), calls=%async_computation.1 | async-start | bytes 8388608 | tf_op jit(solution)/shard_map/all_to_all | solution.py:232
  150.3 7.3 %collective-permute-start = (bf16[64,1152]{1,0:T(8,128)(2,1)}, bf16[64,1152]{1,0:T(8,128)(2,1)S(1)}, u32[]{:S(2)}, u32[]{:S(2)}) collective-permute-start(bf16[64,1152]{1,0:T(8,128)(2,1)} %get-tuple-element.15), channel_id=1, source_target_pairs={{0,1},{1,2},{2,3},{3,0},{4,5},{5,6},{6,7},{7,4},{8,9},{9,10},{10,1... | collective-permute-start | bytes 442376 | tf_op jit(solution)/shard_map/ppermute | solution.py:264
  151.7 9.4 %collective-permute-start.1 = (bf16[64,1152]{1,0:T(8,128)(2,1)}, bf16[64,1152]{1,0:T(8,128)(2,1)S(1)}, u32[]{:S(2)}, u32[]{:S(2)}) collective-permute-start(bf16[64,1152]{1,0:T(8,128)(2,1)} %get-tuple-element.16), channel_id=1, source_target_pairs={{0,2},{1,3},{2,0},{3,1},{4,6},{5,7},{6,4},{7,5},{8,10},{9,11},{10,... | collective-permute-start | bytes 442376 | tf_op jit(solution)/shard_map/ppermute | solution.py:264
  154.4 6.8 %collective-permute-start.2 = (bf16[64,1152]{1,0:T(8,128)(2,1)}, bf16[64,1152]{1,0:T(8,128)(2,1)S(1)}, u32[]{:S(2)}, u32[]{:S(2)}) collective-permute-start(bf16[64,1152]{1,0:T(8,128)(2,1)} %get-tuple-element.17), channel_id=1, source_target_pairs={{0,3},{1,0},{2,1},{3,2},{4,7},{5,4},{6,5},{7,6},{8,11},{9,8},{10,9... | collective-permute-start | bytes 442376 | tf_op jit(solution)/shard_map/ppermute | solution.py:264
  157.5 3.6 %copy-start = (bf16[64,1152]{1,0:T(8,128)(2,1)}, bf16[64,1152]{1,0:T(8,128)(2,1)S(1)}, u32[]{:S(2)}) copy-start(bf16[64,1152]{1,0:T(8,128)(2,1)S(1)} %collective-permute-done.refs_1_) | copy-start | bytes 442372
  161.1 0.7 copy-start.2
  161.2 0.7 copy-start.4
  163.8 7.5 %collective-permute-start.3 = (bf16[64,1024]{1,0:T(8,128)(2,1)}, bf16[64,1024]{1,0:T(8,128)(2,1)S(1)}, u32[]{:S(2)}, u32[]{:S(2)}) collective-permute-start(bf16[64,1024]{1,0:T(8,128)(2,1)} %update.2.refs_0_.refs_4_), channel_id=1, source_target_pairs={{0,3},{1,0},{2,1},{3,2},{4,7},{5,4},{6,5},{7,6},{8,11},{9,8},{10,9... | collective-permute-start | bytes 393224 | tf_op jit(solution)/shard_map/ppermute | solution.py:267
  166.1 7.4 %collective-permute-start.4 = (bf16[64,1024]{1,0:T(8,128)(2,1)}, bf16[64,1024]{1,0:T(8,128)(2,1)S(1)}, u32[]{:S(2)}, u32[]{:S(2)}) collective-permute-start(bf16[64,1024]{1,0:T(8,128)(2,1)} %update.2.refs_0_.refs_4_), channel_id=1, source_target_pairs={{0,2},{1,3},{2,0},{3,1},{4,6},{5,7},{6,4},{7,5},{8,10},{9,11},{10,... | collective-permute-start | bytes 393224 | tf_op jit(solution)/shard_map/ppermute | solution.py:267
  167.2 7.6 %collective-permute-start.5 = (bf16[64,1024]{1,0:T(8,128)(2,1)}, bf16[64,1024]{1,0:T(8,128)(2,1)S(1)}, u32[]{:S(2)}, u32[]{:S(2)}) collective-permute-start(bf16[64,1024]{1,0:T(8,128)(2,1)} %update.2.refs_0_.refs_4_), channel_id=1, source_target_pairs={{0,1},{1,2},{2,3},{3,0},{4,5},{5,6},{6,7},{7,4},{8,9},{9,10},{10,1... | collective-permute-start | bytes 393224 | tf_op jit(solution)/shard_map/ppermute | solution.py:267
  171.3 3.6 %copy-start.6 = (bf16[64,1024]{1,0:T(8,128)(2,1)}, bf16[64,1024]{1,0:T(8,128)(2,1)S(1)}, u32[]{:S(2)}) copy-start(bf16[64,1024]{1,0:T(8,128)(2,1)S(1)} %collective-permute-done.3.refs_1_) | copy-start | bytes 393220
  173.5 1.3 copy-start.7
  174.9 0.7 copy-start.8
  187.3 9.2 %collective-permute-start.6 = (bf16[64,1152]{1,0:T(8,128)(2,1)}, bf16[64,1152]{1,0:T(8,128)(2,1)S(1)}, u32[]{:S(2)}, u32[]{:S(2)}) collective-permute-start(bf16[64,1152]{1,0:T(8,128)(2,1)} %get-tuple-element.19), channel_id=1, source_target_pairs={{0,1},{1,2},{2,3},{3,0},{4,5},{5,6},{6,7},{7,4},{8,9},{9,10},{10,1... | collective-permute-start | bytes 442376 | tf_op jit(solution)/shard_map/ppermute | solution.py:264
  187.3 9.2 %collective-permute-start.7 = (bf16[64,1152]{1,0:T(8,128)(2,1)}, bf16[64,1152]{1,0:T(8,128)(2,1)S(1)}, u32[]{:S(2)}, u32[]{:S(2)}) collective-permute-start(bf16[64,1152]{1,0:T(8,128)(2,1)} %get-tuple-element.20), channel_id=1, source_target_pairs={{0,2},{1,3},{2,0},{3,1},{4,6},{5,7},{6,4},{7,5},{8,10},{9,11},{10,... | collective-permute-start | bytes 442376 | tf_op jit(solution)/shard_map/ppermute | solution.py:264
  189.5 7.6 %collective-permute-start.8 = (bf16[64,1152]{1,0:T(8,128)(2,1)}, bf16[64,1152]{1,0:T(8,128)(2,1)S(1)}, u32[]{:S(2)}, u32[]{:S(2)}) collective-permute-start(bf16[64,1152]{1,0:T(8,128)(2,1)} %get-tuple-element.21), channel_id=1, source_target_pairs={{0,3},{1,0},{2,1},{3,2},{4,7},{5,4},{6,5},{7,6},{8,11},{9,8},{10,9... | collective-permute-start | bytes 442376 | tf_op jit(solution)/shard_map/ppermute | solution.py:264
  196.5 0.7 copy-start.1
  196.5 0.7 copy-start.3
  197.1 0.7 copy-start.5

commit v3 on v0

v3 whole, which is shorter than its diff:
```python
import functools

import jax
import jax.numpy as jnp
from jax import lax
from jax.experimental import pallas as pl
from jax.experimental.pallas import tpu as pltpu
from jax.sharding import Mesh, PartitionSpec as P

ITERS = 2
SCORE_SCALE = 0.25
PRIOR_WEIGHT = 1.0
EXTRA = 128
MARK = 1024.0
MARK_LIMIT = 512.0
GROUP = 256
SUB = 8
MIB = 1024 * 1024
VMEM = 60 * MIB
RING = 4
LINE_Z = 6
TILE = 8
AXES = ("x", "core", "z", "y")
SWAPPED = ((1, 0, 0), (3, 0, 0), (1, 3, 0), (3, 1, 0), (2, 0, 0))
DIRECT = ((1, 0, 3), (3, 0, 1), (0, 1, 3), (0, 3, 1))


def scatter_kernel(capacity, where, ids_ref, base_ref, points_ref, *refs):
    outs, (slots_v, slots_s, x, wide, placed, packed, in_sems, out_sems, slot_sem) = (
        refs[:-9],
        refs[-9:],
    )
    rows, width = points_ref.shape
    lanes = width // SUB
    parts = in_sems.shape[0]
    part = rows // parts
    loads = [
        pltpu.make_async_copy(
            points_ref.at[pl.ds(p * part, part)], x.at[pl.ds(p * part, part)], in_sems.at[p]
        )
        for p in range(parts)
    ]
    for load in loads:
        load.start()

    clusters = base_ref.shape[0]
    before = (
        lax.broadcasted_iota(jnp.int32, (GROUP, GROUP), 0)
        < lax.broadcasted_iota(jnp.int32, (GROUP, GROUP), 1)
    ).astype(jnp.float32).astype(jnp.bfloat16)
    table = lax.broadcasted_iota(jnp.int32, (clusters, GROUP), 0)
    base = base_ref[...].astype(jnp.float32)
    for g in range(rows // GROUP):
        span = pl.ds(g * GROUP, GROUP)
        hit = (table == ids_ref[:, span]).astype(jnp.float32)
        place = jnp.dot(hit.astype(jnp.bfloat16), before, preferred_element_type=jnp.float32)
        slot = jnp.sum(hit * (place + base), axis=0, keepdims=True).astype(jnp.int32)
        slots_v[:, span] = (slot // SUB) * (SUB * SUB) + slot % SUB
        base = base + jnp.sum(hit, axis=1, keepdims=True)
    to_scalars = pltpu.make_async_copy(slots_v, slots_s, slot_sem)
    to_scalars.start()

    def clear(i, _):
        placed[pl.ds(i * 256, 256)] = jnp.full((256, lanes), MARK, jnp.float32)
        return 0

    lax.fori_loop(0, placed.shape[0] // 256, clear, 0)

    def widen(i, _):
        two = x[pl.ds(i * 2 * SUB, 2 * SUB)].astype(jnp.float32)
        for h in range(2):
            for t in range(SUB):
                wide[pl.ds(((2 * i + h) * SUB + t) * SUB, SUB)] = two[
                    h * SUB : (h + 1) * SUB, t * lanes : (t + 1) * lanes
                ]
        return 0

    for p in range(parts):
        loads[p].wait()
        steps = part // (2 * SUB)
        lax.fori_loop(p * steps, (p + 1) * steps, widen, 0, unroll=2)
    to_scalars.wait()

    def move_rows(i, _):
        for r in range(2 * SUB):
            row = wide[pl.ds(i * 2 * SUB * SUB + r // SUB * SUB * SUB + r % SUB, SUB, stride=SUB)]
            placed[pl.ds(slots_s[0, i * 2 * SUB + r], SUB, stride=SUB)] = row
        return 0

    lax.fori_loop(0, rows // (2 * SUB), move_rows, 0)

    stores = []
    for n, (o, k) in enumerate(where):

        def narrow(i, _, n=n):
            first = n * capacity * SUB + i * 2 * SUB * SUB
            for t in range(SUB):
                low = placed[pl.ds(first + t * SUB, SUB)]
                high = placed[pl.ds(first + (SUB + t) * SUB, SUB)]
                packed[n, pl.ds(i * 2 * SUB, 2 * SUB), t * lanes : (t + 1) * lanes] = (
                    jnp.concatenate([low, high], axis=0).astype(jnp.bfloat16)
                )
            return 0

        lax.fori_loop(0, capacity // (2 * SUB), narrow, 0, unroll=2)
        stores.append(pltpu.make_async_copy(packed.at[n], outs[o].at[k], out_sems.at[n]))
        stores[-1].start()
    for store in stores:
        store.wait()


def scatter(cluster_ids, base, points, capacity, blocks):
    rows, width = points.shape
    where = [(o, k) for o, count in enumerate(blocks) for k in range(count)]
    any_space = pl.BlockSpec(memory_space=pl.ANY)
    whole = pl.BlockSpec(memory_space=pltpu.VMEM)
    lanes = width // SUB
    parts = 8
    return pl.pallas_call(
        functools.partial(scatter_kernel, capacity, where),
        in_specs=[whole, whole, any_space],
        out_specs=[any_space] * len(blocks),
        out_shape=[jax.ShapeDtypeStruct((n, capacity, width), jnp.bfloat16) for n in blocks],
        scratch_shapes=[
            pltpu.VMEM((1, rows), jnp.int32),
            pltpu.SMEM((1, rows), jnp.int32),
            pltpu.VMEM((rows, width), jnp.bfloat16),
            pltpu.VMEM((rows * SUB, lanes), jnp.float32),
            pltpu.VMEM((len(where) * capacity * SUB, lanes), jnp.float32),
            pltpu.VMEM((len(where), capacity, width), jnp.bfloat16),
            pltpu.SemaphoreType.DMA((parts,)),
            pltpu.SemaphoreType.DMA((len(where),)),
            pltpu.SemaphoreType.DMA,
        ],
        compiler_params=pltpu.CompilerParams(vmem_limit_bytes=VMEM),
        cost_estimate=pl.CostEstimate(
            flops=rows * width,
            bytes_accessed=8 * width * (rows + len(where) * capacity),
            transcendentals=0,
        ),
        name="scatter",
    )(cluster_ids.reshape(1, rows), base.reshape(-1, 1), points)


def sums_kernel(groups, counts, carried, finish, z_ref, *refs):
    blocks, refs = refs[:groups], refs[groups:]
    sources, refs = refs[: len(counts)], refs[len(counts) :]
    carry, refs = refs[: 2 * carried], refs[2 * carried :]
    outs, (aug, total, mass, bias, rows, sems) = refs[:-6], refs[-6:]
    held, width = blocks[0].shape
    cents = groups * held
    pieces = []
    for ref, count in zip(sources, counts):
        if count == LINE_Z:
            pieces += [
                (ref, c * RING + lax.rem(z_ref[0] + d, RING)) for c in range(2) for d in range(1, RING)
            ]
        else:
            pieces += [(ref, i) for i in range(count)]
    for n, (ref, i) in enumerate(pieces):
        pltpu.make_async_copy(ref.at[i], rows.at[n], sems.at[n]).start()

    for g in range(groups):
        mu = blocks[g][...]
        span = pl.ds(g * held, held)
        aug[span] = mu
        wide = mu.astype(jnp.float32)
        bias[span] = 0.5 * jnp.sum(wide * wide, axis=1, keepdims=True)
    unit = lax.broadcasted_iota(jnp.int32, (aug.shape[0] - cents, width), 1) == 0
    aug[cents:] = unit.astype(jnp.float32).astype(jnp.bfloat16)
    if carried:
        total[...] = carry[0][...]
        mass[...] = carry[1][...]
    else:
        total[...] = jnp.zeros_like(total)
        mass[...] = jnp.zeros_like(mass)

    def tile(t, _):
        for i in range(TILE):
            n = t * TILE + i
            pltpu.make_async_copy(sources[0].at[0], rows.at[n], sems.at[n]).wait()
        x = rows[pl.ds(t * TILE, TILE)].reshape(-1, width)
        raw = lax.dot_general(
            aug[...], x, (((1,), (1,)), ((), ())), preferred_element_type=jnp.float32
        )
        score = (raw[:cents] - bias[...]) * SCORE_SCALE
        present = (raw[cents : cents + 1] < MARK_LIMIT).astype(jnp.float32)
        e = jnp.exp(score - jnp.max(score, axis=0, keepdims=True))
        w = e * (present / jnp.sum(e, axis=0, keepdims=True))
        mass[...] += jnp.sum(w, axis=1, keepdims=True)
        total[...] += jnp.dot(w.astype(jnp.bfloat16), x, preferred_element_type=jnp.float32)
        return 0

    lax.fori_loop(0, len(pieces) // TILE, tile, 0)
    if not finish:
        outs[0][...] = total[...]
        outs[1][...] = mass[...]
        return
    lane = lax.broadcasted_iota(jnp.int32, (held, EXTRA), 1)
    for g in range(groups):
        span = pl.ds(g * held, held)
        outs[g][:, :width] = total[span].astype(jnp.bfloat16)
        outs[g][:, width:] = terms(mass[span], lane)


def cluster_sums(z, blocks, sources, counts, carry=(), finish=True):
    groups = len(blocks)
    held, width = blocks[0].shape
    capacity = sources[0].shape[1]
    cents, pieces = groups * held, sum(counts)
    assert pieces % TILE == 0
    whole = pl.BlockSpec(memory_space=pltpu.VMEM)
    if finish:
        shapes = [jax.ShapeDtypeStruct((held, width + EXTRA), jnp.bfloat16)] * groups
    else:
        shapes = [
            jax.ShapeDtypeStruct((cents, width), jnp.float32),
            jax.ShapeDtypeStruct((cents, 1), jnp.float32),
        ]
    count = pieces * capacity
    return pl.pallas_call(
        functools.partial(sums_kernel, groups, counts, 1 if carry else 0, finish),
        in_specs=[pl.BlockSpec(memory_space=pltpu.SMEM)]
        + [whole] * groups
        + [pl.BlockSpec(memory_space=pl.ANY)] * len(sources)
        + [whole] * len(carry),
        out_specs=[whole] * len(shapes),
        out_shape=shapes,
        scratch_shapes=[
            pltpu.VMEM((cents + 16, width), jnp.bfloat16),
            pltpu.VMEM((cents, width), jnp.float32),
            pltpu.VMEM((cents, 1), jnp.float32),
            pltpu.VMEM((cents, 1), jnp.float32),
            pltpu.VMEM((pieces, capacity, width), jnp.bfloat16),
            pltpu.SemaphoreType.DMA((pieces,)),
        ],
        compiler_params=pltpu.CompilerParams(vmem_limit_bytes=VMEM),
        cost_estimate=pl.CostEstimate(
            flops=4 * count * cents * width,
            bytes_accessed=2 * width * (count + 2 * cents),
            transcendentals=count * cents,
        ),
        name="cluster_sums",
    )(z.reshape(1), *blocks, *sources, *carry)


def terms(m, lane):
    hi = m.astype(jnp.bfloat16).astype(jnp.float32)
    mid = (m - hi).astype(jnp.bfloat16).astype(jnp.float32)
    low = m - hi - mid
    parts = jnp.where(lane == 0, hi, jnp.where(lane == 1, mid, jnp.where(lane == 2, low, 0.0)))
    return parts.astype(jnp.bfloat16)


def update_kernel(packed, count, *refs):
    parts, mu_ref, out_ref = refs[:count], refs[count], refs[count + 1]
    rows, width = mu_ref.shape
    total = parts[0][...].astype(jnp.float32)
    for s in range(1, count):
        total = total + parts[s][...].astype(jnp.float32)
    mass = jnp.sum(total[:, width:], axis=1, keepdims=True)
    mu = mu_ref[...].astype(jnp.float32)
    new = (total[:, :width] + PRIOR_WEIGHT * mu) / (mass + PRIOR_WEIGHT)
    out_ref[:, :width] = new.astype(jnp.bfloat16)
    if packed:
        out_ref[:, width:] = terms(mass, lax.broadcasted_iota(jnp.int32, (rows, EXTRA), 1))


def update(parts, mu, packed):
    rows, width = mu.shape
    return pl.pallas_call(
        functools.partial(update_kernel, packed, len(parts)),
        out_shape=jax.ShapeDtypeStruct((rows, width + (EXTRA if packed else 0)), jnp.bfloat16),
        compiler_params=pltpu.CompilerParams(vmem_limit_bytes=VMEM),
        cost_estimate=pl.CostEstimate(
            flops=len(parts) * rows * width,
            bytes_accessed=2 * (len(parts) + 2) * rows * width,
            transcendentals=0,
        ),
        name="update",
    )(*parts, mu)


def spread_kernel(in_ref, out_ref):
    for i in range(RING):
        for k in range(RING):
            out_ref[i * RING + k] = in_ref[(i - k) % RING]


def spread(centroids):
    return pl.pallas_call(
        spread_kernel,
        out_shape=jax.ShapeDtypeStruct((RING * RING,) + centroids.shape[1:], centroids.dtype),
        compiler_params=pltpu.CompilerParams(vmem_limit_bytes=VMEM),
        name="spread",
    )(centroids)


def finish_kernel(first_ref, *refs):
    parts, (new_ref, mass_ref) = refs[:RING], refs[RING:]
    width = new_ref.shape[2]
    ones = jnp.ones((8, EXTRA), jnp.bfloat16)
    for d in range(RING):
        j = lax.rem(first_ref[0] - d + RING, RING)
        new_ref[j] = parts[d][:, :width]
        mass = lax.dot_general(
            ones, parts[d][:, width:], (((1,), (1,)), ((), ())), preferred_element_type=jnp.float32
        )
        mass_ref[pl.ds(j, 1)] = mass[:1]


def finish(parts, first):
    rows, width = parts[0].shape
    whole = pl.BlockSpec(memory_space=pltpu.VMEM)
    return pl.pallas_call(
        finish_kernel,
        in_specs=[pl.BlockSpec(memory_space=pltpu.SMEM)] + [whole] * RING,
        out_specs=[whole] * 2,
        out_shape=[
            jax.ShapeDtypeStruct((RING, rows, width - EXTRA), jnp.bfloat16),
            jax.ShapeDtypeStruct((RING, rows), jnp.float32),
        ],
        compiler_params=pltpu.CompilerParams(vmem_limit_bytes=VMEM),
        name="finish",
    )(first.reshape(1), *parts)


def exchange(array, axis):
    return lax.all_to_all(array, axis, split_axis=0, concat_axis=0, tiled=True)


def number(x, core, z, y):
    return ((x % RING * 2 + core) * RING + z % RING) * RING + y % RING


def move(array, step):
    pairs = [
        (number(x, c, z, y), number(*step(x, c, z, y)))
        for x in range(RING)
        for c in range(2)
        for z in range(RING)
        for y in range(RING)
    ]
    return lax.ppermute(array, AXES, pairs)


def along(array, dx, dz, dy, flip=0):
    return move(array, lambda x, c, z, y: (x + dx, c ^ flip, z + dz, y + dy))


def first_slots(owner_slot, capacity, x, core, z, y):
    to_x, to_core, j = owner_slot // 8, owner_slot // 4 % 2, owner_slot % 4
    ra, rb = (to_x - x + y) % RING, (j - z + y) % RING
    block = 2 * RING + to_core * RING + (j + y) % RING
    block = jnp.where(ra == rb, to_core * RING + (y - ra) % RING, block)
    n = 4 * RING
    for dx, dz, dy in SWAPPED + DIRECT:
        here = (ra == (dx - dy) % RING) & (rb == (dz - dy) % RING)
        block = jnp.where(here, n + (to_core ^ core), block)
        n += 2
    return block * capacity


def shards(points, cluster_ids, owner_slot, centroids):
    rows, width = points.shape
    capacity = 2 * rows // owner_slot.shape[0]
    held = centroids.shape[1]
    x, core, z, y = (lax.axis_index(a) for a in AXES)

    gathered = exchange(spread(centroids), ("z", "y"))
    gathered = move(gathered, lambda x, c, z, y: (x + y, c, z, y))
    by_y = gathered.reshape(RING, RING, held, width).swapaxes(0, 1).reshape(RING, -1, width)
    blocks = [
        lax.dynamic_index_in_dim(by_y, (y + d) % RING, 0, keepdims=False) for d in range(RING)
    ]
    mine = blocks[0]

    line = 2 * RING
    to_y, to_z, *leaving = scatter(
        cluster_ids,
        first_slots(owner_slot, capacity, x, core, z, y),
        points,
        capacity,
        [line, line] + [2] * len(SWAPPED) + [1] * (2 * len(DIRECT)),
    )
    from_y = exchange(to_y, ("core", "y"))
    from_z = exchange(to_z, ("core", "z"))
    came = [along(leaving[i], *route) for i, route in enumerate(SWAPPED)]
    other = jnp.stack([c[1] for c in came])
    swapped = move(other, lambda x, c, z, y: (x, 1 - c, z, y))
    straight = []
    for i, route in enumerate(DIRECT):
        first = len(SWAPPED) + 2 * i
        straight.append(along(leaving[first], *route))
        straight.append(along(leaving[first + 1], *route, 1))

    arrays = [from_y] + came + [swapped, from_z] + straight
    counts = [line] + [1] * len(SWAPPED) + [len(SWAPPED), LINE_Z] + [1] * len(straight)
    carry = cluster_sums(z, blocks, [from_y], [line], finish=False)
    for iteration in range(ITERS):
        last = iteration == ITERS - 1
        if iteration == 0:
            sums = cluster_sums(z, blocks, arrays[1:], counts[1:], carry)
        else:
            sums = cluster_sums(z, blocks, arrays, counts)
        parts = [sums[0]] + [along(sums[d], d, d, d) for d in range(1, RING)]
        mine = update(parts, mine, last)
        if not last:
            blocks = [mine] + [along(mine, -d, -d, -d) for d in range(1, RING)]
    by_z = mine.reshape(RING, held, width + EXTRA)
    leaving = [lax.dynamic_index_in_dim(by_z, (z + d) % RING, 0, keepdims=False) for d in range(RING)]
    came = [
        move(leaving[d], functools.partial(lambda d, x, c, z, y: (x - y, c, z + d, y), d))
        for d in range(RING)
    ]
    new, mass = finish(came, (z - y) % RING)
    return new, mass


def solution(mesh):
    fine = Mesh(mesh.devices.reshape(RING, 2, RING, RING), AXES)
    point, cent = AXES[:2], AXES[2:]
    return jax.shard_map(
        shards,
        mesh=fine,
        in_specs=(P(point + cent, None), P(point + cent), P(), P(point, cent, None)),
        out_specs=(P(point, cent, None), P(point, cent)),
        check_vma=False,
    )
```

time: 402 us -> 212 us (0.53)
  the two profiles are of different devices: /device:TPU:2 before, /device:TPU:18 now
where the time goes in v3:
time: 212 us; the launch traced here: 211 us
  starting transfers between devices  92.4 us (44%)
  waiting for transfers between devices  62.5 us (29%)
  Pallas kernels  41.3 us (19%)
  local copies, waits for them, and re-layouts  14.2 us (7%)
    ppermute x28, starting transfers between devices, move(): return lax.ppermute(array, AXES, pairs)  74.9 us
    ppermute x28, waiting for transfers between devices, move(): return lax.ppermute(array, AXES, pairs)  56.5 us
    pallas_call x3, Pallas kernels, cluster_sums(): pl.pallas_call(functools.partial(sums_kernel, groups, counts, 1 if carry...  24 us
    all_to_all x3, starting transfers between devices, exchange(): return lax.all_to_all(array, axis, split_axis=0, concat_axis=0, tiled=True)  17.4 us
    unnamed x62, local copies, waits for them, and re-layouts  10.1 us
    pallas_call x1, Pallas kernels, scatter(): pl.pallas_call(functools.partial(scatter_kernel, capacity, where), in_spe...  10.1 us
    all_to_all x3, waiting for transfers between devices, exchange(): return lax.all_to_all(array, axis, split_axis=0, concat_axis=0, tiled=True)  6.02 us
  transfers between devices with their start and end apart: 31, of which 16 were waited for; matrix products, arithmetic and copies ran while one was open for 3% of the time, Pallas kernels for 7%

profile of v3, /device:TPU:18, one launch (start us, length us, event | category | flops | bytes accessed | tf_op | source)
XLA Modules:
  0.0 211.4 jit_solution(12045546060872232804)
XLA Ops:
  0.6 1.7 spread.1
  2.4 8.3 %all-to-all-start = ((bf16[16,16,1024]{2,1,0:T(8,128)(2,1)}), bf16[16,16,1024]{2,1,0:T(8,128)(2,1)S(1)}, u32[]{:S(2)}, u32[]{:S(2)}) async-start(bf16[16,16,1024]{2,1,0:T(8,128)(2,1)} %spread.1), calls=%async_computation | async-start | bytes 1048576 | tf_op jit(solution)/shard_map/all_to_all | solution.py:329
  10.7 0.7 copy.7.base_ref
  11.4 10.1 %scatter.1 = (bf16[8,128,1024]{2,1,0:T(8,128)(2,1)}, bf16[8,128,1024]{2,1,0:T(8,128)(2,1)}, bf16[2,128,1024]{2,1,0:T(8,128)(2,1)}, bf16[2,128,1024]{2,1,0:T(8,12...) custom-call(s32[1,2048]{1,0:T(1,128)} %bitcast.29, ...), custom_call_target="tpu_custom_call" | custom-call | flops 2097152 | bytes 52428800 | tf_op jit(solution)/shard_map/scatter/pallas_call | solution.py:119
  21.5 4.8 %all-to-all-start.2 = ((bf16[8,128,1024]{2,1,0:T(8,128)(2,1)}), bf16[8,128,1024]{2,1,0:T(8,128)(2,1)S(1)}, u32[]{:S(2)}, u32[]{:S(2)}) async-start(bf16[8,128,1024]{2,1,0:T(8,128)(2,1)} %get-tuple-element.41), calls=%async_computation.2 | async-start | bytes 4194304 | tf_op jit(solution)/shard_map/all_to_all | solution.py:329
  26.4 1.5 collective-permute-start.1
  27.8 0.5 collective-permute-start.2
  28.4 3.6 %collective-permute-start.3 = (bf16[2,128,1024]{2,1,0:T(8,128)(2,1)}, bf16[2,128,1024]{2,1,0:T(8,128)(2,1)S(1)}, u32[]{:S(2)}, u32[]{:S(2)}) collective-permute-start(bf16[2,128,1024]{2,1,0:T(8,128)(2,1)} %get-tuple-element.29), channel_id=1, source_target_pairs={{0,44},{1,45},{2,46},{3,47},{4,32},{5,33},{6,34},{7,35},{8,36},{9,... | collective-permute-start | bytes 1572872 | tf_op jit(solution)/shard_map/ppermute | solution.py:344
  32.0 2.3 %collective-permute-start.5 = (bf16[2,128,1024]{2,1,0:T(8,128)(2,1)}, bf16[2,128,1024]{2,1,0:T(8,128)(2,1)}, u32[]{:S(2)}, u32[]{:S(2)}) collective-permute-start(bf16[2,128,1024]{2,1,0:T(8,128)(2,1)} %get-tuple-element.31), channel_id=1, source_target_pairs={{0,64},{1,65},{2,66},{3,67},{4,68},{5,69},{6,70},{7,71},{8,72},{9,... | collective-permute-start | bytes 1572872 | tf_op jit(solution)/shard_map/ppermute | solution.py:344
  34.3 7.0 %collective-permute-done.1.refs_4_.refs_5_ = bf16[2,128,1024]{2,1,0:T(8,128)(2,1)S(1)} collective-permute-done((bf16[2,128,1024]{2,1,0:T(8,128)(2,1)}, bf16[2,128,1024]{2,1,0:T(8,128)(2,1)S(1)}, u32[]{:S(2)}, u32[]{:S(2)}) %collective-permute-start.1) | collective-permute-done | bytes 524320 | tf_op jit(solution)/shard_map/ppermute | solution.py:344
  41.3 0.8 slice_dynamic-update-slice_fusion.4
  42.1 0.7 collective-permute-done.2.refs_5_.refs_6_
  42.9 0.8 copy-done.8
  43.7 0.7 slice_dynamic-update-slice_fusion.3
  44.4 6.0 %all-to-all-done.2.refs_4_ = bf16[8,128,1024]{2,1,0:T(8,128)(2,1)S(1)} async-done(((bf16[8,128,1024]{2,1,0:T(8,128)(2,1)}), bf16[8,128,1024]{2,1,0:T(8,128)(2,1)S(1)}, u32[]{:S(2)}, u32[]{:S(2)}) %all-to-all-start.2) | async-done | bytes 2097184 | tf_op jit(solution)/shard_map/all_to_all | solution.py:329
  50.4 1.3 copy-done
  51.7 4.3 %all-to-all-start.1 = ((bf16[8,128,1024]{2,1,0:T(8,128)(2,1)}), bf16[8,128,1024]{2,1,0:T(8,128)(2,1)}, u32[]{:S(2)}, u32[]{:S(2)}) async-start(bf16[8,128,1024]{2,1,0:T(8,128)(2,1)} %get-tuple-element.32), calls=%async_computation.1 | async-start | bytes 4194304 | tf_op jit(solution)/shard_map/all_to_all | solution.py:329
  56.2 0.7 slice_dynamic-update-slice_fusion.2
  56.9 1.7 slice_dynamic-update-slice_fusion.1
  58.6 6.4 %collective-permute-done.5.refs_8_.refs_9_ = bf16[2,128,1024]{2,1,0:T(8,128)(2,1)} collective-permute-done((bf16[2,128,1024]{2,1,0:T(8,128)(2,1)}, bf16[2,128,1024]{2,1,0:T(8,128)(2,1)}, u32[]{:S(2)}, u32[]{:S(2)}) %collective-permute-start.5) | collective-permute-done | bytes 524320 | tf_op jit(solution)/shard_map/ppermute | solution.py:344
  65.0 1.7 slice_dynamic-update-slice_fusion
  66.7 7.7 %collective-permute-start = (bf16[16,16,1024]{2,1,0:T(8,128)(2,1)S(1)}, bf16[16,16,1024]{2,1,0:T(8,128)(2,1)S(1)}, u32[]{:S(2)}, u32[]{:S(2)}) collective-permute-start(bf16[16,16,1024]{2,1,0:T(8,128)(2,1)S(1)} %all-to-all-done), channel_id=1, source_target_pairs={{0,0},{1,33},{2,66},{3,99},{4,4},{5,37},{6,70},{7,103},{8,8},{9,41... | collective-permute-start | bytes 1572872 | tf_op jit(solution)/shard_map/ppermute | solution.py:344
  74.8 2.4 %collective-permute-start.9 = (bf16[1,128,1024]{2,1,0:T(8,128)(2,1)S(1)}, bf16[1,128,1024]{2,1,0:T(8,128)(2,1)S(1)}, u32[]{:S(2)}, u32[]{:S(2)}) collective-permute-start(bf16[1,128,1024]{2,1,0:T(8,128)(2,1)S(1)} %copy-done.23), channel_id=1, source_target_pairs={{0,97},{1,98},{2,99},{3,96},{4,101},{5,102},{6,103},{7,100},{8,105... | collective-permute-start | bytes 786440 | tf_op jit(solution)/shard_map/ppermute | solution.py:344
  77.2 3.9 %collective-permute-start.10 = (bf16[1,128,1024]{2,1,0:T(8,128)(2,1)S(1)}, bf16[1,128,1024]{2,1,0:T(8,128)(2,1)S(1)}, u32[]{:S(2)}, u32[]{:S(2)}) collective-permute-start(bf16[1,128,1024]{2,1,0:T(8,128)(2,1)S(1)} %copy-done.22), channel_id=1, source_target_pairs={{0,113},{1,114},{2,115},{3,112},{4,117},{5,118},{6,119},{7,116},{8... | collective-permute-start | bytes 786440 | tf_op jit(solution)/shard_map/ppermute | solution.py:344
  81.1 11.3 %collective-permute-done.8.refs_12_.refs_13_ = bf16[1,128,1024]{2,1,0:T(8,128)(2,1)S(1)} collective-permute-done((bf16[1,128,1024]{2,1,0:T(8,128)(2,1)S(1)}, bf16[1,128,1024]{2,1,0:T(8,128)(2,1)S(1)}, u32[]{:S(2)}, u32[]{:S(2)}) %collective-permute-start.8) | collective-permute-done | bytes 262176 | tf_op jit(solution)/shard_map/ppermute | solution.py:344
  92.4 1.5 collective-permute-start.11
  94.0 1.4 collective-permute-start.12
  95.3 2.1 %collective-permute-done.10.refs_14_.refs_15_ = bf16[1,128,1024]{2,1,0:T(8,128)(2,1)S(1)} collective-permute-done((bf16[1,128,1024]{2,1,0:T(8,128)(2,1)S(1)}, bf16[1,128,1024]{2,1,0:T(8,128)(2,1)S(1)}, u32[]{:S(2)}, u32[]{:S(2)}) %collective-permute-start.10) | collective-permute-done | bytes 262176 | tf_op jit(solution)/shard_map/ppermute | solution.py:344
  97.5 2.2 %collective-permute-start.13 = (bf16[1,128,1024]{2,1,0:T(8,128)(2,1)}, bf16[1,128,1024]{2,1,0:T(8,128)(2,1)}, u32[]{:S(2)}, u32[]{:S(2)}) collective-permute-start(bf16[1,128,1024]{2,1,0:T(8,128)(2,1)} %get-tuple-element.39), channel_id=1, source_target_pairs={{0,13},{1,14},{2,15},{3,12},{4,1},{5,2},{6,3},{7,0},{8,5},{9,6},{1... | collective-permute-start | bytes 786440 | tf_op jit(solution)/shard_map/ppermute | solution.py:344
  99.7 2.3 %collective-permute-start.14 = (bf16[1,128,1024]{2,1,0:T(8,128)(2,1)S(1)}, bf16[1,128,1024]{2,1,0:T(8,128)(2,1)S(1)}, u32[]{:S(2)}, u32[]{:S(2)}) collective-permute-start(bf16[1,128,1024]{2,1,0:T(8,128)(2,1)S(1)} %copy-done.18), channel_id=1, source_target_pairs={{0,29},{1,30},{2,31},{3,28},{4,17},{5,18},{6,19},{7,16},{8,21},{9,... | collective-permute-start | bytes 786440 | tf_op jit(solution)/shard_map/ppermute | solution.py:344
  102.0 0.8 dynamic-slice_bitcast_fusion
  102.9 5.3 %cluster_sums.3 = (f32[256,1024]{1,0:T(8,128)}, f32[256,1]{1,0:T(8,128)}) custom-call(s32[1]{0:T(128)} %bitcast.1.z_ref, bf16[64,1024]{1,0:T(8,128)(2,1)} %get-tuple-element.55.refs_0_.refs_4_, bf16[64,1024]{1,0:T(8,128)(2,1)} %get-tuple-element.54.refs_1_, bf16[64,1024]{1,0:T(8,128)(2,1)} %get-tuple-element.53.refs_2_, ...), custom_call_target="tpu_custom_call" | custom-call | flops 1073741824 | bytes 3145728 | tf_op jit(solution)/shard_map/cluster_sums/pallas_call | solution.py:221
  108.2 3.4 %collective-permute-done.14.refs_18_.refs_19_ = bf16[1,128,1024]{2,1,0:T(8,128)(2,1)S(1)} collective-permute-done((bf16[1,128,1024]{2,1,0:T(8,128)(2,1)S(1)}, bf16[1,128,1024]{2,1,0:T(8,128)(2,1)S(1)}, u32[]{:S(2)}, u32[]{:S(2)}) %collective-permute-start.14) | collective-permute-done | bytes 262176 | tf_op jit(solution)/shard_map/ppermute | solution.py:344
  111.6 0.7 copy-done.21
  112.8 8.8 %cluster_sums.4 = (bf16[64,1152]{1,0:T(8,128)(2,1)}, bf16[64,1152]{1,0:T(8,128)(2,1)}, bf16[64,1152]{1,0:T(8,128)(2,1)}, bf16[64,1152]{1,0:T(8,128)(2,1)}) custom-call(s32[1]{0:T(128)} %bitcast.1.z_ref, bf16[64,1024]{1,0:T(8,128)(2,1)} %get-tuple-element.55.refs_0_.refs_4_, bf16[64,1024]{1,0:T(8,128)(2,1)} %get-tuple-element.54.refs_1_, ...), custom_call_target="tpu_custom_call" | custom-call | flops 3221225472 | bytes 7340032 | tf_op jit(solution)/shard_map/cluster_sums/pallas_call | solution.py:221
  121.5 4.8 %collective-permute-start.15 = (bf16[64,1152]{1,0:T(8,128)(2,1)}, bf16[64,1152]{1,0:T(8,128)(2,1)S(1)}, u32[]{:S(2)}, u32[]{:S(2)}) collective-permute-start(bf16[64,1152]{1,0:T(8,128)(2,1)} %get-tuple-element.45), channel_id=1, source_target_pairs={{0,37},{1,38},{2,39},{3,36},{4,41},{5,42},{6,43},{7,40},{8,45},{9,... | collective-permute-start | bytes 442376 | tf_op jit(solution)/shard_map/ppermute | solution.py:344
  126.4 3.8 %collective-permute-start.16 = (bf16[64,1152]{1,0:T(8,128)(2,1)}, bf16[64,1152]{1,0:T(8,128)(2,1)S(1)}, u32[]{:S(2)}, u32[]{:S(2)}) collective-permute-start(bf16[64,1152]{1,0:T(8,128)(2,1)} %get-tuple-element.46), channel_id=1, source_target_pairs={{0,74},{1,75},{2,72},{3,73},{4,78},{5,79},{6,76},{7,77},{8,66},{9,... | collective-permute-start | bytes 442376 | tf_op jit(solution)/shard_map/ppermute | solution.py:344
  130.2 4.3 %collective-permute-start.17 = (bf16[64,1152]{1,0:T(8,128)(2,1)}, bf16[64,1152]{1,0:T(8,128)(2,1)S(1)}, u32[]{:S(2)}, u32[]{:S(2)}) collective-permute-start(bf16[64,1152]{1,0:T(8,128)(2,1)} %get-tuple-element.47), channel_id=1, source_target_pairs={{0,111},{1,108},{2,109},{3,110},{4,99},{5,96},{6,97},{7,98},{8,103... | collective-permute-start | bytes 442376 | tf_op jit(solution)/shard_map/ppermute | solution.py:344
  134.5 5.2 %collective-permute-done.16.refs_2_ = bf16[64,1152]{1,0:T(8,128)(2,1)S(1)} collective-permute-done((bf16[64,1152]{1,0:T(8,128)(2,1)}, bf16[64,1152]{1,0:T(8,128)(2,1)S(1)}, u32[]{:S(2)}, u32[]{:S(2)}) %collective-permute-start.16) | collective-permute-done | bytes 147488 | tf_op jit(solution)/shard_map/ppermute | solution.py:344
  139.6 0.7 collective-permute-done.17.refs_3_
  140.3 0.7 copy-done.6
  141.0 2.0 update.2.refs_0_.refs_4_
  142.9 5.3 %collective-permute-start.18 = (bf16[64,1024]{1,0:T(8,128)(2,1)}, bf16[64,1024]{1,0:T(8,128)(2,1)S(1)}, u32[]{:S(2)}, u32[]{:S(2)}) collective-permute-start(bf16[64,1024]{1,0:T(8,128)(2,1)} %update.2.refs_0_.refs_4_), channel_id=1, source_target_pairs={{0,111},{1,108},{2,109},{3,110},{4,99},{5,96},{6,97},{7,98},{8,103... | collective-permute-start | bytes 393224 | tf_op jit(solution)/shard_map/ppermute | solution.py:344
  148.2 3.7 %collective-permute-start.19 = (bf16[64,1024]{1,0:T(8,128)(2,1)}, bf16[64,1024]{1,0:T(8,128)(2,1)S(1)}, u32[]{:S(2)}, u32[]{:S(2)}) collective-permute-start(bf16[64,1024]{1,0:T(8,128)(2,1)} %update.2.refs_0_.refs_4_), channel_id=1, source_target_pairs={{0,74},{1,75},{2,72},{3,73},{4,78},{5,79},{6,76},{7,77},{8,66},{9,... | collective-permute-start | bytes 393224 | tf_op jit(solution)/shard_map/ppermute | solution.py:344
  151.9 0.6 collective-permute-start.20
  152.5 8.6 %collective-permute-done.19.refs_2_ = bf16[64,1024]{1,0:T(8,128)(2,1)S(1)} collective-permute-done((bf16[64,1024]{1,0:T(8,128)(2,1)}, bf16[64,1024]{1,0:T(8,128)(2,1)S(1)}, u32[]{:S(2)}, u32[]{:S(2)}) %collective-permute-start.19) | collective-permute-done | bytes 131104 | tf_op jit(solution)/shard_map/ppermute | solution.py:344
  161.8 0.7 copy-done.28
  162.4 10.0 %cluster_sums.5 = (bf16[64,1152]{1,0:T(8,128)(2,1)}, bf16[64,1152]{1,0:T(8,128)(2,1)}, bf16[64,1152]{1,0:T(8,128)(2,1)}, bf16[64,1152]{1,0:T(8,128)(2,1)}) custom-call(s32[1]{0:T(128)} %bitcast.1.z_ref, bf16[64,1024]{1,0:T(8,128)(2,1)} %update.2.refs_0_.refs_4_, bf16[64,1024]{1,0:T(8,128)(2,1)} %copy-done.26, bf16[64,1024]{1,0:T(8,128)(2,1)} %copy-done.27, ...), custom_call_target="tpu_custom_call" | custom-call | flops 4294967296 | bytes 9437184 | tf_op jit(solution)/shard_map/cluster_sums/pallas_call | solution.py:221
  172.5 5.9 %collective-permute-start.22 = (bf16[64,1152]{1,0:T(8,128)(2,1)}, bf16[64,1152]{1,0:T(8,128)(2,1)S(1)}, u32[]{:S(2)}, u32[]{:S(2)}) collective-permute-start(bf16[64,1152]{1,0:T(8,128)(2,1)} %get-tuple-element.50), channel_id=1, source_target_pairs={{0,74},{1,75},{2,72},{3,73},{4,78},{5,79},{6,76},{7,77},{8,66},{9,... | collective-permute-start | bytes 442376 | tf_op jit(solution)/shard_map/ppermute | solution.py:344
  178.4 3.5 %collective-permute-start.23 = (bf16[64,1152]{1,0:T(8,128)(2,1)}, bf16[64,1152]{1,0:T(8,128)(2,1)S(1)}, u32[]{:S(2)}, u32[]{:S(2)}) collective-permute-start(bf16[64,1152]{1,0:T(8,128)(2,1)} %get-tuple-element.51), channel_id=1, source_target_pairs={{0,111},{1,108},{2,109},{3,110},{4,99},{5,96},{6,97},{7,98},{8,103... | collective-permute-start | bytes 442376 | tf_op jit(solution)/shard_map/ppermute | solution.py:344
  181.9 0.6 collective-permute-done.21.refs_1_
  182.5 3.3 %collective-permute-done.22.refs_2_ = bf16[64,1152]{1,0:T(8,128)(2,1)S(1)} collective-permute-done((bf16[64,1152]{1,0:T(8,128)(2,1)}, bf16[64,1152]{1,0:T(8,128)(2,1)S(1)}, u32[]{:S(2)}, u32[]{:S(2)}) %collective-permute-start.22) | collective-permute-done | bytes 147488 | tf_op jit(solution)/shard_map/ppermute | solution.py:344
  185.8 1.2 collective-permute-done.23.refs_3_
  187.1 0.7 copy-done.3
  187.7 2.0 update.3
  189.7 0.8 dynamic-slice_bitcast_fusion.4
  190.5 3.0 %collective-permute-start.24 = (bf16[16,1152]{1,0:T(8,128)(2,1)S(1)}, bf16[16,1152]{1,0:T(8,128)(2,1)S(1)}, u32[]{:S(2)}, u32[]{:S(2)}) collective-permute-start(bf16[16,1152]{1,0:T(8,128)(2,1)S(1)} %get-tuple-element.59), channel_id=1, source_target_pairs={{0,0},{1,97},{2,66},{3,35},{4,4},{5,101},{6,70},{7,39},{8,8},{9,10... | collective-permute-start | bytes 110600 | tf_op jit(solution)/shard_map/ppermute | solution.py:344
  193.5 4.5 %collective-permute-start.25 = (bf16[16,1152]{1,0:T(8,128)(2,1)S(1)}, bf16[16,1152]{1,0:T(8,128)(2,1)S(1)}, u32[]{:S(2)}, u32[]{:S(2)}) collective-permute-start(bf16[16,1152]{1,0:T(8,128)(2,1)S(1)} %get-tuple-element.58), channel_id=1, source_target_pairs={{0,4},{1,101},{2,70},{3,39},{4,8},{5,105},{6,74},{7,43},{8,12},{9,... | collective-permute-start | bytes 110600 | tf_op jit(solution)/shard_map/ppermute | solution.py:344
  198.0 4.8 %collective-permute-start.26 = (bf16[16,1152]{1,0:T(8,128)(2,1)S(1)}, bf16[16,1152]{1,0:T(8,128)(2,1)S(1)}, u32[]{:S(2)}, u32[]{:S(2)}) collective-permute-start(bf16[16,1152]{1,0:T(8,128)(2,1)S(1)} %get-tuple-element.57), channel_id=1, source_target_pairs={{0,8},{1,105},{2,74},{3,43},{4,12},{5,109},{6,78},{7,47},{8,0},{9,... | collective-permute-start | bytes 110600 | tf_op jit(solution)/shard_map/ppermute | solution.py:344
  202.9 0.9 collective-permute-start.27
  203.7 2.1 %collective-permute-done.26.refs_2_ = bf16[16,1152]{1,0:T(8,128)(2,1)S(1)} collective-permute-done((bf16[16,1152]{1,0:T(8,128)(2,1)S(1)}, bf16[16,1152]{1,0:T(8,128)(2,1)S(1)}, u32[]{:S(2)}, u32[]{:S(2)}) %collective-permute-start.26) | collective-permute-done | bytes 36896 | tf_op jit(solution)/shard_map/ppermute | solution.py:344
  205.9 3.3 %collective-permute-done.27.refs_3_ = bf16[16,1152]{1,0:T(8,128)(2,1)S(1)} collective-permute-done((bf16[16,1152]{1,0:T(8,128)(2,1)S(1)}, bf16[16,1152]{1,0:T(8,128)(2,1)S(1)}, u32[]{:S(2)}, u32[]{:S(2)}) %collective-permute-start.27) | collective-permute-done | bytes 36896 | tf_op jit(solution)/shard_map/ppermute | solution.py:344
  209.2 0.6 copy-done.13
  209.8 1.5 finish.1
  (74 shorter events, 1.9 us)
Async XLA Ops:
  0.6 10.0 %copy-start.14 = (s32[32]{0:T(128)S(1)}, s32[32]{0:T(128)}, u32[]{:S(2)}) copy-start(s32[32]{0:T(128)} %param.6) | copy-start | bytes 388
  2.4 19.2 %all-to-all-start = ((bf16[16,16,1024]{2,1,0:T(8,128)(2,1)}), bf16[16,16,1024]{2,1,0:T(8,128)(2,1)S(1)}, u32[]{:S(2)}, u32[]{:S(2)}) async-start(bf16[16,16,1024]{2,1,0:T(8,128)(2,1)} %spread.1), calls=%async_computation | async-start | bytes 1048576 | tf_op jit(solution)/shard_map/all_to_all | solution.py:329
  21.5 28.9 %all-to-all-start.2 = ((bf16[8,128,1024]{2,1,0:T(8,128)(2,1)}), bf16[8,128,1024]{2,1,0:T(8,128)(2,1)S(1)}, u32[]{:S(2)}, u32[]{:S(2)}) async-start(bf16[8,128,1024]{2,1,0:T(8,128)(2,1)} %get-tuple-element.41), calls=%async_computation.2 | async-start | bytes 4194304 | tf_op jit(solution)/shard_map/all_to_all | solution.py:329
  26.4 15.0 %collective-permute-start.1 = (bf16[2,128,1024]{2,1,0:T(8,128)(2,1)}, bf16[2,128,1024]{2,1,0:T(8,128)(2,1)S(1)}, u32[]{:S(2)}, u32[]{:S(2)}) collective-permute-start(bf16[2,128,1024]{2,1,0:T(8,128)(2,1)} %get-tuple-element.27), channel_id=1, source_target_pairs={{0,32},{1,33},{2,34},{3,35},{4,36},{5,37},{6,38},{7,39},{8,40},{9,... | collective-permute-start | bytes 1572872 | tf_op jit(solution)/shard_map/ppermute | solution.py:344
  27.8 15.0 %collective-permute-start.2 = (bf16[2,128,1024]{2,1,0:T(8,128)(2,1)}, bf16[2,128,1024]{2,1,0:T(8,128)(2,1)S(1)}, u32[]{:S(2)}, u32[]{:S(2)}) collective-permute-start(bf16[2,128,1024]{2,1,0:T(8,128)(2,1)} %get-tuple-element.28), channel_id=1, source_target_pairs={{0,96},{1,97},{2,98},{3,99},{4,100},{5,101},{6,102},{7,103},{8,104... | collective-permute-start | bytes 1572872 | tf_op jit(solution)/shard_map/ppermute | solution.py:344
  28.4 27.8 %collective-permute-start.3 = (bf16[2,128,1024]{2,1,0:T(8,128)(2,1)}, bf16[2,128,1024]{2,1,0:T(8,128)(2,1)S(1)}, u32[]{:S(2)}, u32[]{:S(2)}) collective-permute-start(bf16[2,128,1024]{2,1,0:T(8,128)(2,1)} %get-tuple-element.29), channel_id=1, source_target_pairs={{0,44},{1,45},{2,46},{3,47},{4,32},{5,33},{6,34},{7,35},{8,36},{9,... | collective-permute-start | bytes 1572872 | tf_op jit(solution)/shard_map/ppermute | solution.py:344
  32.0 24.9 %collective-permute-start.4 = (bf16[2,128,1024]{2,1,0:T(8,128)(2,1)}, bf16[2,128,1024]{2,1,0:T(8,128)(2,1)}, u32[]{:S(2)}, u32[]{:S(2)}) collective-permute-start(bf16[2,128,1024]{2,1,0:T(8,128)(2,1)} %get-tuple-element.30), channel_id=1, source_target_pairs={{0,100},{1,101},{2,102},{3,103},{4,104},{5,105},{6,106},{7,107},{8... | collective-permute-start | bytes 1572872 | tf_op jit(solution)/shard_map/ppermute | solution.py:344
  32.0 33.0 %collective-permute-start.5 = (bf16[2,128,1024]{2,1,0:T(8,128)(2,1)}, bf16[2,128,1024]{2,1,0:T(8,128)(2,1)}, u32[]{:S(2)}, u32[]{:S(2)}) collective-permute-start(bf16[2,128,1024]{2,1,0:T(8,128)(2,1)} %get-tuple-element.31), channel_id=1, source_target_pairs={{0,64},{1,65},{2,66},{3,67},{4,68},{5,69},{6,70},{7,71},{8,72},{9,... | collective-permute-start | bytes 1572872 | tf_op jit(solution)/shard_map/ppermute | solution.py:344
  41.3 1.5 copy-start.7
  42.9 0.8 copy-start.8
  50.4 1.3 copy-start
  51.7 59.8 %all-to-all-start.1 = ((bf16[8,128,1024]{2,1,0:T(8,128)(2,1)}), bf16[8,128,1024]{2,1,0:T(8,128)(2,1)}, u32[]{:S(2)}, u32[]{:S(2)}) async-start(bf16[8,128,1024]{2,1,0:T(8,128)(2,1)} %get-tuple-element.32), calls=%async_computation.1 | async-start | bytes 4194304 | tf_op jit(solution)/shard_map/all_to_all | solution.py:329
  56.1 10.6 %copy-start.25 = (bf16[1,128,1024]{2,1,0:T(8,128)(2,1)S(1)}, bf16[1,128,1024]{2,1,0:T(8,128)(2,1)}, u32[]{:S(2)}) copy-start(bf16[1,128,1024]{2,1,0:T(8,128)(2,1)} %get-tuple-element.33) | copy-start | bytes 786436
  56.1 18.3 %copy-start.24 = (bf16[1,128,1024]{2,1,0:T(8,128)(2,1)S(1)}, bf16[1,128,1024]{2,1,0:T(8,128)(2,1)}, u32[]{:S(2)}) copy-start(bf16[1,128,1024]{2,1,0:T(8,128)(2,1)} %get-tuple-element.34) | copy-start | bytes 786436
  56.1 18.7 %copy-start.23 = (bf16[1,128,1024]{2,1,0:T(8,128)(2,1)S(1)}, bf16[1,128,1024]{2,1,0:T(8,128)(2,1)}, u32[]{:S(2)}) copy-start(bf16[1,128,1024]{2,1,0:T(8,128)(2,1)} %get-tuple-element.35) | copy-start | bytes 786436
  56.1 21.1 %copy-start.22 = (bf16[1,128,1024]{2,1,0:T(8,128)(2,1)S(1)}, bf16[1,128,1024]{2,1,0:T(8,128)(2,1)}, u32[]{:S(2)}) copy-start(bf16[1,128,1024]{2,1,0:T(8,128)(2,1)} %get-tuple-element.36) | copy-start | bytes 786436
  56.1 43.6 %copy-start.18 = (bf16[1,128,1024]{2,1,0:T(8,128)(2,1)S(1)}, bf16[1,128,1024]{2,1,0:T(8,128)(2,1)}, u32[]{:S(2)}) copy-start(bf16[1,128,1024]{2,1,0:T(8,128)(2,1)} %get-tuple-element.40) | copy-start | bytes 786436
  56.2 10.5 %copy-start.9 = (bf16[2,128,1024]{2,1,0:T(8,128)(2,1)}, bf16[2,128,1024]{2,1,0:T(8,128)(2,1)S(1)}, u32[]{:S(2)}) copy-start(bf16[2,128,1024]{2,1,0:T(8,128)(2,1)S(1)} %collective-permute-done.3.refs_6_.refs_7_) | copy-start | bytes 1572868
  66.7 44.9 %collective-permute-start.6 = (bf16[5,128,1024]{2,1,0:T(8,128)(2,1)}, bf16[5,128,1024]{2,1,0:T(8,128)(2,1)S(1)}, u32[]{:S(2)}, u32[]{:S(2)}) collective-permute-start(bf16[5,128,1024]{2,1,0:T(8,128)(2,1)} %slice_dynamic-update-slice_fusion), channel_id=1, source_target_pairs={{0,16},{1,17},{2,18},{3,19},{4,20},{5,21},{6,22},{7,23},{8,24},{9,... | collective-permute-start | bytes 3932168 | tf_op jit(solution)/shard_map/ppermute | solution.py:344
  66.7 10.5 %collective-permute-start.7 = (bf16[1,128,1024]{2,1,0:T(8,128)(2,1)S(1)}, bf16[1,128,1024]{2,1,0:T(8,128)(2,1)S(1)}, u32[]{:S(2)}, u32[]{:S(2)}) collective-permute-start(bf16[1,128,1024]{2,1,0:T(8,128)(2,1)S(1)} %copy-done.25), channel_id=1, source_target_pairs={{0,35},{1,32},{2,33},{3,34},{4,39},{5,36},{6,37},{7,38},{8,43},{9,... | collective-permute-start | bytes 786440 | tf_op jit(solution)/shard_map/ppermute | solution.py:344
  66.7 33.0 %collective-permute-start = (bf16[16,16,1024]{2,1,0:T(8,128)(2,1)S(1)}, bf16[16,16,1024]{2,1,0:T(8,128)(2,1)S(1)}, u32[]{:S(2)}, u32[]{:S(2)}) collective-permute-start(bf16[16,16,1024]{2,1,0:T(8,128)(2,1)S(1)} %all-to-all-done), channel_id=1, source_target_pairs={{0,0},{1,33},{2,66},{3,99},{4,4},{5,37},{6,70},{7,103},{8,8},{9,41... | collective-permute-start | bytes 1572872 | tf_op jit(solution)/shard_map/ppermute | solution.py:344
  74.4 18.0 %collective-permute-start.8 = (bf16[1,128,1024]{2,1,0:T(8,128)(2,1)S(1)}, bf16[1,128,1024]{2,1,0:T(8,128)(2,1)S(1)}, u32[]{:S(2)}, u32[]{:S(2)}) collective-permute-start(bf16[1,128,1024]{2,1,0:T(8,128)(2,1)S(1)} %copy-done.24), channel_id=1, source_target_pairs={{0,51},{1,48},{2,49},{3,50},{4,55},{5,52},{6,53},{7,54},{8,59},{9,... | collective-permute-start | bytes 786440 | tf_op jit(solution)/shard_map/ppermute | solution.py:344
  74.8 19.1 %collective-permute-start.9 = (bf16[1,128,1024]{2,1,0:T(8,128)(2,1)S(1)}, bf16[1,128,1024]{2,1,0:T(8,128)(2,1)S(1)}, u32[]{:S(2)}, u32[]{:S(2)}) collective-permute-start(bf16[1,128,1024]{2,1,0:T(8,128)(2,1)S(1)} %copy-done.23), channel_id=1, source_target_pairs={{0,97},{1,98},{2,99},{3,96},{4,101},{5,102},{6,103},{7,100},{8,105... | collective-permute-start | bytes 786440 | tf_op jit(solution)/shard_map/ppermute | solution.py:344
  77.2 30.9 %copy-start.16 = (bf16[1,128,1024]{2,1,0:T(8,128)(2,1)}, bf16[1,128,1024]{2,1,0:T(8,128)(2,1)S(1)}, u32[]{:S(2)}) copy-start(bf16[1,128,1024]{2,1,0:T(8,128)(2,1)S(1)} %collective-permute-done.7.refs_11_.refs_12_) | copy-start | bytes 786436
  77.2 20.3 %collective-permute-start.10 = (bf16[1,128,1024]{2,1,0:T(8,128)(2,1)S(1)}, bf16[1,128,1024]{2,1,0:T(8,128)(2,1)S(1)}, u32[]{:S(2)}, u32[]{:S(2)}) collective-permute-start(bf16[1,128,1024]{2,1,0:T(8,128)(2,1)S(1)} %copy-done.22), channel_id=1, source_target_pairs={{0,113},{1,114},{2,115},{3,112},{4,117},{5,118},{6,119},{7,116},{8... | collective-permute-start | bytes 786440 | tf_op jit(solution)/shard_map/ppermute | solution.py:344
  92.4 15.7 %copy-start.17 = (bf16[1,128,1024]{2,1,0:T(8,128)(2,1)}, bf16[1,128,1024]{2,1,0:T(8,128)(2,1)S(1)}, u32[]{:S(2)}) copy-start(bf16[1,128,1024]{2,1,0:T(8,128)(2,1)S(1)} %collective-permute-done.8.refs_12_.refs_13_) | copy-start | bytes 786436
  92.4 15.7 %collective-permute-start.11 = (bf16[1,128,1024]{2,1,0:T(8,128)(2,1)}, bf16[1,128,1024]{2,1,0:T(8,128)(2,1)}, u32[]{:S(2)}, u32[]{:S(2)}) collective-permute-start(bf16[1,128,1024]{2,1,0:T(8,128)(2,1)} %get-tuple-element.37), channel_id=1, source_target_pairs={{0,7},{1,4},{2,5},{3,6},{4,11},{5,8},{6,9},{7,10},{8,15},{9,12},{1... | collective-permute-start | bytes 786440 | tf_op jit(solution)/shard_map/ppermute | solution.py:344
  94.0 14.2 %copy-start.19 = (bf16[1,128,1024]{2,1,0:T(8,128)(2,1)}, bf16[1,128,1024]{2,1,0:T(8,128)(2,1)S(1)}, u32[]{:S(2)}) copy-start(bf16[1,128,1024]{2,1,0:T(8,128)(2,1)S(1)} %collective-permute-done.9.refs_13_.refs_14_) | copy-start | bytes 786436
  94.0 14.2 %collective-permute-start.12 = (bf16[1,128,1024]{2,1,0:T(8,128)(2,1)}, bf16[1,128,1024]{2,1,0:T(8,128)(2,1)}, u32[]{:S(2)}, u32[]{:S(2)}) collective-permute-start(bf16[1,128,1024]{2,1,0:T(8,128)(2,1)} %get-tuple-element.38), channel_id=1, source_target_pairs={{0,23},{1,20},{2,21},{3,22},{4,27},{5,24},{6,25},{7,26},{8,31},{9,... | collective-permute-start | bytes 786440 | tf_op jit(solution)/shard_map/ppermute | solution.py:344
  97.5 2.3 %copy-start.20 = (bf16[1,128,1024]{2,1,0:T(8,128)(2,1)}, bf16[1,128,1024]{2,1,0:T(8,128)(2,1)S(1)}, u32[]{:S(2)}) copy-start(bf16[1,128,1024]{2,1,0:T(8,128)(2,1)S(1)} %collective-permute-done.10.refs_14_.refs_15_) | copy-start | bytes 786436
  97.5 10.7 %collective-permute-start.13 = (bf16[1,128,1024]{2,1,0:T(8,128)(2,1)}, bf16[1,128,1024]{2,1,0:T(8,128)(2,1)}, u32[]{:S(2)}, u32[]{:S(2)}) collective-permute-start(bf16[1,128,1024]{2,1,0:T(8,128)(2,1)} %get-tuple-element.39), channel_id=1, source_target_pairs={{0,13},{1,14},{2,15},{3,12},{4,1},{5,2},{6,3},{7,0},{8,5},{9,6},{1... | collective-permute-start | bytes 786440 | tf_op jit(solution)/shard_map/ppermute | solution.py:344
  99.7 11.8 %collective-permute-start.14 = (bf16[1,128,1024]{2,1,0:T(8,128)(2,1)S(1)}, bf16[1,128,1024]{2,1,0:T(8,128)(2,1)S(1)}, u32[]{:S(2)}, u32[]{:S(2)}) collective-permute-start(bf16[1,128,1024]{2,1,0:T(8,128)(2,1)S(1)} %copy-done.18), channel_id=1, source_target_pairs={{0,29},{1,30},{2,31},{3,28},{4,17},{5,18},{6,19},{7,16},{8,21},{9,... | collective-permute-start | bytes 786440 | tf_op jit(solution)/shard_map/ppermute | solution.py:344
  111.6 0.7 copy-start.21
  111.6 1.2 copy-start.15
  121.5 12.9 %collective-permute-start.15 = (bf16[64,1152]{1,0:T(8,128)(2,1)}, bf16[64,1152]{1,0:T(8,128)(2,1)S(1)}, u32[]{:S(2)}, u32[]{:S(2)}) collective-permute-start(bf16[64,1152]{1,0:T(8,128)(2,1)} %get-tuple-element.45), channel_id=1, source_target_pairs={{0,37},{1,38},{2,39},{3,36},{4,41},{5,42},{6,43},{7,40},{8,45},{9,... | collective-permute-start | bytes 442376 | tf_op jit(solution)/shard_map/ppermute | solution.py:344
  126.4 13.3 %collective-permute-start.16 = (bf16[64,1152]{1,0:T(8,128)(2,1)}, bf16[64,1152]{1,0:T(8,128)(2,1)S(1)}, u32[]{:S(2)}, u32[]{:S(2)}) collective-permute-start(bf16[64,1152]{1,0:T(8,128)(2,1)} %get-tuple-element.46), channel_id=1, source_target_pairs={{0,74},{1,75},{2,72},{3,73},{4,78},{5,79},{6,76},{7,77},{8,66},{9,... | collective-permute-start | bytes 442376 | tf_op jit(solution)/shard_map/ppermute | solution.py:344
  130.2 10.1 %collective-permute-start.17 = (bf16[64,1152]{1,0:T(8,128)(2,1)}, bf16[64,1152]{1,0:T(8,128)(2,1)S(1)}, u32[]{:S(2)}, u32[]{:S(2)}) collective-permute-start(bf16[64,1152]{1,0:T(8,128)(2,1)} %get-tuple-element.47), channel_id=1, source_target_pairs={{0,111},{1,108},{2,109},{3,110},{4,99},{5,96},{6,97},{7,98},{8,103... | collective-permute-start | bytes 442376 | tf_op jit(solution)/shard_map/ppermute | solution.py:344
  134.4 5.8 %copy-start.4 = (bf16[64,1152]{1,0:T(8,128)(2,1)}, bf16[64,1152]{1,0:T(8,128)(2,1)S(1)}, u32[]{:S(2)}) copy-start(bf16[64,1152]{1,0:T(8,128)(2,1)S(1)} %collective-permute-done.15.refs_1_) | copy-start | bytes 442372
  139.6 0.7 copy-start.5
  140.3 0.7 copy-start.6
  142.9 9.6 %collective-permute-start.18 = (bf16[64,1024]{1,0:T(8,128)(2,1)}, bf16[64,1024]{1,0:T(8,128)(2,1)S(1)}, u32[]{:S(2)}, u32[]{:S(2)}) collective-permute-start(bf16[64,1024]{1,0:T(8,128)(2,1)} %update.2.refs_0_.refs_4_), channel_id=1, source_target_pairs={{0,111},{1,108},{2,109},{3,110},{4,99},{5,96},{6,97},{7,98},{8,103... | collective-permute-start | bytes 393224 | tf_op jit(solution)/shard_map/ppermute | solution.py:344
  148.2 12.9 %collective-permute-start.19 = (bf16[64,1024]{1,0:T(8,128)(2,1)}, bf16[64,1024]{1,0:T(8,128)(2,1)S(1)}, u32[]{:S(2)}, u32[]{:S(2)}) collective-permute-start(bf16[64,1024]{1,0:T(8,128)(2,1)} %update.2.refs_0_.refs_4_), channel_id=1, source_target_pairs={{0,74},{1,75},{2,72},{3,73},{4,78},{5,79},{6,76},{7,77},{8,66},{9,... | collective-permute-start | bytes 393224 | tf_op jit(solution)/shard_map/ppermute | solution.py:344
  151.9 9.7 %collective-permute-start.20 = (bf16[64,1024]{1,0:T(8,128)(2,1)}, bf16[64,1024]{1,0:T(8,128)(2,1)S(1)}, u32[]{:S(2)}, u32[]{:S(2)}) collective-permute-start(bf16[64,1024]{1,0:T(8,128)(2,1)} %update.2.refs_0_.refs_4_), channel_id=1, source_target_pairs={{0,37},{1,38},{2,39},{3,36},{4,41},{5,42},{6,43},{7,40},{8,45},{9,... | collective-permute-start | bytes 393224 | tf_op jit(solution)/shard_map/ppermute | solution.py:344
  152.5 9.1 %copy-start.26 = (bf16[64,1024]{1,0:T(8,128)(2,1)}, bf16[64,1024]{1,0:T(8,128)(2,1)S(1)}, u32[]{:S(2)}) copy-start(bf16[64,1024]{1,0:T(8,128)(2,1)S(1)} %collective-permute-done.18.refs_1_) | copy-start | bytes 393220
  161.1 0.7 copy-start.27
  161.8 0.7 copy-start.28
  172.4 10.1 %collective-permute-start.21 = (bf16[64,1152]{1,0:T(8,128)(2,1)}, bf16[64,1152]{1,0:T(8,128)(2,1)S(1)}, u32[]{:S(2)}, u32[]{:S(2)}) collective-permute-start(bf16[64,1152]{1,0:T(8,128)(2,1)} %get-tuple-element.49), channel_id=1, source_target_pairs={{0,37},{1,38},{2,39},{3,36},{4,41},{5,42},{6,43},{7,40},{8,45},{9,... | collective-permute-start | bytes 442376 | tf_op jit(solution)/shard_map/ppermute | solution.py:344
  172.5 13.3 %collective-permute-start.22 = (bf16[64,1152]{1,0:T(8,128)(2,1)}, bf16[64,1152]{1,0:T(8,128)(2,1)S(1)}, u32[]{:S(2)}, u32[]{:S(2)}) collective-permute-start(bf16[64,1152]{1,0:T(8,128)(2,1)} %get-tuple-element.50), channel_id=1, source_target_pairs={{0,74},{1,75},{2,72},{3,73},{4,78},{5,79},{6,76},{7,77},{8,66},{9,... | collective-permute-start | bytes 442376 | tf_op jit(solution)/shard_map/ppermute | solution.py:344
  178.4 8.7 %collective-permute-start.23 = (bf16[64,1152]{1,0:T(8,128)(2,1)}, bf16[64,1152]{1,0:T(8,128)(2,1)S(1)}, u32[]{:S(2)}, u32[]{:S(2)}) collective-permute-start(bf16[64,1152]{1,0:T(8,128)(2,1)} %get-tuple-element.51), channel_id=1, source_target_pairs={{0,111},{1,108},{2,109},{3,110},{4,99},{5,96},{6,97},{7,98},{8,103... | collective-permute-start | bytes 442376 | tf_op jit(solution)/shard_map/ppermute | solution.py:344
  182.5 4.6 %copy-start.1 = (bf16[64,1152]{1,0:T(8,128)(2,1)}, bf16[64,1152]{1,0:T(8,128)(2,1)S(1)}, u32[]{:S(2)}) copy-start(bf16[64,1152]{1,0:T(8,128)(2,1)S(1)} %collective-permute-done.21.refs_1_) | copy-start | bytes 442372
  185.8 1.2 copy-start.2
  187.1 0.7 copy-start.3
  190.5 13.2 %collective-permute-start.24 = (bf16[16,1152]{1,0:T(8,128)(2,1)S(1)}, bf16[16,1152]{1,0:T(8,128)(2,1)S(1)}, u32[]{:S(2)}, u32[]{:S(2)}) collective-permute-start(bf16[16,1152]{1,0:T(8,128)(2,1)S(1)} %get-tuple-element.59), channel_id=1, source_target_pairs={{0,0},{1,97},{2,66},{3,35},{4,4},{5,101},{6,70},{7,39},{8,8},{9,10... | collective-permute-start | bytes 110600 | tf_op jit(solution)/shard_map/ppermute | solution.py:344
  193.5 10.2 %collective-permute-start.25 = (bf16[16,1152]{1,0:T(8,128)(2,1)S(1)}, bf16[16,1152]{1,0:T(8,128)(2,1)S(1)}, u32[]{:S(2)}, u32[]{:S(2)}) collective-permute-start(bf16[16,1152]{1,0:T(8,128)(2,1)S(1)} %get-tuple-element.58), channel_id=1, source_target_pairs={{0,4},{1,101},{2,70},{3,39},{4,8},{5,105},{6,74},{7,43},{8,12},{9,... | collective-permute-start | bytes 110600 | tf_op jit(solution)/shard_map/ppermute | solution.py:344
  198.0 7.9 %collective-permute-start.26 = (bf16[16,1152]{1,0:T(8,128)(2,1)S(1)}, bf16[16,1152]{1,0:T(8,128)(2,1)S(1)}, u32[]{:S(2)}, u32[]{:S(2)}) collective-permute-start(bf16[16,1152]{1,0:T(8,128)(2,1)S(1)} %get-tuple-element.57), channel_id=1, source_target_pairs={{0,8},{1,105},{2,74},{3,43},{4,12},{5,109},{6,78},{7,47},{8,0},{9,... | collective-permute-start | bytes 110600 | tf_op jit(solution)/shard_map/ppermute | solution.py:344
  202.9 6.4 %collective-permute-start.27 = (bf16[16,1152]{1,0:T(8,128)(2,1)S(1)}, bf16[16,1152]{1,0:T(8,128)(2,1)S(1)}, u32[]{:S(2)}, u32[]{:S(2)}) collective-permute-start(bf16[16,1152]{1,0:T(8,128)(2,1)S(1)} %get-tuple-element.56), channel_id=1, source_target_pairs={{0,12},{1,109},{2,78},{3,47},{4,0},{5,97},{6,66},{7,35},{8,4},{9,1... | collective-permute-start | bytes 110600 | tf_op jit(solution)/shard_map/ppermute | solution.py:344
  203.7 5.5 %copy-start.10 = (bf16[16,1152]{1,0:T(8,128)(2,1)}, bf16[16,1152]{1,0:T(8,128)(2,1)S(1)}, u32[]{:S(2)}) copy-start(bf16[16,1152]{1,0:T(8,128)(2,1)S(1)} %collective-permute-done.24.refs_0_) | copy-start | bytes 110596
  203.7 5.5 %copy-start.11 = (bf16[16,1152]{1,0:T(8,128)(2,1)}, bf16[16,1152]{1,0:T(8,128)(2,1)S(1)}, u32[]{:S(2)}) copy-start(bf16[16,1152]{1,0:T(8,128)(2,1)S(1)} %collective-permute-done.25.refs_1_) | copy-start | bytes 110596
  205.9 3.4 %copy-start.12 = (bf16[16,1152]{1,0:T(8,128)(2,1)}, bf16[16,1152]{1,0:T(8,128)(2,1)S(1)}, u32[]{:S(2)}) copy-start(bf16[16,1152]{1,0:T(8,128)(2,1)S(1)} %collective-permute-done.26.refs_2_) | copy-start | bytes 110596
  209.2 0.6 copy-start.13

commit v4 on v3

--- a/solution.py
+++ b/solution.py
@@ -18,11 +18,8 @@
 MIB = 1024 * 1024
 VMEM = 60 * MIB
 RING = 4
-LINE_Z = 6
 TILE = 8
 AXES = ("x", "core", "z", "y")
-SWAPPED = ((1, 0, 0), (3, 0, 0), (1, 3, 0), (3, 1, 0), (2, 0, 0))
-DIRECT = ((1, 0, 3), (3, 0, 1), (0, 1, 3), (0, 3, 1))
 
 
 def scatter_kernel(capacity, where, ids_ref, base_ref, points_ref, *refs):
@@ -142,21 +139,14 @@
     )(cluster_ids.reshape(1, rows), base.reshape(-1, 1), points)
 
 
-def sums_kernel(groups, counts, carried, finish, z_ref, *refs):
+def sums_kernel(groups, counts, carried, last, y_ref, *refs):
     blocks, refs = refs[:groups], refs[groups:]
     sources, refs = refs[: len(counts)], refs[len(counts) :]
     carry, refs = refs[: 2 * carried], refs[2 * carried :]
     outs, (aug, total, mass, bias, rows, sems) = refs[:-6], refs[-6:]
     held, width = blocks[0].shape
     cents = groups * held
-    pieces = []
-    for ref, count in zip(sources, counts):
-        if count == LINE_Z:
-            pieces += [
-                (ref, c * RING + lax.rem(z_ref[0] + d, RING)) for c in range(2) for d in range(1, RING)
-            ]
-        else:
-            pieces += [(ref, i) for i in range(count)]
+    pieces = [(ref, i) for ref, count in zip(sources, counts) for i in range(count)]
     for n, (ref, i) in enumerate(pieces):
         pltpu.make_async_copy(ref.at[i], rows.at[n], sems.at[n]).start()
 
@@ -174,6 +164,8 @@
     else:
         total[...] = jnp.zeros_like(total)
         mass[...] = jnp.zeros_like(mass)
+    if last:
+        total[:held] += PRIOR_WEIGHT * blocks[0][...].astype(jnp.float32)
 
     def tile(t, _):
         for i in range(TILE):
@@ -192,34 +184,48 @@
         return 0
 
     lax.fori_loop(0, len(pieces) // TILE, tile, 0)
-    if not finish:
+    if not last and len(outs) == 2:
         outs[0][...] = total[...]
         outs[1][...] = mass[...]
         return
-    lane = lax.broadcasted_iota(jnp.int32, (held, EXTRA), 1)
+    if not last:
+        lane = lax.broadcasted_iota(jnp.int32, (held, EXTRA), 1)
+        for g in range(groups):
+            span = pl.ds(g * held, held)
+            outs[g][:, :width] = total[span].astype(jnp.bfloat16)
+            outs[g][:, width:] = terms(mass[span], lane)
+        return
+    shard = held // RING
+    lane = lax.broadcasted_iota(jnp.int32, (shard, EXTRA), 1)
     for g in range(groups):
-        span = pl.ds(g * held, held)
-        outs[g][:, :width] = total[span].astype(jnp.bfloat16)
-        outs[g][:, width:] = terms(mass[span], lane)
-
-
-def cluster_sums(z, blocks, sources, counts, carry=(), finish=True):
+        to_y = lax.rem(y_ref[0] + g, RING)
+        for z in range(RING):
+            span = pl.ds(g * held + z * shard, shard)
+            holder = z * RING + to_y
+            outs[0][holder, :, :width] = total[span].astype(jnp.bfloat16)
+            outs[0][holder, :, width:] = terms(mass[span], lane)
+
+
+def cluster_sums(y, blocks, sources, counts, carry=(), partial=False, last=False):
     groups = len(blocks)
     held, width = blocks[0].shape
     capacity = sources[0].shape[1]
     cents, pieces = groups * held, sum(counts)
     assert pieces % TILE == 0
     whole = pl.BlockSpec(memory_space=pltpu.VMEM)
-    if finish:
-        shapes = [jax.ShapeDtypeStruct((held, width + EXTRA), jnp.bfloat16)] * groups
-    else:
+    if partial:
         shapes = [
             jax.ShapeDtypeStruct((cents, width), jnp.float32),
             jax.ShapeDtypeStruct((cents, 1), jnp.float32),
         ]
+    elif last:
+        shape = (groups * RING, held // RING, width + EXTRA)
+        shapes = [jax.ShapeDtypeStruct(shape, jnp.bfloat16)]
+    else:
+        shapes = [jax.ShapeDtypeStruct((held, width + EXTRA), jnp.bfloat16)] * groups
     count = pieces * capacity
     return pl.pallas_call(
-        functools.partial(sums_kernel, groups, counts, 1 if carry else 0, finish),
+        functools.partial(sums_kernel, groups, counts, 1 if carry else 0, last),
         in_specs=[pl.BlockSpec(memory_space=pltpu.SMEM)]
         + [whole] * groups
         + [pl.BlockSpec(memory_space=pl.ANY)] * len(sources)
@@ -241,7 +247,7 @@
             transcendentals=count * cents,
         ),
         name="cluster_sums",
-    )(z.reshape(1), *blocks, *sources, *carry)
+    )(y.reshape(1), *blocks, *sources, *carry)
 
 
 def terms(m, lane):
@@ -252,25 +258,23 @@
     return parts.astype(jnp.bfloat16)
 
 
-def update_kernel(packed, count, *refs):
-    parts, mu_ref, out_ref = refs[:count], refs[count], refs[count + 1]
-    rows, width = mu_ref.shape
+def update_kernel(*refs):
+    parts, mu_ref, out_ref = refs[:-2], refs[-2], refs[-1]
+    width = mu_ref.shape[1]
     total = parts[0][...].astype(jnp.float32)
-    for s in range(1, count):
-        total = total + parts[s][...].astype(jnp.float32)
+    for part in parts[1:]:
+        total = total + part[...].astype(jnp.float32)
     mass = jnp.sum(total[:, width:], axis=1, keepdims=True)
     mu = mu_ref[...].astype(jnp.float32)
     new = (total[:, :width] + PRIOR_WEIGHT * mu) / (mass + PRIOR_WEIGHT)
-    out_ref[:, :width] = new.astype(jnp.bfloat16)
-    if packed:
-        out_ref[:, width:] = terms(mass, lax.broadcasted_iota(jnp.int32, (rows, EXTRA), 1))
-
-
-def update(parts, mu, packed):
+    out_ref[...] = new.astype(jnp.bfloat16)
+
+
+def update(parts, mu):
     rows, width = mu.shape
     return pl.pallas_call(
-        functools.partial(update_kernel, packed, len(parts)),
-        out_shape=jax.ShapeDtypeStruct((rows, width + (EXTRA if packed else 0)), jnp.bfloat16),
+        update_kernel,
+        out_shape=jax.ShapeDtypeStruct((rows, width), jnp.bfloat16),
         compiler_params=pltpu.CompilerParams(vmem_limit_bytes=VMEM),
         cost_estimate=pl.CostEstimate(
             flops=len(parts) * rows * width,
@@ -281,139 +285,84 @@
     )(*parts, mu)
 
 
-def spread_kernel(in_ref, out_ref):
-    for i in range(RING):
-        for k in range(RING):
-            out_ref[i * RING + k] = in_ref[(i - k) % RING]
-
-
-def spread(centroids):
-    return pl.pallas_call(
-        spread_kernel,
-        out_shape=jax.ShapeDtypeStruct((RING * RING,) + centroids.shape[1:], centroids.dtype),
-        compiler_params=pltpu.CompilerParams(vmem_limit_bytes=VMEM),
-        name="spread",
-    )(centroids)
-
-
-def finish_kernel(first_ref, *refs):
-    parts, (new_ref, mass_ref) = refs[:RING], refs[RING:]
+def assemble_kernel(z_ref, *refs):
+    parts, out_ref = refs[:-1], refs[-1]
+    shard = parts[0].shape[0]
+    for d, part in enumerate(parts):
+        start = pl.multiple_of(lax.rem(z_ref[0] - d + RING, RING) * shard, shard)
+        out_ref[pl.ds(start, shard)] = part[...]
+
+
+def assemble(z, parts):
+    rows, width = parts[0].shape
+    whole = pl.BlockSpec(memory_space=pltpu.VMEM)
+    return pl.pallas_call(
+        assemble_kernel,
+        in_specs=[pl.BlockSpec(memory_space=pltpu.SMEM)] + [whole] * len(parts),
+        out_specs=whole,
+        out_shape=jax.ShapeDtypeStruct((len(parts) * rows, width), jnp.bfloat16),
+        compiler_params=pltpu.CompilerParams(vmem_limit_bytes=VMEM),
+        name="assemble",
+    )(z.reshape(1), *parts)
+
+
+def finish_kernel(parts_ref, new_ref, mass_ref):
     width = new_ref.shape[2]
     ones = jnp.ones((8, EXTRA), jnp.bfloat16)
-    for d in range(RING):
-        j = lax.rem(first_ref[0] - d + RING, RING)
-        new_ref[j] = parts[d][:, :width]
-        mass = lax.dot_general(
-            ones, parts[d][:, width:], (((1,), (1,)), ((), ())), preferred_element_type=jnp.float32
-        )
+    for j in range(RING):
+        total, mass = 0.0, 0.0
+        for y in range(RING):
+            part = parts_ref[j * RING + y]
+            total = total + part.astype(jnp.float32)
+            mass = mass + lax.dot_general(
+                ones, part[:, width:], (((1,), (1,)), ((), ())), preferred_element_type=jnp.float32
+            )
+        column = jnp.sum(total[:, width:], axis=1, keepdims=True)
+        new_ref[j] = (total[:, :width] / (column + PRIOR_WEIGHT)).astype(jnp.bfloat16)
         mass_ref[pl.ds(j, 1)] = mass[:1]
 
 
-def finish(parts, first):
-    rows, width = parts[0].shape
-    whole = pl.BlockSpec(memory_space=pltpu.VMEM)
+def finish(parts):
+    _, rows, width = parts.shape
     return pl.pallas_call(
         finish_kernel,
-        in_specs=[pl.BlockSpec(memory_space=pltpu.SMEM)] + [whole] * RING,
-        out_specs=[whole] * 2,
         out_shape=[
             jax.ShapeDtypeStruct((RING, rows, width - EXTRA), jnp.bfloat16),
             jax.ShapeDtypeStruct((RING, rows), jnp.float32),
         ],
         compiler_params=pltpu.CompilerParams(vmem_limit_bytes=VMEM),
         name="finish",
-    )(first.reshape(1), *parts)
+    )(parts)
 
 
 def exchange(array, axis):
     return lax.all_to_all(array, axis, split_axis=0, concat_axis=0, tiled=True)
 
 
-def number(x, core, z, y):
-    return ((x % RING * 2 + core) * RING + z % RING) * RING + y % RING
-
-
-def move(array, step):
-    pairs = [
-        (number(x, c, z, y), number(*step(x, c, z, y)))
-        for x in range(RING)
-        for c in range(2)
-        for z in range(RING)
-        for y in range(RING)
-    ]
-    return lax.ppermute(array, AXES, pairs)
-
-
-def along(array, dx, dz, dy, flip=0):
-    return move(array, lambda x, c, z, y: (x + dx, c ^ flip, z + dz, y + dy))
-
-
-def first_slots(owner_slot, capacity, x, core, z, y):
-    to_x, to_core, j = owner_slot // 8, owner_slot // 4 % 2, owner_slot % 4
-    ra, rb = (to_x - x + y) % RING, (j - z + y) % RING
-    block = 2 * RING + to_core * RING + (j + y) % RING
-    block = jnp.where(ra == rb, to_core * RING + (y - ra) % RING, block)
-    n = 4 * RING
-    for dx, dz, dy in SWAPPED + DIRECT:
-        here = (ra == (dx - dy) % RING) & (rb == (dz - dy) % RING)
-        block = jnp.where(here, n + (to_core ^ core), block)
-        n += 2
-    return block * capacity
+def shift(array, axis, d):
+    return lax.ppermute(array, axis, [(i, (i + d) % RING) for i in range(RING)])
 
 
 def shards(points, cluster_ids, owner_slot, centroids):
     rows, width = points.shape
-    capacity = 2 * rows // owner_slot.shape[0]
-    held = centroids.shape[1]
-    x, core, z, y = (lax.axis_index(a) for a in AXES)
-
-    gathered = exchange(spread(centroids), ("z", "y"))
-    gathered = move(gathered, lambda x, c, z, y: (x + y, c, z, y))
-    by_y = gathered.reshape(RING, RING, held, width).swapaxes(0, 1).reshape(RING, -1, width)
-    blocks = [
-        lax.dynamic_index_in_dim(by_y, (y + d) % RING, 0, keepdims=False) for d in range(RING)
-    ]
-    mine = blocks[0]
-
-    line = 2 * RING
-    to_y, to_z, *leaving = scatter(
-        cluster_ids,
-        first_slots(owner_slot, capacity, x, core, z, y),
-        points,
-        capacity,
-        [line, line] + [2] * len(SWAPPED) + [1] * (2 * len(DIRECT)),
-    )
-    from_y = exchange(to_y, ("core", "y"))
-    from_z = exchange(to_z, ("core", "z"))
-    came = [along(leaving[i], *route) for i, route in enumerate(SWAPPED)]
-    other = jnp.stack([c[1] for c in came])
-    swapped = move(other, lambda x, c, z, y: (x, 1 - c, z, y))
-    straight = []
-    for i, route in enumerate(DIRECT):
-        first = len(SWAPPED) + 2 * i
-        straight.append(along(leaving[first], *route))
-        straight.append(along(leaving[first + 1], *route, 1))
-
-    arrays = [from_y] + came + [swapped, from_z] + straight
-    counts = [line] + [1] * len(SWAPPED) + [len(SWAPPED), LINE_Z] + [1] * len(straight)
-    carry = cluster_sums(z, blocks, [from_y], [line], finish=False)
+    clusters = owner_slot.shape[0]
+    capacity = 2 * rows // clusters
+    z, y = lax.axis_index("z"), lax.axis_index("y")
+
+    (leaving,) = scatter(cluster_ids, owner_slot * capacity, points, capacity, [clusters])
+    arrived = exchange(leaving, ("x", "core", "z"))
+
+    own = [lax.dynamic_index_in_dim(centroids, (z + d) % RING, 0, keepdims=False) for d in range(RING)]
+    own = own[:1] + [shift(own[d], "z", d) for d in range(1, RING)]
+    mine = assemble(z, own)
     for iteration in range(ITERS):
+        blocks = [mine] + [shift(mine, "y", -d) for d in range(1, RING)]
         last = iteration == ITERS - 1
-        if iteration == 0:
-            sums = cluster_sums(z, blocks, arrays[1:], counts[1:], carry)
-        else:
-            sums = cluster_sums(z, blocks, arrays, counts)
-        parts = [sums[0]] + [along(sums[d], d, d, d) for d in range(1, RING)]
-        mine = update(parts, mine, last)
+        sums = cluster_sums(y, blocks, [arrived], [clusters], last=last)
         if not last:
-            blocks = [mine] + [along(mine, -d, -d, -d) for d in range(1, RING)]
-    by_z = mine.reshape(RING, held, width + EXTRA)
-    leaving = [lax.dynamic_index_in_dim(by_z, (z + d) % RING, 0, keepdims=False) for d in range(RING)]
-    came = [
-        move(leaving[d], functools.partial(lambda d, x, c, z, y: (x - y, c, z + d, y), d))
-        for d in range(RING)
-    ]
-    new, mass = finish(came, (z - y) % RING)
+            parts = [sums[0]] + [shift(sums[d], "y", d) for d in range(1, RING)]
+            mine = update(parts, mine)
+    new, mass = finish(exchange(sums[0], ("z", "y")))
     return new, mass
 
 

time: 212 us -> 194 us (0.915)
  the two profiles are of different devices: /device:TPU:18 before, /device:TPU:2 now
where the time goes in v4:
time: 194 us
  waiting for transfers between devices  108 us (56%)
  Pallas kernels  35.2 us (18%)
  starting transfers between devices  30.5 us (16%)
  blocking collectives  14.8 us (8%)
  local copies, waits for them, and re-layouts  3.95 us (2%)
    ppermute x12, waiting for transfers between devices, shift(): return lax.ppermute(array, axis, [(i, (i + d) % RING) for i in range(RING)])  104 us
    ppermute x12, starting transfers between devices, shift(): return lax.ppermute(array, axis, [(i, (i + d) % RING) for i in range(RING)])  21.9 us
    pallas_call x2, Pallas kernels, cluster_sums(): pl.pallas_call(functools.partial(sums_kernel, groups, counts, 1 if carry...  20.1 us
    all_to_all x1, blocking collectives, exchange(): return lax.all_to_all(array, axis, split_axis=0, concat_axis=0, tiled=True)  14.8 us
    pallas_call x1, Pallas kernels, scatter(): pl.pallas_call(functools.partial(scatter_kernel, capacity, where), in_spe...  9.76 us
    all_to_all x1, starting transfers between devices, exchange(): return lax.all_to_all(array, axis, split_axis=0, concat_axis=0, tiled=True)  8.66 us
  transfers between devices with their start and end apart: 13, of which 9 were waited for; matrix products, arithmetic and copies ran while one was open for 0% of the time, Pallas kernels for 1%

profile of v4, /device:TPU:2, one launch (start us, length us, event | category | flops | bytes accessed | tf_op | source)
XLA Modules:
  0.0 193.7 jit_solution(9229235586648147150)
XLA Ops:
  0.6 0.7 multiply_bitcast_fusion
  1.3 0.7 copy.6.base_ref
  2.0 9.8 %scatter.1 = bf16[32,128,1024]{2,1,0:T(8,128)(2,1)} custom-call(s32[1,2048]{1,0:T(1,128)} %bitcast.13, s32[32,1]{1,0:T(8,128)} %copy.6.base_ref, bf16[2048,1024]{1,0:T(8,128)(2,1)} %points_ref.1), custom_call_target="tpu_custom_call" | custom-call | flops 2097152 | bytes 50331648 | tf_op jit(solution)/shard_map/scatter/pallas_call | solution.py:116
  11.7 0.0 copy-start.3
  11.8 8.7 %all-to-all-start = ((bf16[32,128,1024]{2,1,0:T(8,128)(2,1)}), bf16[32,128,1024]{2,1,0:T(8,128)(2,1)}, u32[]{:S(2)}, u32[]{:S(2)}) async-start(bf16[32,128,1024]{2,1,0:T(8,128)(2,1)} %scatter.1), calls=%async_computation | async-start | bytes 16777216 | tf_op jit(solution)/shard_map/all_to_all | solution.py:339
  20.5 0.0 copy-done.3
  20.5 0.6 dynamic-slice_bitcast_fusion
  21.1 2.7 %collective-permute-start.2 = (bf16[16,1024]{1,0:T(8,128)(2,1)S(1)}, bf16[16,1024]{1,0:T(8,128)(2,1)S(1)}, u32[]{:S(2)}, u32[]{:S(2)}) collective-permute-start(bf16[16,1024]{1,0:T(8,128)(2,1)S(1)} %get-tuple-element.10), channel_id=1, source_target_pairs={{0,12},{4,0},{8,4},{12,8},{1,13},{5,1},{9,5},{13,9},{2,14},{6,2},{... | collective-permute-start | bytes 98312 | tf_op jit(solution)/shard_map/ppermute | solution.py:343
  23.8 0.0 collective-permute-start
  23.8 2.3 %collective-permute-start.1 = (bf16[16,1024]{1,0:T(8,128)(2,1)S(1)}, bf16[16,1024]{1,0:T(8,128)(2,1)S(1)}, u32[]{:S(2)}, u32[]{:S(2)}) collective-permute-start(bf16[16,1024]{1,0:T(8,128)(2,1)S(1)} %get-tuple-element.13), channel_id=1, source_target_pairs={{0,8},{4,12},{8,0},{12,4},{1,9},{5,13},{9,1},{13,5},{2,10},{6,14},... | collective-permute-start | bytes 98312 | tf_op jit(solution)/shard_map/ppermute | solution.py:343
  26.1 90.6 %collective-permute-done.2.refs_3_ = bf16[16,1024]{1,0:T(8,128)(2,1)S(1)} collective-permute-done((bf16[16,1024]{1,0:T(8,128)(2,1)S(1)}, bf16[16,1024]{1,0:T(8,128)(2,1)S(1)}, u32[]{:S(2)}, u32[]{:S(2)}) %collective-permute-start.2) | collective-permute-done | bytes 32800 | tf_op jit(solution)/shard_map/ppermute | solution.py:343
  116.7 0.0 copy-start.4
  116.7 0.0 collective-permute-done.refs_1_
  116.7 0.0 copy-start.5
  116.7 0.0 collective-permute-done.1.refs_2_
  116.7 0.0 copy-start.6
  116.8 0.6 copy-done.4
  117.3 0.0 copy-done.5
  117.4 0.0 copy-done.6
  117.4 1.5 assemble.1.refs_0_.refs_4_
  118.9 1.6 collective-permute-start.5
  120.4 2.9 %collective-permute-start.4 = (bf16[64,1024]{1,0:T(8,128)(2,1)}, bf16[64,1024]{1,0:T(8,128)(2,1)S(1)}, u32[]{:S(2)}, u32[]{:S(2)}) collective-permute-start(bf16[64,1024]{1,0:T(8,128)(2,1)} %assemble.1.refs_0_.refs_4_), channel_id=1, source_target_pairs={{0,2},{1,3},{2,0},{3,1},{4,6},{5,7},{6,4},{7,5},{8,10},{9,11},{10,... | collective-permute-start | bytes 393224 | tf_op jit(solution)/shard_map/ppermute | solution.py:343
  123.3 1.3 collective-permute-start.3
  124.7 1.1 collective-permute-done.5.refs_3_
  125.8 0.0 copy-start.7
  125.8 3.3 %collective-permute-done.4.refs_2_ = bf16[64,1024]{1,0:T(8,128)(2,1)S(1)} collective-permute-done((bf16[64,1024]{1,0:T(8,128)(2,1)}, bf16[64,1024]{1,0:T(8,128)(2,1)S(1)}, u32[]{:S(2)}, u32[]{:S(2)}) %collective-permute-start.4) | collective-permute-done | bytes 131104 | tf_op jit(solution)/shard_map/ppermute | solution.py:343
  129.1 0.0 copy-start.8
  129.1 0.0 collective-permute-done.3.refs_1_
  129.1 0.0 copy-start.9
  129.1 3.3 %all-to-all-done.refs_4_ = bf16[32,128,1024]{2,1,0:T(8,128)(2,1)} async-done(((bf16[32,128,1024]{2,1,0:T(8,128)(2,1)}), bf16[32,128,1024]{2,1,0:T(8,128)(2,1)}, u32[]{:S(2)}, u32[]{:S(2)}) %all-to-all-start) | async-done | bytes 8388640 | tf_op jit(solution)/shard_map/all_to_all | solution.py:339
  132.5 0.0 copy-done.7
  132.5 0.0 copy-done.8
  132.5 0.0 copy-done.9
  132.5 10.0 %cluster_sums.2 = (bf16[64,1152]{1,0:T(8,128)(2,1)}, bf16[64,1152]{1,0:T(8,128)(2,1)}, bf16[64,1152]{1,0:T(8,128)(2,1)}, bf16[64,1152]{1,0:T(8,128)(2,1)}) custom-call(s32[1]{0:T(128)} %bitcast.y_ref, bf16[64,1024]{1,0:T(8,128)(2,1)} %assemble.1.refs_0_.refs_4_, bf16[64,1024]{1,0:T(8,128)(2,1)} %copy-done.9, bf16[64,1024]{1,0:T(8,128)(2,1)} %copy-done.8, ...), custom_call_target="tpu_custom_call" | custom-call | flops 4294967296 | bytes 9437184 | tf_op jit(solution)/shard_map/cluster_sums/pallas_call | solution.py:227
  142.5 1.7 collective-permute-start.6
  144.1 2.9 %collective-permute-start.7 = (bf16[64,1152]{1,0:T(8,128)(2,1)}, bf16[64,1152]{1,0:T(8,128)(2,1)S(1)}, u32[]{:S(2)}, u32[]{:S(2)}) collective-permute-start(bf16[64,1152]{1,0:T(8,128)(2,1)} %get-tuple-element.8), channel_id=1, source_target_pairs={{0,2},{1,3},{2,0},{3,1},{4,6},{5,7},{6,4},{7,5},{8,10},{9,11},{10,... | collective-permute-start | bytes 442376 | tf_op jit(solution)/shard_map/ppermute | solution.py:343
  147.0 1.3 collective-permute-start.8
  148.4 1.2 collective-permute-done.6.refs_1_
  149.6 0.0 copy-start
  149.6 4.1 %collective-permute-done.7.refs_2_ = bf16[64,1152]{1,0:T(8,128)(2,1)S(1)} collective-permute-done((bf16[64,1152]{1,0:T(8,128)(2,1)}, bf16[64,1152]{1,0:T(8,128)(2,1)S(1)}, u32[]{:S(2)}, u32[]{:S(2)}) %collective-permute-start.7) | collective-permute-done | bytes 147488 | tf_op jit(solution)/shard_map/ppermute | solution.py:343
  153.8 0.0 copy-start.1
  153.8 0.0 collective-permute-done.8.refs_3_
  153.8 0.0 copy-start.2
  153.8 0.0 copy-done
  153.8 0.7 copy-done.1
  154.4 0.1 copy-done.2
  154.5 2.0 %update.1.refs_0_ = bf16[64,1024]{1,0:T(8,128)(2,1)} custom-call(bf16[64,1152]{1,0:T(8,128)(2,1)} %get-tuple-element.6.refs_0_, bf16[64,1152]{1,0:T(8,128)(2,1)} %copy-done, bf16[64,1152]{1,0:T(8,128)(2,1)} %copy-done.1, bf16[64,1152]{1,0:T(8,128)(2,1)} %copy-done.2, bf16[64,1024]{1,0:T(8,128)(2,1)} %assemble.1.refs_0_.refs_4_), custom_call_target="tpu_custom_call" | custom-call | flops 262144 | bytes 786432 | tf_op jit(solution)/shard_map/update/pallas_call | solution.py:275
  156.5 1.2 collective-permute-start.11
  157.6 2.4 %collective-permute-start.10 = (bf16[64,1024]{1,0:T(8,128)(2,1)}, bf16[64,1024]{1,0:T(8,128)(2,1)S(1)}, u32[]{:S(2)}, u32[]{:S(2)}) collective-permute-start(bf16[64,1024]{1,0:T(8,128)(2,1)} %update.1.refs_0_), channel_id=1, source_target_pairs={{0,2},{1,3},{2,0},{3,1},{4,6},{5,7},{6,4},{7,5},{8,10},{9,11},{10,... | collective-permute-start | bytes 393224 | tf_op jit(solution)/shard_map/ppermute | solution.py:343
  160.0 1.6 collective-permute-start.9
  161.6 2.5 %collective-permute-done.11.refs_3_ = bf16[64,1024]{1,0:T(8,128)(2,1)S(1)} collective-permute-done((bf16[64,1024]{1,0:T(8,128)(2,1)}, bf16[64,1024]{1,0:T(8,128)(2,1)S(1)}, u32[]{:S(2)}, u32[]{:S(2)}) %collective-permute-start.11) | collective-permute-done | bytes 131104 | tf_op jit(solution)/shard_map/ppermute | solution.py:343
  164.1 0.0 copy-start.10
  164.1 1.4 collective-permute-done.10.refs_2_
  165.5 0.0 copy-start.11
  165.5 0.1 collective-permute-done.9.refs_1_
  165.6 0.0 copy-done.10
  165.6 0.6 copy-done.11
  166.2 0.0 copy-start.12
  166.2 0.7 copy-done.12
  166.8 10.1 %cluster_sums.3 = bf16[16,16,1152]{2,1,0:T(8,128)(2,1)} custom-call(s32[1]{0:T(128)} %bitcast.y_ref, bf16[64,1024]{1,0:T(8,128)(2,1)} %update.1.refs_0_, bf16[64,1024]{1,0:T(8,128)(2,1)} %copy-done.12, bf16[64,1024]{1,0:T(8,128)(2,1)} %copy-done.11, bf16[64,1024]{1,0:T(8,128)(2,1)} %copy-done.10, bf16[32,128,1024]{2,1,0:T(8,128)(2,1)} %all-to-all-done.refs_4_), custom_call_target="tpu_custom_call" | custom-call | flops 4294967296 | bytes 9437184 | tf_op jit(solution)/shard_map/cluster_sums/pallas_call | solution.py:227
  176.9 14.8 %all_to_all.10.parts_ref = bf16[16,16,1152]{2,1,0:T(8,128)(2,1)} all-to-all(bf16[16,16,1152]{2,1,0:T(8,128)(2,1)} %cluster_sums.3), channel_id=1, replica_groups=mesh['x'=4,'core'=2,'z'=4,'y'=4] {'z','y'}, dimensions={0} | all-to-all | bytes 1179648 | tf_op jit(solution)/shard_map/all_to_all | solution.py:339
  191.8 1.9 finish.1
Async XLA Ops:
  11.7 8.7 %copy-start.3 = (bf16[4,16,1024]{2,1,0:T(8,128)(2,1)S(1)}, bf16[4,16,1024]{2,1,0:T(8,128)(2,1)}, u32[]{:S(2)}) copy-start(bf16[4,16,1024]{2,1,0:T(8,128)(2,1)} %param.7) | copy-start | bytes 393220
  11.8 120.7 %all-to-all-start = ((bf16[32,128,1024]{2,1,0:T(8,128)(2,1)}), bf16[32,128,1024]{2,1,0:T(8,128)(2,1)}, u32[]{:S(2)}, u32[]{:S(2)}) async-start(bf16[32,128,1024]{2,1,0:T(8,128)(2,1)} %scatter.1), calls=%async_computation | async-start | bytes 16777216 | tf_op jit(solution)/shard_map/all_to_all | solution.py:339
  21.1 95.6 %collective-permute-start.2 = (bf16[16,1024]{1,0:T(8,128)(2,1)S(1)}, bf16[16,1024]{1,0:T(8,128)(2,1)S(1)}, u32[]{:S(2)}, u32[]{:S(2)}) collective-permute-start(bf16[16,1024]{1,0:T(8,128)(2,1)S(1)} %get-tuple-element.10), channel_id=1, source_target_pairs={{0,12},{4,0},{8,4},{12,8},{1,13},{5,1},{9,5},{13,9},{2,14},{6,2},{... | collective-permute-start | bytes 98312 | tf_op jit(solution)/shard_map/ppermute | solution.py:343
  23.8 92.9 %collective-permute-start = (bf16[16,1024]{1,0:T(8,128)(2,1)S(1)}, bf16[16,1024]{1,0:T(8,128)(2,1)S(1)}, u32[]{:S(2)}, u32[]{:S(2)}) collective-permute-start(bf16[16,1024]{1,0:T(8,128)(2,1)S(1)} %get-tuple-element.11), channel_id=1, source_target_pairs={{0,4},{4,8},{8,12},{12,0},{1,5},{5,9},{9,13},{13,1},{2,6},{6,10},{... | collective-permute-start | bytes 98312 | tf_op jit(solution)/shard_map/ppermute | solution.py:343
  23.8 92.9 %collective-permute-start.1 = (bf16[16,1024]{1,0:T(8,128)(2,1)S(1)}, bf16[16,1024]{1,0:T(8,128)(2,1)S(1)}, u32[]{:S(2)}, u32[]{:S(2)}) collective-permute-start(bf16[16,1024]{1,0:T(8,128)(2,1)S(1)} %get-tuple-element.13), channel_id=1, source_target_pairs={{0,8},{4,12},{8,0},{12,4},{1,9},{5,13},{9,1},{13,5},{2,10},{6,14},... | collective-permute-start | bytes 98312 | tf_op jit(solution)/shard_map/ppermute | solution.py:343
  116.7 0.6 copy-start.4
  116.7 0.6 copy-start.5
  116.7 0.6 copy-start.6
  118.9 6.9 %collective-permute-start.5 = (bf16[64,1024]{1,0:T(8,128)(2,1)}, bf16[64,1024]{1,0:T(8,128)(2,1)S(1)}, u32[]{:S(2)}, u32[]{:S(2)}) collective-permute-start(bf16[64,1024]{1,0:T(8,128)(2,1)} %assemble.1.refs_0_.refs_4_), channel_id=1, source_target_pairs={{0,1},{1,2},{2,3},{3,0},{4,5},{5,6},{6,7},{7,4},{8,9},{9,10},{10,1... | collective-permute-start | bytes 393224 | tf_op jit(solution)/shard_map/ppermute | solution.py:343
  120.4 8.7 %collective-permute-start.4 = (bf16[64,1024]{1,0:T(8,128)(2,1)}, bf16[64,1024]{1,0:T(8,128)(2,1)S(1)}, u32[]{:S(2)}, u32[]{:S(2)}) collective-permute-start(bf16[64,1024]{1,0:T(8,128)(2,1)} %assemble.1.refs_0_.refs_4_), channel_id=1, source_target_pairs={{0,2},{1,3},{2,0},{3,1},{4,6},{5,7},{6,4},{7,5},{8,10},{9,11},{10,... | collective-permute-start | bytes 393224 | tf_op jit(solution)/shard_map/ppermute | solution.py:343
  123.3 5.8 %collective-permute-start.3 = (bf16[64,1024]{1,0:T(8,128)(2,1)}, bf16[64,1024]{1,0:T(8,128)(2,1)S(1)}, u32[]{:S(2)}, u32[]{:S(2)}) collective-permute-start(bf16[64,1024]{1,0:T(8,128)(2,1)} %assemble.1.refs_0_.refs_4_), channel_id=1, source_target_pairs={{0,3},{1,0},{2,1},{3,2},{4,7},{5,4},{6,5},{7,6},{8,11},{9,8},{10,9... | collective-permute-start | bytes 393224 | tf_op jit(solution)/shard_map/ppermute | solution.py:343
  125.8 6.7 %copy-start.7 = (bf16[64,1024]{1,0:T(8,128)(2,1)}, bf16[64,1024]{1,0:T(8,128)(2,1)S(1)}, u32[]{:S(2)}) copy-start(bf16[64,1024]{1,0:T(8,128)(2,1)S(1)} %collective-permute-done.5.refs_3_) | copy-start | bytes 393220
  129.1 3.3 %copy-start.8 = (bf16[64,1024]{1,0:T(8,128)(2,1)}, bf16[64,1024]{1,0:T(8,128)(2,1)S(1)}, u32[]{:S(2)}) copy-start(bf16[64,1024]{1,0:T(8,128)(2,1)S(1)} %collective-permute-done.4.refs_2_) | copy-start | bytes 393220
  129.1 3.3 %copy-start.9 = (bf16[64,1024]{1,0:T(8,128)(2,1)}, bf16[64,1024]{1,0:T(8,128)(2,1)S(1)}, u32[]{:S(2)}) copy-start(bf16[64,1024]{1,0:T(8,128)(2,1)S(1)} %collective-permute-done.3.refs_1_) | copy-start | bytes 393220
  142.5 7.1 %collective-permute-start.6 = (bf16[64,1152]{1,0:T(8,128)(2,1)}, bf16[64,1152]{1,0:T(8,128)(2,1)S(1)}, u32[]{:S(2)}, u32[]{:S(2)}) collective-permute-start(bf16[64,1152]{1,0:T(8,128)(2,1)} %get-tuple-element.7), channel_id=1, source_target_pairs={{0,1},{1,2},{2,3},{3,0},{4,5},{5,6},{6,7},{7,4},{8,9},{9,10},{10,1... | collective-permute-start | bytes 442376 | tf_op jit(solution)/shard_map/ppermute | solution.py:343
  144.1 9.6 %collective-permute-start.7 = (bf16[64,1152]{1,0:T(8,128)(2,1)}, bf16[64,1152]{1,0:T(8,128)(2,1)S(1)}, u32[]{:S(2)}, u32[]{:S(2)}) collective-permute-start(bf16[64,1152]{1,0:T(8,128)(2,1)} %get-tuple-element.8), channel_id=1, source_target_pairs={{0,2},{1,3},{2,0},{3,1},{4,6},{5,7},{6,4},{7,5},{8,10},{9,11},{10,... | collective-permute-start | bytes 442376 | tf_op jit(solution)/shard_map/ppermute | solution.py:343
  147.0 6.7 %collective-permute-start.8 = (bf16[64,1152]{1,0:T(8,128)(2,1)}, bf16[64,1152]{1,0:T(8,128)(2,1)S(1)}, u32[]{:S(2)}, u32[]{:S(2)}) collective-permute-start(bf16[64,1152]{1,0:T(8,128)(2,1)} %get-tuple-element.9), channel_id=1, source_target_pairs={{0,3},{1,0},{2,1},{3,2},{4,7},{5,4},{6,5},{7,6},{8,11},{9,8},{10,9... | collective-permute-start | bytes 442376 | tf_op jit(solution)/shard_map/ppermute | solution.py:343
  149.6 4.1 %copy-start = (bf16[64,1152]{1,0:T(8,128)(2,1)}, bf16[64,1152]{1,0:T(8,128)(2,1)S(1)}, u32[]{:S(2)}) copy-start(bf16[64,1152]{1,0:T(8,128)(2,1)S(1)} %collective-permute-done.6.refs_1_) | copy-start | bytes 442372
  153.8 0.7 copy-start.1
  153.8 0.7 copy-start.2
  156.5 7.7 %collective-permute-start.11 = (bf16[64,1024]{1,0:T(8,128)(2,1)}, bf16[64,1024]{1,0:T(8,128)(2,1)S(1)}, u32[]{:S(2)}, u32[]{:S(2)}) collective-permute-start(bf16[64,1024]{1,0:T(8,128)(2,1)} %update.1.refs_0_), channel_id=1, source_target_pairs={{0,1},{1,2},{2,3},{3,0},{4,5},{5,6},{6,7},{7,4},{8,9},{9,10},{10,1... | collective-permute-start | bytes 393224 | tf_op jit(solution)/shard_map/ppermute | solution.py:343
  157.6 7.9 %collective-permute-start.10 = (bf16[64,1024]{1,0:T(8,128)(2,1)}, bf16[64,1024]{1,0:T(8,128)(2,1)S(1)}, u32[]{:S(2)}, u32[]{:S(2)}) collective-permute-start(bf16[64,1024]{1,0:T(8,128)(2,1)} %update.1.refs_0_), channel_id=1, source_target_pairs={{0,2},{1,3},{2,0},{3,1},{4,6},{5,7},{6,4},{7,5},{8,10},{9,11},{10,... | collective-permute-start | bytes 393224 | tf_op jit(solution)/shard_map/ppermute | solution.py:343
  160.0 5.6 %collective-permute-start.9 = (bf16[64,1024]{1,0:T(8,128)(2,1)}, bf16[64,1024]{1,0:T(8,128)(2,1)S(1)}, u32[]{:S(2)}, u32[]{:S(2)}) collective-permute-start(bf16[64,1024]{1,0:T(8,128)(2,1)} %update.1.refs_0_), channel_id=1, source_target_pairs={{0,3},{1,0},{2,1},{3,2},{4,7},{5,4},{6,5},{7,6},{8,11},{9,8},{10,9... | collective-permute-start | bytes 393224 | tf_op jit(solution)/shard_map/ppermute | solution.py:343
  164.1 1.5 copy-start.10
  165.5 0.7 copy-start.11
  166.2 0.7 copy-start.12

commit v5 on v4

--- a/solution.py
+++ b/solution.py
@@ -7,7 +7,6 @@
 from jax.experimental.pallas import tpu as pltpu
 from jax.sharding import Mesh, PartitionSpec as P
 
-ITERS = 2
 SCORE_SCALE = 0.25
 PRIOR_WEIGHT = 1.0
 EXTRA = 128
@@ -22,7 +21,7 @@
 AXES = ("x", "core", "z", "y")
 
 
-def scatter_kernel(capacity, where, ids_ref, base_ref, points_ref, *refs):
+def scatter_kernel(capacity, where, ids_ref, owner_ref, points_ref, *refs):
     outs, (slots_v, slots_s, x, wide, placed, packed, in_sems, out_sems, slot_sem) = (
         refs[:-9],
         refs[-9:],
@@ -40,13 +39,17 @@
     for load in loads:
         load.start()
 
-    clusters = base_ref.shape[0]
+    clusters = owner_ref.shape[1]
     before = (
         lax.broadcasted_iota(jnp.int32, (GROUP, GROUP), 0)
         < lax.broadcasted_iota(jnp.int32, (GROUP, GROUP), 1)
     ).astype(jnp.float32).astype(jnp.bfloat16)
     table = lax.broadcasted_iota(jnp.int32, (clusters, GROUP), 0)
-    base = base_ref[...].astype(jnp.float32)
+    same = lax.broadcasted_iota(jnp.int32, (clusters, clusters), 0) == (
+        lax.broadcasted_iota(jnp.int32, (clusters, clusters), 1)
+    )
+    owners = jnp.broadcast_to(owner_ref[...], (clusters, clusters)).astype(jnp.float32)
+    base = jnp.sum(jnp.where(same, owners, 0.0), axis=1, keepdims=True) * capacity
     for g in range(rows // GROUP):
         span = pl.ds(g * GROUP, GROUP)
         hit = (table == ids_ref[:, span]).astype(jnp.float32)
@@ -106,7 +109,7 @@
         store.wait()
 
 
-def scatter(cluster_ids, base, points, capacity, blocks):
+def scatter(cluster_ids, owner_slot, points, capacity, blocks):
     rows, width = points.shape
     where = [(o, k) for o, count in enumerate(blocks) for k in range(count)]
     any_space = pl.BlockSpec(memory_space=pl.ANY)
@@ -136,19 +139,24 @@
             transcendentals=0,
         ),
         name="scatter",
-    )(cluster_ids.reshape(1, rows), base.reshape(-1, 1), points)
-
-
-def sums_kernel(groups, counts, carried, last, y_ref, *refs):
-    blocks, refs = refs[:groups], refs[groups:]
-    sources, refs = refs[: len(counts)], refs[len(counts) :]
-    carry, refs = refs[: 2 * carried], refs[2 * carried :]
-    outs, (aug, total, mass, bias, rows, sems) = refs[:-6], refs[-6:]
-    held, width = blocks[0].shape
+    )(cluster_ids.reshape(1, rows), owner_slot.reshape(1, -1), points)
+
+
+def sums_kernel(groups, last, y_ref, source, *refs):
+    if last:
+        blocks, refs = refs[:groups], refs[groups:]
+    else:
+        blocks, refs = [refs[0].at[g] for g in range(groups)], refs[1:]
+    if last:
+        rows, outs, (aug, total, mass, bias) = source, refs[:1], refs[1:]
+    else:
+        rows, outs, (aug, total, mass, bias, sems) = refs[0], refs[1:-5], refs[-5:]
+    held, width = blocks[0].shape[-2:]
     cents = groups * held
-    pieces = [(ref, i) for ref, count in zip(sources, counts) for i in range(count)]
-    for n, (ref, i) in enumerate(pieces):
-        pltpu.make_async_copy(ref.at[i], rows.at[n], sems.at[n]).start()
+    pieces = rows.shape[0]
+    if not last:
+        for n in range(pieces):
+            pltpu.make_async_copy(source.at[n], rows.at[n], sems.at[n]).start()
 
     for g in range(groups):
         mu = blocks[g][...]
@@ -158,19 +166,16 @@
         bias[span] = 0.5 * jnp.sum(wide * wide, axis=1, keepdims=True)
     unit = lax.broadcasted_iota(jnp.int32, (aug.shape[0] - cents, width), 1) == 0
     aug[cents:] = unit.astype(jnp.float32).astype(jnp.bfloat16)
-    if carried:
-        total[...] = carry[0][...]
-        mass[...] = carry[1][...]
-    else:
-        total[...] = jnp.zeros_like(total)
-        mass[...] = jnp.zeros_like(mass)
+    total[...] = jnp.zeros_like(total)
+    mass[...] = jnp.zeros_like(mass)
     if last:
         total[:held] += PRIOR_WEIGHT * blocks[0][...].astype(jnp.float32)
 
     def tile(t, _):
-        for i in range(TILE):
-            n = t * TILE + i
-            pltpu.make_async_copy(sources[0].at[0], rows.at[n], sems.at[n]).wait()
+        if not last:
+            for i in range(TILE):
+                n = t * TILE + i
+                pltpu.make_async_copy(source.at[n], rows.at[n], sems.at[n]).wait()
         x = rows[pl.ds(t * TILE, TILE)].reshape(-1, width)
         raw = lax.dot_general(
             aug[...], x, (((1,), (1,)), ((), ())), preferred_element_type=jnp.float32
@@ -183,11 +188,7 @@
         total[...] += jnp.dot(w.astype(jnp.bfloat16), x, preferred_element_type=jnp.float32)
         return 0
 
-    lax.fori_loop(0, len(pieces) // TILE, tile, 0)
-    if not last and len(outs) == 2:
-        outs[0][...] = total[...]
-        outs[1][...] = mass[...]
-        return
+    lax.fori_loop(0, pieces // TILE, tile, 0)
     if not last:
         lane = lax.broadcasted_iota(jnp.int32, (held, EXTRA), 1)
         for g in range(groups):
@@ -206,30 +207,29 @@
             outs[0][holder, :, width:] = terms(mass[span], lane)
 
 
-def cluster_sums(y, blocks, sources, counts, carry=(), partial=False, last=False):
-    groups = len(blocks)
-    held, width = blocks[0].shape
-    capacity = sources[0].shape[1]
-    cents, pieces = groups * held, sum(counts)
+def cluster_sums(y, blocks, rows, last):
+    groups = RING
+    held, width = blocks[0].shape[-2:]
+    pieces, capacity, _ = rows.shape
+    cents = groups * held
     assert pieces % TILE == 0
     whole = pl.BlockSpec(memory_space=pltpu.VMEM)
-    if partial:
-        shapes = [
-            jax.ShapeDtypeStruct((cents, width), jnp.float32),
-            jax.ShapeDtypeStruct((cents, 1), jnp.float32),
-        ]
-    elif last:
+    if last:
         shape = (groups * RING, held // RING, width + EXTRA)
         shapes = [jax.ShapeDtypeStruct(shape, jnp.bfloat16)]
+        sems = []
     else:
-        shapes = [jax.ShapeDtypeStruct((held, width + EXTRA), jnp.bfloat16)] * groups
+        shapes = [pltpu.VMEM(rows.shape, rows.dtype)]
+        shapes += [jax.ShapeDtypeStruct((held, width + EXTRA), jnp.bfloat16)] * groups
+        sems = [pltpu.SemaphoreType.DMA((pieces,))]
     count = pieces * capacity
     return pl.pallas_call(
-        functools.partial(sums_kernel, groups, counts, 1 if carry else 0, last),
-        in_specs=[pl.BlockSpec(memory_space=pltpu.SMEM)]
-        + [whole] * groups
-        + [pl.BlockSpec(memory_space=pl.ANY)] * len(sources)
-        + [whole] * len(carry),
+        functools.partial(sums_kernel, groups, last),
+        in_specs=[
+            pl.BlockSpec(memory_space=pltpu.SMEM),
+            whole if last else pl.BlockSpec(memory_space=pl.ANY),
+        ]
+        + [whole] * len(blocks),
         out_specs=[whole] * len(shapes),
         out_shape=shapes,
         scratch_shapes=[
@@ -237,17 +237,16 @@
             pltpu.VMEM((cents, width), jnp.float32),
             pltpu.VMEM((cents, 1), jnp.float32),
             pltpu.VMEM((cents, 1), jnp.float32),
-            pltpu.VMEM((pieces, capacity, width), jnp.bfloat16),
-            pltpu.SemaphoreType.DMA((pieces,)),
-        ],
-        compiler_params=pltpu.CompilerParams(vmem_limit_bytes=VMEM),
+        ]
+        + sems,
+        compiler_params=pltpu.CompilerParams(vmem_limit_bytes=32 * MIB),
         cost_estimate=pl.CostEstimate(
             flops=4 * count * cents * width,
             bytes_accessed=2 * width * (count + 2 * cents),
             transcendentals=count * cents,
         ),
         name="cluster_sums",
-    )(y.reshape(1), *blocks, *sources, *carry)
+    )(y.reshape(1), rows, *blocks)
 
 
 def terms(m, lane):
@@ -260,22 +259,22 @@
 
 def update_kernel(*refs):
     parts, mu_ref, out_ref = refs[:-2], refs[-2], refs[-1]
-    width = mu_ref.shape[1]
+    width = mu_ref.shape[-1]
     total = parts[0][...].astype(jnp.float32)
     for part in parts[1:]:
         total = total + part[...].astype(jnp.float32)
     mass = jnp.sum(total[:, width:], axis=1, keepdims=True)
-    mu = mu_ref[...].astype(jnp.float32)
+    mu = mu_ref[0].astype(jnp.float32)
     new = (total[:, :width] + PRIOR_WEIGHT * mu) / (mass + PRIOR_WEIGHT)
     out_ref[...] = new.astype(jnp.bfloat16)
 
 
 def update(parts, mu):
-    rows, width = mu.shape
+    rows, width = mu.shape[-2:]
     return pl.pallas_call(
         update_kernel,
         out_shape=jax.ShapeDtypeStruct((rows, width), jnp.bfloat16),
-        compiler_params=pltpu.CompilerParams(vmem_limit_bytes=VMEM),
+        compiler_params=pltpu.CompilerParams(vmem_limit_bytes=16 * MIB),
         cost_estimate=pl.CostEstimate(
             flops=len(parts) * rows * width,
             bytes_accessed=2 * (len(parts) + 2) * rows * width,
@@ -285,23 +284,44 @@
     )(*parts, mu)
 
 
+def choose_kernel(z_ref, *refs):
+    parts, outs = refs[:RING], refs[RING:]
+    for d, out_ref in enumerate(outs):
+        j = lax.rem(z_ref[0] + d, RING)
+        for g, part in enumerate(parts):
+            out_ref[g] = part[j]
+
+
+def choose(z, parts):
+    whole = pl.BlockSpec(memory_space=pltpu.VMEM)
+    return pl.pallas_call(
+        choose_kernel,
+        in_specs=[pl.BlockSpec(memory_space=pltpu.SMEM)] + [whole] * RING,
+        out_specs=[whole] * RING,
+        out_shape=[jax.ShapeDtypeStruct(parts[0].shape, parts[0].dtype)] * RING,
+        compiler_params=pltpu.CompilerParams(vmem_limit_bytes=16 * MIB),
+        name="choose",
+    )(z.reshape(1), *parts)
+
+
 def assemble_kernel(z_ref, *refs):
     parts, out_ref = refs[:-1], refs[-1]
-    shard = parts[0].shape[0]
+    groups, shard, _ = parts[0].shape
     for d, part in enumerate(parts):
         start = pl.multiple_of(lax.rem(z_ref[0] - d + RING, RING) * shard, shard)
-        out_ref[pl.ds(start, shard)] = part[...]
+        for g in range(groups):
+            out_ref[g, pl.ds(start, shard)] = part[g]
 
 
 def assemble(z, parts):
-    rows, width = parts[0].shape
+    groups, rows, width = parts[0].shape
     whole = pl.BlockSpec(memory_space=pltpu.VMEM)
     return pl.pallas_call(
         assemble_kernel,
         in_specs=[pl.BlockSpec(memory_space=pltpu.SMEM)] + [whole] * len(parts),
         out_specs=whole,
-        out_shape=jax.ShapeDtypeStruct((len(parts) * rows, width), jnp.bfloat16),
-        compiler_params=pltpu.CompilerParams(vmem_limit_bytes=VMEM),
+        out_shape=jax.ShapeDtypeStruct((groups, len(parts) * rows, width), jnp.bfloat16),
+        compiler_params=pltpu.CompilerParams(vmem_limit_bytes=16 * MIB),
         name="assemble",
     )(z.reshape(1), *parts)
 
@@ -330,7 +350,7 @@
             jax.ShapeDtypeStruct((RING, rows, width - EXTRA), jnp.bfloat16),
             jax.ShapeDtypeStruct((RING, rows), jnp.float32),
         ],
-        compiler_params=pltpu.CompilerParams(vmem_limit_bytes=VMEM),
+        compiler_params=pltpu.CompilerParams(vmem_limit_bytes=16 * MIB),
         name="finish",
     )(parts)
 
@@ -349,20 +369,18 @@
     capacity = 2 * rows // clusters
     z, y = lax.axis_index("z"), lax.axis_index("y")
 
-    (leaving,) = scatter(cluster_ids, owner_slot * capacity, points, capacity, [clusters])
+    (leaving,) = scatter(cluster_ids, owner_slot, points, capacity, [clusters])
     arrived = exchange(leaving, ("x", "core", "z"))
 
-    own = [lax.dynamic_index_in_dim(centroids, (z + d) % RING, 0, keepdims=False) for d in range(RING)]
-    own = own[:1] + [shift(own[d], "z", d) for d in range(1, RING)]
-    mine = assemble(z, own)
-    for iteration in range(ITERS):
-        blocks = [mine] + [shift(mine, "y", -d) for d in range(1, RING)]
-        last = iteration == ITERS - 1
-        sums = cluster_sums(y, blocks, [arrived], [clusters], last=last)
-        if not last:
-            parts = [sums[0]] + [shift(sums[d], "y", d) for d in range(1, RING)]
-            mine = update(parts, mine)
-    new, mass = finish(exchange(sums[0], ("z", "y")))
+    by_y = [centroids] + [shift(centroids, "y", -d) for d in range(1, RING)]
+    to_z = list(choose(z, by_y))
+    block = assemble(z, to_z[:1] + [shift(to_z[d], "z", d) for d in range(1, RING)])
+    arrived, *sums = cluster_sums(y, [block], arrived, False)
+    parts = [sums[0]] + [shift(sums[d], "y", d) for d in range(1, RING)]
+    mine = update(parts, block)
+    blocks = [mine] + [shift(mine, "y", -d) for d in range(1, RING)]
+    (sums,) = cluster_sums(y, blocks, arrived, True)
+    new, mass = finish(exchange(sums, ("z", "y")))
     return new, mass
 
 

time: 194 us -> 181 us (0.933)
  Pallas kernels: 35.2 us -> 25.1 us
  local copies, waits for them, and re-layouts: 3.95 us -> 0.01 us
  waiting for transfers between devices: 108 us -> 110 us
    all_to_all x1, waiting for transfers between devices: 3.33 us -> 9.13 us  [exchange(): return lax.all_to_all(array, axis, split_axis=0, concat_axis=0, tiled=True)]
    pallas_call x2 -> x3, Pallas kernels: 20.1 us -> 14.5 us  [the longest x2 14.4 us: cluster_sums(): pl.pallas_call(functools.partial(sums_kernel, groups, last), in_specs=[pl...]
    ppermute x12, waiting for transfers between devices: 104 us -> 101 us  [shift(): return lax.ppermute(array, axis, [(i, (i + d) % RING) for i in range(RING)])]
    unnamed x26 -> x2, local copies, waits for them, and re-layouts: 2.63 us -> 0.01 us
  transfers between devices with their start and end apart: 13 -> 13, of which waited for: 9 -> 11; matrix products, arithmetic and copies ran while one was open for 0% -> 0% of each run, Pallas kernels for 1% -> 0%
where the time goes in v5:
time: 181 us
  waiting for transfers between devices  110 us (61%)
  starting transfers between devices  30.8 us (17%)
  Pallas kernels  25.1 us (14%)
  blocking collectives  14.3 us (8%)
    ppermute x12, waiting for transfers between devices, shift(): return lax.ppermute(array, axis, [(i, (i + d) % RING) for i in range(RING)])  101 us
    ppermute x12, starting transfers between devices, shift(): return lax.ppermute(array, axis, [(i, (i + d) % RING) for i in range(RING)])  22.1 us
    pallas_call x2, Pallas kernels, cluster_sums(): pl.pallas_call(functools.partial(sums_kernel, groups, last), in_specs=[pl...  14.4 us
    all_to_all x1, blocking collectives, exchange(): return lax.all_to_all(array, axis, split_axis=0, concat_axis=0, tiled=True)  14.3 us
    pallas_call x1, Pallas kernels, scatter(): pl.pallas_call(functools.partial(scatter_kernel, capacity, where), in_spe...  9.71 us
    all_to_all x1, waiting for transfers between devices, exchange(): return lax.all_to_all(array, axis, split_axis=0, concat_axis=0, tiled=True)  9.13 us
    all_to_all x1, starting transfers between devices, exchange(): return lax.all_to_all(array, axis, split_axis=0, concat_axis=0, tiled=True)  8.66 us
  transfers between devices with their start and end apart: 13, of which 11 were waited for; matrix products, arithmetic and copies ran while one was open for 0% of the time, Pallas kernels for 0%

profile of v5, /device:TPU:2, one launch (start us, length us, event | category | flops | bytes accessed | tf_op | source)
XLA Modules:
  0.0 180.9 jit_solution(672892791435270455)
XLA Ops:
  0.6 9.7 %scatter.1 = bf16[32,128,1024]{2,1,0:T(8,128)(2,1)} custom-call(s32[1,2048]{1,0:T(1,128)} %bitcast.4, s32[1,32]{1,0:T(1,128)} %bitcast.5, bf16[2048,1024]{1,0:T(8,128)(2,1)} %points_ref.1), custom_call_target="tpu_custom_call" | custom-call | flops 2097152 | bytes 50331648 | tf_op jit(solution)/shard_map/scatter/pallas_call | solution.py:119
  10.4 0.0 copy-start
  10.4 8.7 %all-to-all-start = ((bf16[32,128,1024]{2,1,0:T(8,128)(2,1)}), bf16[32,128,1024]{2,1,0:T(8,128)(2,1)}, u32[]{:S(2)}, u32[]{:S(2)}) async-start(bf16[32,128,1024]{2,1,0:T(8,128)(2,1)} %scatter.1), calls=%async_computation | async-start | bytes 16777216 | tf_op jit(solution)/shard_map/all_to_all | solution.py:359
  19.0 0.0 copy-done
  19.0 3.3 %collective-permute-start.1 = (bf16[4,16,1024]{2,1,0:T(8,128)(2,1)S(1)}, bf16[4,16,1024]{2,1,0:T(8,128)(2,1)S(1)}, u32[]{:S(2)}, u32[]{:S(2)}) collective-permute-start(bf16[4,16,1024]{2,1,0:T(8,128)(2,1)S(1)} %copy-done), channel_id=1, source_target_pairs={{0,2},{1,3},{2,0},{3,1},{4,6},{5,7},{6,4},{7,5},{8,10},{9,11},{10,... | collective-permute-start | bytes 393224 | tf_op jit(solution)/shard_map/ppermute | solution.py:363
  22.3 1.1 collective-permute-start
  23.4 1.0 collective-permute-start.2
  24.3 2.5 %collective-permute-done.1.refs_2_ = bf16[4,16,1024]{2,1,0:T(8,128)(2,1)S(1)} collective-permute-done((bf16[4,16,1024]{2,1,0:T(8,128)(2,1)S(1)}, bf16[4,16,1024]{2,1,0:T(8,128)(2,1)S(1)}, u32[]{:S(2)}, u32[]{:S(2)}) %collective-permute-start.1) | collective-permute-done | bytes 131104 | tf_op jit(solution)/shard_map/ppermute | solution.py:363
  26.8 2.5 %collective-permute-done.refs_1_ = bf16[4,16,1024]{2,1,0:T(8,128)(2,1)S(1)} collective-permute-done((bf16[4,16,1024]{2,1,0:T(8,128)(2,1)S(1)}, bf16[4,16,1024]{2,1,0:T(8,128)(2,1)S(1)}, u32[]{:S(2)}, u32[]{:S(2)}) %collective-permute-start) | collective-permute-done | bytes 131104 | tf_op jit(solution)/shard_map/ppermute | solution.py:363
  29.3 0.3 collective-permute-done.2.refs_3_
  29.6 1.5 collective-permute-start.3
  31.2 2.7 %collective-permute-start.4 = (bf16[4,16,1024]{2,1,0:T(8,128)(2,1)S(1)}, bf16[4,16,1024]{2,1,0:T(8,128)(2,1)S(1)}, u32[]{:S(2)}, u32[]{:S(2)}) collective-permute-start(bf16[4,16,1024]{2,1,0:T(8,128)(2,1)S(1)} %get-tuple-element.13), channel_id=1, source_target_pairs={{0,8},{4,12},{8,0},{12,4},{1,9},{5,13},{9,1},{13,5},{2,10},{6,14},... | collective-permute-start | bytes 393224 | tf_op jit(solution)/shard_map/ppermute | solution.py:363
  33.8 1.5 collective-permute-start.5
  35.3 79.8 %collective-permute-done.3.refs_1_ = bf16[4,16,1024]{2,1,0:T(8,128)(2,1)S(1)} collective-permute-done((bf16[4,16,1024]{2,1,0:T(8,128)(2,1)S(1)}, bf16[4,16,1024]{2,1,0:T(8,128)(2,1)S(1)}, u32[]{:S(2)}, u32[]{:S(2)}) %collective-permute-start.3) | collective-permute-done | bytes 131104 | tf_op jit(solution)/shard_map/ppermute | solution.py:363
  115.1 6.7 %collective-permute-done.4.refs_2_ = bf16[4,16,1024]{2,1,0:T(8,128)(2,1)S(1)} collective-permute-done((bf16[4,16,1024]{2,1,0:T(8,128)(2,1)S(1)}, bf16[4,16,1024]{2,1,0:T(8,128)(2,1)S(1)}, u32[]{:S(2)}, u32[]{:S(2)}) %collective-permute-start.4) | collective-permute-done | bytes 131104 | tf_op jit(solution)/shard_map/ppermute | solution.py:363
  121.9 0.0 collective-permute-done.5.refs_3_
  121.9 9.1 %all-to-all-done.source = bf16[32,128,1024]{2,1,0:T(8,128)(2,1)} async-done(((bf16[32,128,1024]{2,1,0:T(8,128)(2,1)}), bf16[32,128,1024]{2,1,0:T(8,128)(2,1)}, u32[]{:S(2)}, u32[]{:S(2)}) %all-to-all-start) | async-done | bytes 8388640 | tf_op jit(solution)/shard_map/all_to_all | solution.py:359
  131.0 8.0 %cluster_sums.2 = (bf16[32,128,1024]{2,1,0:T(8,128)(2,1)S(1)}, bf16[64,1152]{1,0:T(8,128)(2,1)S(1)}, bf16[64,1152]{1,0:T(8,128)(2,1)S(1)}, bf16[64,1152]{1,0:T(8,128)(2,1)S(1)}, bf16[64,1152]{1,0:T(8,128)(2,1)S(1)}) custom-call(s32[1]{0:T(128)} %bitcast.y_ref, bf16[32,128,1024]{2,1,0:T(8,128)(2,1)} %all-to-all-done.source, ...), custom_call_target="tpu_custom_call" | custom-call | flops 4294967296 | bytes 9437184 | tf_op jit(solution)/shard_map/cluster_sums/pallas_call | solution.py:226
  139.1 1.7 collective-permute-start.6
  140.7 2.9 %collective-permute-start.7 = (bf16[64,1152]{1,0:T(8,128)(2,1)S(1)}, bf16[64,1152]{1,0:T(8,128)(2,1)S(1)}, u32[]{:S(2)}, u32[]{:S(2)}) collective-permute-start(bf16[64,1152]{1,0:T(8,128)(2,1)S(1)} %get-tuple-element.18), channel_id=1, source_target_pairs={{0,2},{1,3},{2,0},{3,1},{4,6},{5,7},{6,4},{7,5},{8,10},{9,11},{10,... | collective-permute-start | bytes 442376 | tf_op jit(solution)/shard_map/ppermute | solution.py:363
  143.6 1.3 collective-permute-start.8
  145.0 1.0 collective-permute-done.6.refs_1_
  146.0 4.1 %collective-permute-done.7.refs_2_ = bf16[64,1152]{1,0:T(8,128)(2,1)S(1)} collective-permute-done((bf16[64,1152]{1,0:T(8,128)(2,1)S(1)}, bf16[64,1152]{1,0:T(8,128)(2,1)S(1)}, u32[]{:S(2)}, u32[]{:S(2)}) %collective-permute-start.7) | collective-permute-done | bytes 147488 | tf_op jit(solution)/shard_map/ppermute | solution.py:363
  150.2 0.0 collective-permute-done.8.refs_3_
  150.2 0.1 update.1.refs_0_
  150.3 1.3 collective-permute-start.11
  151.6 2.4 %collective-permute-start.10 = (bf16[64,1024]{1,0:T(8,128)(2,1)S(1)}, bf16[64,1024]{1,0:T(8,128)(2,1)S(1)}, u32[]{:S(2)}, u32[]{:S(2)}) collective-permute-start(bf16[64,1024]{1,0:T(8,128)(2,1)S(1)} %update.1.refs_0_), channel_id=1, source_target_pairs={{0,2},{1,3},{2,0},{3,1},{4,6},{5,7},{6,4},{7,5},{8,10},{9,11},{10,... | collective-permute-start | bytes 393224 | tf_op jit(solution)/shard_map/ppermute | solution.py:363
  154.0 1.6 collective-permute-start.9
  155.6 2.3 %collective-permute-done.11.refs_3_ = bf16[64,1024]{1,0:T(8,128)(2,1)S(1)} collective-permute-done((bf16[64,1024]{1,0:T(8,128)(2,1)S(1)}, bf16[64,1024]{1,0:T(8,128)(2,1)S(1)}, u32[]{:S(2)}, u32[]{:S(2)}) %collective-permute-start.11) | collective-permute-done | bytes 131104 | tf_op jit(solution)/shard_map/ppermute | solution.py:363
  157.9 1.4 collective-permute-done.10.refs_2_
  159.3 0.1 collective-permute-done.9.refs_1_
  159.3 6.4 %cluster_sums.3 = bf16[16,16,1152]{2,1,0:T(8,128)(2,1)S(1)} custom-call(s32[1]{0:T(128)} %bitcast.y_ref, bf16[32,128,1024]{2,1,0:T(8,128)(2,1)S(1)} %get-tuple-element.15.source, bf16[64,1024]{1,0:T(8,128)(2,1)S(1)} %update.1.refs_0_, bf16[64,1024]{1,0:T(8,128)(2,1)S(1)} %collective-permute-done.9.refs_1_, ...), custom_call_target="tpu_custom_call" | custom-call | flops 4294967296 | bytes 9437184 | tf_op jit(solution)/shard_map/cluster_sums/pallas_call | solution.py:226
  165.8 14.3 %all_to_all.10.parts_ref = bf16[16,16,1152]{2,1,0:T(8,128)(2,1)S(1)} all-to-all(bf16[16,16,1152]{2,1,0:T(8,128)(2,1)S(1)} %cluster_sums.3), channel_id=1, replica_groups=mesh['x'=4,'core'=2,'z'=4,'y'=4] {'z','y'}, dimensions={0} | all-to-all | bytes 1179648 | tf_op jit(solution)/shard_map/all_to_all | solution.py:359
  180.1 0.8 finish.1
  (2 shorter events, 0.1 us)
Async XLA Ops:
  10.4 8.7 %copy-start = (bf16[4,16,1024]{2,1,0:T(8,128)(2,1)S(1)}, bf16[4,16,1024]{2,1,0:T(8,128)(2,1)}, u32[]{:S(2)}) copy-start(bf16[4,16,1024]{2,1,0:T(8,128)(2,1)} %refs_0_.1) | copy-start | bytes 393220
  10.4 120.7 %all-to-all-start = ((bf16[32,128,1024]{2,1,0:T(8,128)(2,1)}), bf16[32,128,1024]{2,1,0:T(8,128)(2,1)}, u32[]{:S(2)}, u32[]{:S(2)}) async-start(bf16[32,128,1024]{2,1,0:T(8,128)(2,1)} %scatter.1), calls=%async_computation | async-start | bytes 16777216 | tf_op jit(solution)/shard_map/all_to_all | solution.py:359
  19.0 7.8 %collective-permute-start.1 = (bf16[4,16,1024]{2,1,0:T(8,128)(2,1)S(1)}, bf16[4,16,1024]{2,1,0:T(8,128)(2,1)S(1)}, u32[]{:S(2)}, u32[]{:S(2)}) collective-permute-start(bf16[4,16,1024]{2,1,0:T(8,128)(2,1)S(1)} %copy-done), channel_id=1, source_target_pairs={{0,2},{1,3},{2,0},{3,1},{4,6},{5,7},{6,4},{7,5},{8,10},{9,11},{10,... | collective-permute-start | bytes 393224 | tf_op jit(solution)/shard_map/ppermute | solution.py:363
  22.3 7.0 %collective-permute-start = (bf16[4,16,1024]{2,1,0:T(8,128)(2,1)S(1)}, bf16[4,16,1024]{2,1,0:T(8,128)(2,1)S(1)}, u32[]{:S(2)}, u32[]{:S(2)}) collective-permute-start(bf16[4,16,1024]{2,1,0:T(8,128)(2,1)S(1)} %copy-done), channel_id=1, source_target_pairs={{0,3},{1,0},{2,1},{3,2},{4,7},{5,4},{6,5},{7,6},{8,11},{9,8},{10,9... | collective-permute-start | bytes 393224 | tf_op jit(solution)/shard_map/ppermute | solution.py:363
  23.4 6.2 %collective-permute-start.2 = (bf16[4,16,1024]{2,1,0:T(8,128)(2,1)S(1)}, bf16[4,16,1024]{2,1,0:T(8,128)(2,1)S(1)}, u32[]{:S(2)}, u32[]{:S(2)}) collective-permute-start(bf16[4,16,1024]{2,1,0:T(8,128)(2,1)S(1)} %copy-done), channel_id=1, source_target_pairs={{0,1},{1,2},{2,3},{3,0},{4,5},{5,6},{6,7},{7,4},{8,9},{9,10},{10,1... | collective-permute-start | bytes 393224 | tf_op jit(solution)/shard_map/ppermute | solution.py:363
  29.6 85.5 %collective-permute-start.3 = (bf16[4,16,1024]{2,1,0:T(8,128)(2,1)S(1)}, bf16[4,16,1024]{2,1,0:T(8,128)(2,1)S(1)}, u32[]{:S(2)}, u32[]{:S(2)}) collective-permute-start(bf16[4,16,1024]{2,1,0:T(8,128)(2,1)S(1)} %get-tuple-element.12), channel_id=1, source_target_pairs={{0,4},{4,8},{8,12},{12,0},{1,5},{5,9},{9,13},{13,1},{2,6},{6,10},{... | collective-permute-start | bytes 393224 | tf_op jit(solution)/shard_map/ppermute | solution.py:363
  31.2 90.7 %collective-permute-start.4 = (bf16[4,16,1024]{2,1,0:T(8,128)(2,1)S(1)}, bf16[4,16,1024]{2,1,0:T(8,128)(2,1)S(1)}, u32[]{:S(2)}, u32[]{:S(2)}) collective-permute-start(bf16[4,16,1024]{2,1,0:T(8,128)(2,1)S(1)} %get-tuple-element.13), channel_id=1, source_target_pairs={{0,8},{4,12},{8,0},{12,4},{1,9},{5,13},{9,1},{13,5},{2,10},{6,14},... | collective-permute-start | bytes 393224 | tf_op jit(solution)/shard_map/ppermute | solution.py:363
  33.8 88.0 %collective-permute-start.5 = (bf16[4,16,1024]{2,1,0:T(8,128)(2,1)S(1)}, bf16[4,16,1024]{2,1,0:T(8,128)(2,1)S(1)}, u32[]{:S(2)}, u32[]{:S(2)}) collective-permute-start(bf16[4,16,1024]{2,1,0:T(8,128)(2,1)S(1)} %get-tuple-element.14), channel_id=1, source_target_pairs={{0,12},{4,0},{8,4},{12,8},{1,13},{5,1},{9,5},{13,9},{2,14},{6,2},{... | collective-permute-start | bytes 393224 | tf_op jit(solution)/shard_map/ppermute | solution.py:363
  139.1 6.9 %collective-permute-start.6 = (bf16[64,1152]{1,0:T(8,128)(2,1)S(1)}, bf16[64,1152]{1,0:T(8,128)(2,1)S(1)}, u32[]{:S(2)}, u32[]{:S(2)}) collective-permute-start(bf16[64,1152]{1,0:T(8,128)(2,1)S(1)} %get-tuple-element.17), channel_id=1, source_target_pairs={{0,1},{1,2},{2,3},{3,0},{4,5},{5,6},{6,7},{7,4},{8,9},{9,10},{10,1... | collective-permute-start | bytes 442376 | tf_op jit(solution)/shard_map/ppermute | solution.py:363
  140.7 9.4 %collective-permute-start.7 = (bf16[64,1152]{1,0:T(8,128)(2,1)S(1)}, bf16[64,1152]{1,0:T(8,128)(2,1)S(1)}, u32[]{:S(2)}, u32[]{:S(2)}) collective-permute-start(bf16[64,1152]{1,0:T(8,128)(2,1)S(1)} %get-tuple-element.18), channel_id=1, source_target_pairs={{0,2},{1,3},{2,0},{3,1},{4,6},{5,7},{6,4},{7,5},{8,10},{9,11},{10,... | collective-permute-start | bytes 442376 | tf_op jit(solution)/shard_map/ppermute | solution.py:363
  143.6 6.5 %collective-permute-start.8 = (bf16[64,1152]{1,0:T(8,128)(2,1)S(1)}, bf16[64,1152]{1,0:T(8,128)(2,1)S(1)}, u32[]{:S(2)}, u32[]{:S(2)}) collective-permute-start(bf16[64,1152]{1,0:T(8,128)(2,1)S(1)} %get-tuple-element.19), channel_id=1, source_target_pairs={{0,3},{1,0},{2,1},{3,2},{4,7},{5,4},{6,5},{7,6},{8,11},{9,8},{10,9... | collective-permute-start | bytes 442376 | tf_op jit(solution)/shard_map/ppermute | solution.py:363
  150.3 7.6 %collective-permute-start.11 = (bf16[64,1024]{1,0:T(8,128)(2,1)S(1)}, bf16[64,1024]{1,0:T(8,128)(2,1)S(1)}, u32[]{:S(2)}, u32[]{:S(2)}) collective-permute-start(bf16[64,1024]{1,0:T(8,128)(2,1)S(1)} %update.1.refs_0_), channel_id=1, source_target_pairs={{0,1},{1,2},{2,3},{3,0},{4,5},{5,6},{6,7},{7,4},{8,9},{9,10},{10,1... | collective-permute-start | bytes 393224 | tf_op jit(solution)/shard_map/ppermute | solution.py:363
  151.6 7.7 %collective-permute-start.10 = (bf16[64,1024]{1,0:T(8,128)(2,1)S(1)}, bf16[64,1024]{1,0:T(8,128)(2,1)S(1)}, u32[]{:S(2)}, u32[]{:S(2)}) collective-permute-start(bf16[64,1024]{1,0:T(8,128)(2,1)S(1)} %update.1.refs_0_), channel_id=1, source_target_pairs={{0,2},{1,3},{2,0},{3,1},{4,6},{5,7},{6,4},{7,5},{8,10},{9,11},{10,... | collective-permute-start | bytes 393224 | tf_op jit(solution)/shard_map/ppermute | solution.py:363
  154.0 5.4 %collective-permute-start.9 = (bf16[64,1024]{1,0:T(8,128)(2,1)S(1)}, bf16[64,1024]{1,0:T(8,128)(2,1)S(1)}, u32[]{:S(2)}, u32[]{:S(2)}) collective-permute-start(bf16[64,1024]{1,0:T(8,128)(2,1)S(1)} %update.1.refs_0_), channel_id=1, source_target_pairs={{0,3},{1,0},{2,1},{3,2},{4,7},{5,4},{6,5},{7,6},{8,11},{9,8},{10,9... | collective-permute-start | bytes 393224 | tf_op jit(solution)/shard_map/ppermute | solution.py:363

commit v6 on v5

--- a/solution.py
+++ b/solution.py
@@ -48,7 +48,9 @@
     same = lax.broadcasted_iota(jnp.int32, (clusters, clusters), 0) == (
         lax.broadcasted_iota(jnp.int32, (clusters, clusters), 1)
     )
-    owners = jnp.broadcast_to(owner_ref[...], (clusters, clusters)).astype(jnp.float32)
+    owner = owner_ref[...]
+    order = (owner // 8) * 1 + (owner // 4 % 2) * 4 + (owner % 4) * 8
+    owners = jnp.broadcast_to(order, (clusters, clusters)).astype(jnp.float32)
     base = jnp.sum(jnp.where(same, owners, 0.0), axis=1, keepdims=True) * capacity
     for g in range(rows // GROUP):
         span = pl.ds(g * GROUP, GROUP)
@@ -87,7 +89,7 @@
             placed[pl.ds(slots_s[0, i * 2 * SUB + r], SUB, stride=SUB)] = row
         return 0
 
-    lax.fori_loop(0, rows // (2 * SUB), move_rows, 0)
+    lax.fori_loop(0, rows // (2 * SUB), move_rows, 0, unroll=2)
 
     stores = []
     for n, (o, k) in enumerate(where):
@@ -171,24 +173,32 @@
     if last:
         total[:held] += PRIOR_WEIGHT * blocks[0][...].astype(jnp.float32)
 
-    def tile(t, _):
+    def load(t):
         if not last:
-            for i in range(TILE):
-                n = t * TILE + i
+            for n in range(t * TILE, (t + 1) * TILE):
                 pltpu.make_async_copy(source.at[n], rows.at[n], sems.at[n]).wait()
-        x = rows[pl.ds(t * TILE, TILE)].reshape(-1, width)
-        raw = lax.dot_general(
+        return rows[t * TILE : (t + 1) * TILE].reshape(-1, width)
+
+    def product(x):
+        return lax.dot_general(
             aug[...], x, (((1,), (1,)), ((), ())), preferred_element_type=jnp.float32
         )
-        score = (raw[:cents] - bias[...]) * SCORE_SCALE
-        present = (raw[cents : cents + 1] < MARK_LIMIT).astype(jnp.float32)
+
+    x = load(0)
+    raw = product(x)
+    for t in range(pieces // TILE):
+        now, members = raw, x
+        if (t + 1) * TILE < pieces:
+            x = load(t + 1)
+            raw = product(x)
+        score = (now[:cents] - bias[...]) * SCORE_SCALE
+        present = (now[cents : cents + 1] < MARK_LIMIT).astype(jnp.float32)
         e = jnp.exp(score - jnp.max(score, axis=0, keepdims=True))
         w = e * (present / jnp.sum(e, axis=0, keepdims=True))
         mass[...] += jnp.sum(w, axis=1, keepdims=True)
-        total[...] += jnp.dot(w.astype(jnp.bfloat16), x, preferred_element_type=jnp.float32)
-        return 0
-
-    lax.fori_loop(0, pieces // TILE, tile, 0)
+        total[...] += jnp.dot(
+            w.astype(jnp.bfloat16), members, preferred_element_type=jnp.float32
+        )
     if not last:
         lane = lax.broadcasted_iota(jnp.int32, (held, EXTRA), 1)
         for g in range(groups):
@@ -370,15 +380,16 @@
     z, y = lax.axis_index("z"), lax.axis_index("y")
 
     (leaving,) = scatter(cluster_ids, owner_slot, points, capacity, [clusters])
-    arrived = exchange(leaving, ("x", "core", "z"))
+    arrived = exchange(leaving, ("z", "core", "x"))
 
     by_y = [centroids] + [shift(centroids, "y", -d) for d in range(1, RING)]
     to_z = list(choose(z, by_y))
     block = assemble(z, to_z[:1] + [shift(to_z[d], "z", d) for d in range(1, RING)])
     arrived, *sums = cluster_sums(y, [block], arrived, False)
-    parts = [sums[0]] + [shift(sums[d], "y", d) for d in range(1, RING)]
+    parts = [sums[0]] + [shift(sums[d], "y", d) for d in (2, 1, 3)]
     mine = update(parts, block)
-    blocks = [mine] + [shift(mine, "y", -d) for d in range(1, RING)]
+    near, back, far = (shift(mine, "y", -d) for d in (1, 3, 2))
+    blocks = [mine, near, far, back]
     (sums,) = cluster_sums(y, blocks, arrived, True)
     new, mass = finish(exchange(sums, ("z", "y")))
     return new, mass

time: 181 us -> 171 us (0.945); the launches traced: 181 us -> 168 us
  waiting for transfers between devices: 110 us -> 97.6 us
    all_to_all x1, waiting for transfers between devices: 9.13 us -> 0.01 us  [exchange(): return lax.all_to_all(array, axis, split_axis=0, concat_axis=0, tiled=True)]
    ppermute x12, waiting for transfers between devices: 101 us -> 97.6 us  [shift(): return lax.ppermute(array, axis, [(i, (i + d) % RING) for i in range(RING)])]
  transfers between devices with their start and end apart: 13 -> 13, of which waited for: 11 -> 10; matrix products, arithmetic and copies ran while one was open for 0% -> 0% of each run, Pallas kernels for 0% -> 0%
where the time goes in v6:
time: 171 us; the launch traced here: 168 us
  waiting for transfers between devices  97.6 us (57%)
  starting transfers between devices  30.9 us (18%)
  Pallas kernels  23.4 us (14%)
  blocking collectives  15.4 us (9%)
    ppermute x12, waiting for transfers between devices, shift(): return lax.ppermute(array, axis, [(i, (i + d) % RING) for i in range(RING)])  97.6 us
    ppermute x12, starting transfers between devices, shift(): return lax.ppermute(array, axis, [(i, (i + d) % RING) for i in range(RING)])  22.2 us
    all_to_all x1, blocking collectives, exchange(): return lax.all_to_all(array, axis, split_axis=0, concat_axis=0, tiled=True)  15.4 us
    pallas_call x2, Pallas kernels, cluster_sums(): pl.pallas_call(functools.partial(sums_kernel, groups, last), in_specs=[pl...  12.9 us
    pallas_call x1, Pallas kernels, scatter(): pl.pallas_call(functools.partial(scatter_kernel, capacity, where), in_spe...  9.43 us
    all_to_all x1, starting transfers between devices, exchange(): return lax.all_to_all(array, axis, split_axis=0, concat_axis=0, tiled=True)  8.66 us
  transfers between devices with their start and end apart: 13, of which 10 were waited for; matrix products, arithmetic and copies ran while one was open for 0% of the time, Pallas kernels for 0%

profile of v6, /device:TPU:2, one launch (start us, length us, event | category | flops | bytes accessed | tf_op | source)
XLA Modules:
  0.0 168.0 jit_solution(7983855452317791946)
XLA Ops:
  0.6 9.4 %scatter.1 = bf16[32,128,1024]{2,1,0:T(8,128)(2,1)} custom-call(s32[1,2048]{1,0:T(1,128)} %bitcast.4, s32[1,32]{1,0:T(1,128)} %bitcast.5, bf16[2048,1024]{1,0:T(8,128)(2,1)} %points_ref.1), custom_call_target="tpu_custom_call" | custom-call | flops 2097152 | bytes 50331648 | tf_op jit(solution)/shard_map/scatter/pallas_call | solution.py:121
  10.1 0.0 copy-start
  10.1 8.7 %all-to-all-start = ((bf16[32,128,1024]{2,1,0:T(8,128)(2,1)}), bf16[32,128,1024]{2,1,0:T(8,128)(2,1)}, u32[]{:S(2)}, u32[]{:S(2)}) async-start(bf16[32,128,1024]{2,1,0:T(8,128)(2,1)} %scatter.1), calls=%async_computation | async-start | bytes 16777216 | tf_op jit(solution)/shard_map/all_to_all | solution.py:369
  18.7 0.0 copy-done
  18.8 3.3 %collective-permute-start.1 = (bf16[4,16,1024]{2,1,0:T(8,128)(2,1)S(1)}, bf16[4,16,1024]{2,1,0:T(8,128)(2,1)S(1)}, u32[]{:S(2)}, u32[]{:S(2)}) collective-permute-start(bf16[4,16,1024]{2,1,0:T(8,128)(2,1)S(1)} %copy-done), channel_id=1, source_target_pairs={{0,2},{1,3},{2,0},{3,1},{4,6},{5,7},{6,4},{7,5},{8,10},{9,11},{10,... | collective-permute-start | bytes 393224 | tf_op jit(solution)/shard_map/ppermute | solution.py:373
  22.0 1.1 collective-permute-start
  23.1 1.0 collective-permute-start.2
  24.1 2.5 %collective-permute-done.1.refs_2_ = bf16[4,16,1024]{2,1,0:T(8,128)(2,1)S(1)} collective-permute-done((bf16[4,16,1024]{2,1,0:T(8,128)(2,1)S(1)}, bf16[4,16,1024]{2,1,0:T(8,128)(2,1)S(1)}, u32[]{:S(2)}, u32[]{:S(2)}) %collective-permute-start.1) | collective-permute-done | bytes 131104 | tf_op jit(solution)/shard_map/ppermute | solution.py:373
  26.5 2.5 %collective-permute-done.refs_1_ = bf16[4,16,1024]{2,1,0:T(8,128)(2,1)S(1)} collective-permute-done((bf16[4,16,1024]{2,1,0:T(8,128)(2,1)S(1)}, bf16[4,16,1024]{2,1,0:T(8,128)(2,1)S(1)}, u32[]{:S(2)}, u32[]{:S(2)}) %collective-permute-start) | collective-permute-done | bytes 131104 | tf_op jit(solution)/shard_map/ppermute | solution.py:373
  29.0 0.3 collective-permute-done.2.refs_3_
  29.3 1.5 collective-permute-start.3
  30.9 2.7 %collective-permute-start.4 = (bf16[4,16,1024]{2,1,0:T(8,128)(2,1)S(1)}, bf16[4,16,1024]{2,1,0:T(8,128)(2,1)S(1)}, u32[]{:S(2)}, u32[]{:S(2)}) collective-permute-start(bf16[4,16,1024]{2,1,0:T(8,128)(2,1)S(1)} %get-tuple-element.13), channel_id=1, source_target_pairs={{0,8},{4,12},{8,0},{12,4},{1,9},{5,13},{9,1},{13,5},{2,10},{6,14},... | collective-permute-start | bytes 393224 | tf_op jit(solution)/shard_map/ppermute | solution.py:373
  33.6 1.4 collective-permute-start.5
  35.0 76.2 %collective-permute-done.3.refs_1_ = bf16[4,16,1024]{2,1,0:T(8,128)(2,1)S(1)} collective-permute-done((bf16[4,16,1024]{2,1,0:T(8,128)(2,1)S(1)}, bf16[4,16,1024]{2,1,0:T(8,128)(2,1)S(1)}, u32[]{:S(2)}, u32[]{:S(2)}) %collective-permute-start.3) | collective-permute-done | bytes 131104 | tf_op jit(solution)/shard_map/ppermute | solution.py:373
  111.3 7.0 %collective-permute-done.4.refs_2_ = bf16[4,16,1024]{2,1,0:T(8,128)(2,1)S(1)} collective-permute-done((bf16[4,16,1024]{2,1,0:T(8,128)(2,1)S(1)}, bf16[4,16,1024]{2,1,0:T(8,128)(2,1)S(1)}, u32[]{:S(2)}, u32[]{:S(2)}) %collective-permute-start.4) | collective-permute-done | bytes 131104 | tf_op jit(solution)/shard_map/ppermute | solution.py:373
  118.3 0.0 collective-permute-done.5.refs_3_
  118.3 0.0 all-to-all-done.source
  118.3 7.7 %cluster_sums.2 = (bf16[32,128,1024]{2,1,0:T(8,128)(2,1)S(1)}, bf16[64,1152]{1,0:T(8,128)(2,1)S(1)}, bf16[64,1152]{1,0:T(8,128)(2,1)S(1)}, bf16[64,1152]{1,0:T(8,128)(2,1)S(1)}, bf16[64,1152]{1,0:T(8,128)(2,1)S(1)}) custom-call(s32[1]{0:T(128)} %bitcast.y_ref, bf16[32,128,1024]{2,1,0:T(8,128)(2,1)} %all-to-all-done.source, ...), custom_call_target="tpu_custom_call" | custom-call | flops 4294967296 | bytes 9437184 | tf_op jit(solution)/shard_map/cluster_sums/pallas_call | solution.py:236
  126.1 3.3 %collective-permute-start.6 = (bf16[64,1152]{1,0:T(8,128)(2,1)S(1)}, bf16[64,1152]{1,0:T(8,128)(2,1)S(1)}, u32[]{:S(2)}, u32[]{:S(2)}) collective-permute-start(bf16[64,1152]{1,0:T(8,128)(2,1)S(1)} %get-tuple-element.17), channel_id=1, source_target_pairs={{0,2},{1,3},{2,0},{3,1},{4,6},{5,7},{6,4},{7,5},{8,10},{9,11},{10,... | collective-permute-start | bytes 442376 | tf_op jit(solution)/shard_map/ppermute | solution.py:373
  129.4 0.7 collective-permute-start.7
  130.0 2.6 %collective-permute-start.8 = (bf16[64,1152]{1,0:T(8,128)(2,1)S(1)}, bf16[64,1152]{1,0:T(8,128)(2,1)S(1)}, u32[]{:S(2)}, u32[]{:S(2)}) collective-permute-start(bf16[64,1152]{1,0:T(8,128)(2,1)S(1)} %get-tuple-element.19), channel_id=1, source_target_pairs={{0,3},{1,0},{2,1},{3,2},{4,7},{5,4},{6,5},{7,6},{8,11},{9,8},{10,9... | collective-permute-start | bytes 442376 | tf_op jit(solution)/shard_map/ppermute | solution.py:373
  132.6 1.7 %collective-permute-done.6.refs_1_ = bf16[64,1152]{1,0:T(8,128)(2,1)S(1)} collective-permute-done((bf16[64,1152]{1,0:T(8,128)(2,1)S(1)}, bf16[64,1152]{1,0:T(8,128)(2,1)S(1)}, u32[]{:S(2)}, u32[]{:S(2)}) %collective-permute-start.6) | collective-permute-done | bytes 147488 | tf_op jit(solution)/shard_map/ppermute | solution.py:373
  134.3 2.2 %collective-permute-done.7.refs_2_ = bf16[64,1152]{1,0:T(8,128)(2,1)S(1)} collective-permute-done((bf16[64,1152]{1,0:T(8,128)(2,1)S(1)}, bf16[64,1152]{1,0:T(8,128)(2,1)S(1)}, u32[]{:S(2)}, u32[]{:S(2)}) %collective-permute-start.7) | collective-permute-done | bytes 147488 | tf_op jit(solution)/shard_map/ppermute | solution.py:373
  136.6 0.0 collective-permute-done.8.refs_3_
  136.6 0.1 update.1.refs_0_
  136.7 1.4 collective-permute-start.11
  138.1 3.1 %collective-permute-start.10 = (bf16[64,1024]{1,0:T(8,128)(2,1)S(1)}, bf16[64,1024]{1,0:T(8,128)(2,1)S(1)}, u32[]{:S(2)}, u32[]{:S(2)}) collective-permute-start(bf16[64,1024]{1,0:T(8,128)(2,1)S(1)} %update.1.refs_0_), channel_id=1, source_target_pairs={{0,2},{1,3},{2,0},{3,1},{4,6},{5,7},{6,4},{7,5},{8,10},{9,11},{10,... | collective-permute-start | bytes 393224 | tf_op jit(solution)/shard_map/ppermute | solution.py:373
  141.3 0.2 collective-permute-start.9
  141.4 2.7 %collective-permute-done.11.refs_3_ = bf16[64,1024]{1,0:T(8,128)(2,1)S(1)} collective-permute-done((bf16[64,1024]{1,0:T(8,128)(2,1)S(1)}, bf16[64,1024]{1,0:T(8,128)(2,1)S(1)}, u32[]{:S(2)}, u32[]{:S(2)}) %collective-permute-start.11) | collective-permute-done | bytes 131104 | tf_op jit(solution)/shard_map/ppermute | solution.py:373
  144.1 2.4 %collective-permute-done.10.refs_2_ = bf16[64,1024]{1,0:T(8,128)(2,1)S(1)} collective-permute-done((bf16[64,1024]{1,0:T(8,128)(2,1)S(1)}, bf16[64,1024]{1,0:T(8,128)(2,1)S(1)}, u32[]{:S(2)}, u32[]{:S(2)}) %collective-permute-start.10) | collective-permute-done | bytes 131104 | tf_op jit(solution)/shard_map/ppermute | solution.py:373
  146.5 0.1 collective-permute-done.9.refs_1_
  146.6 5.2 %cluster_sums.3 = bf16[16,16,1152]{2,1,0:T(8,128)(2,1)S(1)} custom-call(s32[1]{0:T(128)} %bitcast.y_ref, bf16[32,128,1024]{2,1,0:T(8,128)(2,1)S(1)} %get-tuple-element.15.source, bf16[64,1024]{1,0:T(8,128)(2,1)S(1)} %update.1.refs_0_, bf16[64,1024]{1,0:T(8,128)(2,1)S(1)} %collective-permute-done.9.refs_1_, ...), custom_call_target="tpu_custom_call" | custom-call | flops 4294967296 | bytes 9437184 | tf_op jit(solution)/shard_map/cluster_sums/pallas_call | solution.py:236
  151.8 15.4 %all_to_all.10.parts_ref = bf16[16,16,1152]{2,1,0:T(8,128)(2,1)S(1)} all-to-all(bf16[16,16,1152]{2,1,0:T(8,128)(2,1)S(1)} %cluster_sums.3), channel_id=1, replica_groups=mesh['x'=4,'core'=2,'z'=4,'y'=4] {'z','y'}, dimensions={0} | all-to-all | bytes 1179648 | tf_op jit(solution)/shard_map/all_to_all | solution.py:369
  167.2 0.8 finish.1
  (2 shorter events, 0.1 us)
Async XLA Ops:
  10.1 8.7 %copy-start = (bf16[4,16,1024]{2,1,0:T(8,128)(2,1)S(1)}, bf16[4,16,1024]{2,1,0:T(8,128)(2,1)}, u32[]{:S(2)}) copy-start(bf16[4,16,1024]{2,1,0:T(8,128)(2,1)} %refs_0_.1) | copy-start | bytes 393220
  10.1 108.2 %all-to-all-start = ((bf16[32,128,1024]{2,1,0:T(8,128)(2,1)}), bf16[32,128,1024]{2,1,0:T(8,128)(2,1)}, u32[]{:S(2)}, u32[]{:S(2)}) async-start(bf16[32,128,1024]{2,1,0:T(8,128)(2,1)} %scatter.1), calls=%async_computation | async-start | bytes 16777216 | tf_op jit(solution)/shard_map/all_to_all | solution.py:369
  18.8 7.8 %collective-permute-start.1 = (bf16[4,16,1024]{2,1,0:T(8,128)(2,1)S(1)}, bf16[4,16,1024]{2,1,0:T(8,128)(2,1)S(1)}, u32[]{:S(2)}, u32[]{:S(2)}) collective-permute-start(bf16[4,16,1024]{2,1,0:T(8,128)(2,1)S(1)} %copy-done), channel_id=1, source_target_pairs={{0,2},{1,3},{2,0},{3,1},{4,6},{5,7},{6,4},{7,5},{8,10},{9,11},{10,... | collective-permute-start | bytes 393224 | tf_op jit(solution)/shard_map/ppermute | solution.py:373
  22.0 7.0 %collective-permute-start = (bf16[4,16,1024]{2,1,0:T(8,128)(2,1)S(1)}, bf16[4,16,1024]{2,1,0:T(8,128)(2,1)S(1)}, u32[]{:S(2)}, u32[]{:S(2)}) collective-permute-start(bf16[4,16,1024]{2,1,0:T(8,128)(2,1)S(1)} %copy-done), channel_id=1, source_target_pairs={{0,3},{1,0},{2,1},{3,2},{4,7},{5,4},{6,5},{7,6},{8,11},{9,8},{10,9... | collective-permute-start | bytes 393224 | tf_op jit(solution)/shard_map/ppermute | solution.py:373
  23.1 6.2 %collective-permute-start.2 = (bf16[4,16,1024]{2,1,0:T(8,128)(2,1)S(1)}, bf16[4,16,1024]{2,1,0:T(8,128)(2,1)S(1)}, u32[]{:S(2)}, u32[]{:S(2)}) collective-permute-start(bf16[4,16,1024]{2,1,0:T(8,128)(2,1)S(1)} %copy-done), channel_id=1, source_target_pairs={{0,1},{1,2},{2,3},{3,0},{4,5},{5,6},{6,7},{7,4},{8,9},{9,10},{10,1... | collective-permute-start | bytes 393224 | tf_op jit(solution)/shard_map/ppermute | solution.py:373
  29.3 81.9 %collective-permute-start.3 = (bf16[4,16,1024]{2,1,0:T(8,128)(2,1)S(1)}, bf16[4,16,1024]{2,1,0:T(8,128)(2,1)S(1)}, u32[]{:S(2)}, u32[]{:S(2)}) collective-permute-start(bf16[4,16,1024]{2,1,0:T(8,128)(2,1)S(1)} %get-tuple-element.12), channel_id=1, source_target_pairs={{0,4},{4,8},{8,12},{12,0},{1,5},{5,9},{9,13},{13,1},{2,6},{6,10},{... | collective-permute-start | bytes 393224 | tf_op jit(solution)/shard_map/ppermute | solution.py:373
  30.9 87.4 %collective-permute-start.4 = (bf16[4,16,1024]{2,1,0:T(8,128)(2,1)S(1)}, bf16[4,16,1024]{2,1,0:T(8,128)(2,1)S(1)}, u32[]{:S(2)}, u32[]{:S(2)}) collective-permute-start(bf16[4,16,1024]{2,1,0:T(8,128)(2,1)S(1)} %get-tuple-element.13), channel_id=1, source_target_pairs={{0,8},{4,12},{8,0},{12,4},{1,9},{5,13},{9,1},{13,5},{2,10},{6,14},... | collective-permute-start | bytes 393224 | tf_op jit(solution)/shard_map/ppermute | solution.py:373
  33.6 84.7 %collective-permute-start.5 = (bf16[4,16,1024]{2,1,0:T(8,128)(2,1)S(1)}, bf16[4,16,1024]{2,1,0:T(8,128)(2,1)S(1)}, u32[]{:S(2)}, u32[]{:S(2)}) collective-permute-start(bf16[4,16,1024]{2,1,0:T(8,128)(2,1)S(1)} %get-tuple-element.14), channel_id=1, source_target_pairs={{0,12},{4,0},{8,4},{12,8},{1,13},{5,1},{9,5},{13,9},{2,14},{6,2},{... | collective-permute-start | bytes 393224 | tf_op jit(solution)/shard_map/ppermute | solution.py:373
  126.1 8.3 %collective-permute-start.6 = (bf16[64,1152]{1,0:T(8,128)(2,1)S(1)}, bf16[64,1152]{1,0:T(8,128)(2,1)S(1)}, u32[]{:S(2)}, u32[]{:S(2)}) collective-permute-start(bf16[64,1152]{1,0:T(8,128)(2,1)S(1)} %get-tuple-element.17), channel_id=1, source_target_pairs={{0,2},{1,3},{2,0},{3,1},{4,6},{5,7},{6,4},{7,5},{8,10},{9,11},{10,... | collective-permute-start | bytes 442376 | tf_op jit(solution)/shard_map/ppermute | solution.py:373
  129.4 7.2 %collective-permute-start.7 = (bf16[64,1152]{1,0:T(8,128)(2,1)S(1)}, bf16[64,1152]{1,0:T(8,128)(2,1)S(1)}, u32[]{:S(2)}, u32[]{:S(2)}) collective-permute-start(bf16[64,1152]{1,0:T(8,128)(2,1)S(1)} %get-tuple-element.18), channel_id=1, source_target_pairs={{0,1},{1,2},{2,3},{3,0},{4,5},{5,6},{6,7},{7,4},{8,9},{9,10},{10,1... | collective-permute-start | bytes 442376 | tf_op jit(solution)/shard_map/ppermute | solution.py:373
  130.0 6.5 %collective-permute-start.8 = (bf16[64,1152]{1,0:T(8,128)(2,1)S(1)}, bf16[64,1152]{1,0:T(8,128)(2,1)S(1)}, u32[]{:S(2)}, u32[]{:S(2)}) collective-permute-start(bf16[64,1152]{1,0:T(8,128)(2,1)S(1)} %get-tuple-element.19), channel_id=1, source_target_pairs={{0,3},{1,0},{2,1},{3,2},{4,7},{5,4},{6,5},{7,6},{8,11},{9,8},{10,9... | collective-permute-start | bytes 442376 | tf_op jit(solution)/shard_map/ppermute | solution.py:373
  136.7 7.4 %collective-permute-start.11 = (bf16[64,1024]{1,0:T(8,128)(2,1)S(1)}, bf16[64,1024]{1,0:T(8,128)(2,1)S(1)}, u32[]{:S(2)}, u32[]{:S(2)}) collective-permute-start(bf16[64,1024]{1,0:T(8,128)(2,1)S(1)} %update.1.refs_0_), channel_id=1, source_target_pairs={{0,1},{1,2},{2,3},{3,0},{4,5},{5,6},{6,7},{7,4},{8,9},{9,10},{10,1... | collective-permute-start | bytes 393224 | tf_op jit(solution)/shard_map/ppermute | solution.py:373
  138.1 8.4 %collective-permute-start.10 = (bf16[64,1024]{1,0:T(8,128)(2,1)S(1)}, bf16[64,1024]{1,0:T(8,128)(2,1)S(1)}, u32[]{:S(2)}, u32[]{:S(2)}) collective-permute-start(bf16[64,1024]{1,0:T(8,128)(2,1)S(1)} %update.1.refs_0_), channel_id=1, source_target_pairs={{0,2},{1,3},{2,0},{3,1},{4,6},{5,7},{6,4},{7,5},{8,10},{9,11},{10,... | collective-permute-start | bytes 393224 | tf_op jit(solution)/shard_map/ppermute | solution.py:373
  141.3 5.3 %collective-permute-start.9 = (bf16[64,1024]{1,0:T(8,128)(2,1)S(1)}, bf16[64,1024]{1,0:T(8,128)(2,1)S(1)}, u32[]{:S(2)}, u32[]{:S(2)}) collective-permute-start(bf16[64,1024]{1,0:T(8,128)(2,1)S(1)} %update.1.refs_0_), channel_id=1, source_target_pairs={{0,3},{1,0},{2,1},{3,2},{4,7},{5,4},{6,5},{7,6},{8,11},{9,8},{10,9... | collective-permute-start | bytes 393224 | tf_op jit(solution)/shard_map/ppermute | solution.py:373

commit v7 on v6

--- a/solution.py
+++ b/solution.py
@@ -156,6 +156,7 @@
     held, width = blocks[0].shape[-2:]
     cents = groups * held
     pieces = rows.shape[0]
+    tile = TILE // 2 if last else TILE
     if not last:
         for n in range(pieces):
             pltpu.make_async_copy(source.at[n], rows.at[n], sems.at[n]).start()
@@ -175,9 +176,9 @@
 
     def load(t):
         if not last:
-            for n in range(t * TILE, (t + 1) * TILE):
+            for n in range(t * tile, (t + 1) * tile):
                 pltpu.make_async_copy(source.at[n], rows.at[n], sems.at[n]).wait()
-        return rows[t * TILE : (t + 1) * TILE].reshape(-1, width)
+        return rows[t * tile : (t + 1) * tile].reshape(-1, width)
 
     def product(x):
         return lax.dot_general(
@@ -186,9 +187,9 @@
 
     x = load(0)
     raw = product(x)
-    for t in range(pieces // TILE):
+    for t in range(pieces // tile):
         now, members = raw, x
-        if (t + 1) * TILE < pieces:
+        if (t + 1) * tile < pieces:
             x = load(t + 1)
             raw = product(x)
         score = (now[:cents] - bias[...]) * SCORE_SCALE
@@ -212,7 +213,7 @@
         to_y = lax.rem(y_ref[0] + g, RING)
         for z in range(RING):
             span = pl.ds(g * held + z * shard, shard)
-            holder = z * RING + to_y
+            holder = to_y * RING + z
             outs[0][holder, :, :width] = total[span].astype(jnp.bfloat16)
             outs[0][holder, :, width:] = terms(mass[span], lane)
 
@@ -342,7 +343,7 @@
     for j in range(RING):
         total, mass = 0.0, 0.0
         for y in range(RING):
-            part = parts_ref[j * RING + y]
+            part = parts_ref[y * RING + j]
             total = total + part.astype(jnp.float32)
             mass = mass + lax.dot_general(
                 ones, part[:, width:], (((1,), (1,)), ((), ())), preferred_element_type=jnp.float32
@@ -391,7 +392,7 @@
     near, back, far = (shift(mine, "y", -d) for d in (1, 3, 2))
     blocks = [mine, near, far, back]
     (sums,) = cluster_sums(y, blocks, arrived, True)
-    new, mass = finish(exchange(sums, ("z", "y")))
+    new, mass = finish(exchange(sums, ("y", "z")))
     return new, mass
 
 

time: 171 us -> 171 us (level)
  no operation moved by 1% of the time
where the time goes in v7:
time: 171 us; the launch traced here: 168 us
  waiting for transfers between devices  97.6 us (57%)
  starting transfers between devices  30.9 us (18%)
  Pallas kernels  23.3 us (14%)
  blocking collectives  15.4 us (9%)
    ppermute x12, waiting for transfers between devices, shift(): return lax.ppermute(array, axis, [(i, (i + d) % RING) for i in range(RING)])  97.6 us
    ppermute x12, starting transfers between devices, shift(): return lax.ppermute(array, axis, [(i, (i + d) % RING) for i in range(RING)])  22.2 us
    all_to_all x1, blocking collectives, exchange(): return lax.all_to_all(array, axis, split_axis=0, concat_axis=0, tiled=True)  15.4 us
    pallas_call x2, Pallas kernels, cluster_sums(): pl.pallas_call(functools.partial(sums_kernel, groups, last), in_specs=[pl...  12.9 us
    pallas_call x1, Pallas kernels, scatter(): pl.pallas_call(functools.partial(scatter_kernel, capacity, where), in_spe...  9.43 us
    all_to_all x1, starting transfers between devices, exchange(): return lax.all_to_all(array, axis, split_axis=0, concat_axis=0, tiled=True)  8.66 us
  transfers between devices with their start and end apart: 13, of which 10 were waited for; matrix products, arithmetic and copies ran while one was open for 0% of the time, Pallas kernels for 0%

profile of v7, /device:TPU:2, one launch (start us, length us, event | category | flops | bytes accessed | tf_op | source)
XLA Modules:
  0.0 167.9 jit_solution(3484473686199260636)
XLA Ops:
  0.6 9.4 %scatter.1 = bf16[32,128,1024]{2,1,0:T(8,128)(2,1)} custom-call(s32[1,2048]{1,0:T(1,128)} %bitcast.4, s32[1,32]{1,0:T(1,128)} %bitcast.5, bf16[2048,1024]{1,0:T(8,128)(2,1)} %points_ref.1), custom_call_target="tpu_custom_call" | custom-call | flops 2097152 | bytes 50331648 | tf_op jit(solution)/shard_map/scatter/pallas_call | solution.py:121
  10.1 0.0 copy-start
  10.1 8.7 %all-to-all-start = ((bf16[32,128,1024]{2,1,0:T(8,128)(2,1)}), bf16[32,128,1024]{2,1,0:T(8,128)(2,1)}, u32[]{:S(2)}, u32[]{:S(2)}) async-start(bf16[32,128,1024]{2,1,0:T(8,128)(2,1)} %scatter.1), calls=%async_computation | async-start | bytes 16777216 | tf_op jit(solution)/shard_map/all_to_all | solution.py:370
  18.7 0.0 copy-done
  18.8 3.3 %collective-permute-start.1 = (bf16[4,16,1024]{2,1,0:T(8,128)(2,1)S(1)}, bf16[4,16,1024]{2,1,0:T(8,128)(2,1)S(1)}, u32[]{:S(2)}, u32[]{:S(2)}) collective-permute-start(bf16[4,16,1024]{2,1,0:T(8,128)(2,1)S(1)} %copy-done), channel_id=1, source_target_pairs={{0,2},{1,3},{2,0},{3,1},{4,6},{5,7},{6,4},{7,5},{8,10},{9,11},{10,... | collective-permute-start | bytes 393224 | tf_op jit(solution)/shard_map/ppermute | solution.py:374
  22.0 1.1 collective-permute-start
  23.1 1.0 collective-permute-start.2
  24.1 2.5 %collective-permute-done.1.refs_2_ = bf16[4,16,1024]{2,1,0:T(8,128)(2,1)S(1)} collective-permute-done((bf16[4,16,1024]{2,1,0:T(8,128)(2,1)S(1)}, bf16[4,16,1024]{2,1,0:T(8,128)(2,1)S(1)}, u32[]{:S(2)}, u32[]{:S(2)}) %collective-permute-start.1) | collective-permute-done | bytes 131104 | tf_op jit(solution)/shard_map/ppermute | solution.py:374
  26.5 2.5 %collective-permute-done.refs_1_ = bf16[4,16,1024]{2,1,0:T(8,128)(2,1)S(1)} collective-permute-done((bf16[4,16,1024]{2,1,0:T(8,128)(2,1)S(1)}, bf16[4,16,1024]{2,1,0:T(8,128)(2,1)S(1)}, u32[]{:S(2)}, u32[]{:S(2)}) %collective-permute-start) | collective-permute-done | bytes 131104 | tf_op jit(solution)/shard_map/ppermute | solution.py:374
  29.0 0.3 collective-permute-done.2.refs_3_
  29.3 1.5 collective-permute-start.3
  30.9 2.7 %collective-permute-start.4 = (bf16[4,16,1024]{2,1,0:T(8,128)(2,1)S(1)}, bf16[4,16,1024]{2,1,0:T(8,128)(2,1)S(1)}, u32[]{:S(2)}, u32[]{:S(2)}) collective-permute-start(bf16[4,16,1024]{2,1,0:T(8,128)(2,1)S(1)} %get-tuple-element.13), channel_id=1, source_target_pairs={{0,8},{4,12},{8,0},{12,4},{1,9},{5,13},{9,1},{13,5},{2,10},{6,14},... | collective-permute-start | bytes 393224 | tf_op jit(solution)/shard_map/ppermute | solution.py:374
  33.6 1.4 collective-permute-start.5
  35.0 76.2 %collective-permute-done.3.refs_1_ = bf16[4,16,1024]{2,1,0:T(8,128)(2,1)S(1)} collective-permute-done((bf16[4,16,1024]{2,1,0:T(8,128)(2,1)S(1)}, bf16[4,16,1024]{2,1,0:T(8,128)(2,1)S(1)}, u32[]{:S(2)}, u32[]{:S(2)}) %collective-permute-start.3) | collective-permute-done | bytes 131104 | tf_op jit(solution)/shard_map/ppermute | solution.py:374
  111.3 7.0 %collective-permute-done.4.refs_2_ = bf16[4,16,1024]{2,1,0:T(8,128)(2,1)S(1)} collective-permute-done((bf16[4,16,1024]{2,1,0:T(8,128)(2,1)S(1)}, bf16[4,16,1024]{2,1,0:T(8,128)(2,1)S(1)}, u32[]{:S(2)}, u32[]{:S(2)}) %collective-permute-start.4) | collective-permute-done | bytes 131104 | tf_op jit(solution)/shard_map/ppermute | solution.py:374
  118.3 0.0 collective-permute-done.5.refs_3_
  118.3 0.0 all-to-all-done.source
  118.3 7.7 %cluster_sums.2 = (bf16[32,128,1024]{2,1,0:T(8,128)(2,1)S(1)}, bf16[64,1152]{1,0:T(8,128)(2,1)S(1)}, bf16[64,1152]{1,0:T(8,128)(2,1)S(1)}, bf16[64,1152]{1,0:T(8,128)(2,1)S(1)}, bf16[64,1152]{1,0:T(8,128)(2,1)S(1)}) custom-call(s32[1]{0:T(128)} %bitcast.y_ref, bf16[32,128,1024]{2,1,0:T(8,128)(2,1)} %all-to-all-done.source, ...), custom_call_target="tpu_custom_call" | custom-call | flops 4294967296 | bytes 9437184 | tf_op jit(solution)/shard_map/cluster_sums/pallas_call | solution.py:237
  126.1 3.3 %collective-permute-start.6 = (bf16[64,1152]{1,0:T(8,128)(2,1)S(1)}, bf16[64,1152]{1,0:T(8,128)(2,1)S(1)}, u32[]{:S(2)}, u32[]{:S(2)}) collective-permute-start(bf16[64,1152]{1,0:T(8,128)(2,1)S(1)} %get-tuple-element.17), channel_id=1, source_target_pairs={{0,2},{1,3},{2,0},{3,1},{4,6},{5,7},{6,4},{7,5},{8,10},{9,11},{10,... | collective-permute-start | bytes 442376 | tf_op jit(solution)/shard_map/ppermute | solution.py:374
  129.4 0.7 collective-permute-start.7
  130.0 2.6 %collective-permute-start.8 = (bf16[64,1152]{1,0:T(8,128)(2,1)S(1)}, bf16[64,1152]{1,0:T(8,128)(2,1)S(1)}, u32[]{:S(2)}, u32[]{:S(2)}) collective-permute-start(bf16[64,1152]{1,0:T(8,128)(2,1)S(1)} %get-tuple-element.19), channel_id=1, source_target_pairs={{0,3},{1,0},{2,1},{3,2},{4,7},{5,4},{6,5},{7,6},{8,11},{9,8},{10,9... | collective-permute-start | bytes 442376 | tf_op jit(solution)/shard_map/ppermute | solution.py:374
  132.6 1.7 %collective-permute-done.6.refs_1_ = bf16[64,1152]{1,0:T(8,128)(2,1)S(1)} collective-permute-done((bf16[64,1152]{1,0:T(8,128)(2,1)S(1)}, bf16[64,1152]{1,0:T(8,128)(2,1)S(1)}, u32[]{:S(2)}, u32[]{:S(2)}) %collective-permute-start.6) | collective-permute-done | bytes 147488 | tf_op jit(solution)/shard_map/ppermute | solution.py:374
  134.3 2.2 %collective-permute-done.7.refs_2_ = bf16[64,1152]{1,0:T(8,128)(2,1)S(1)} collective-permute-done((bf16[64,1152]{1,0:T(8,128)(2,1)S(1)}, bf16[64,1152]{1,0:T(8,128)(2,1)S(1)}, u32[]{:S(2)}, u32[]{:S(2)}) %collective-permute-start.7) | collective-permute-done | bytes 147488 | tf_op jit(solution)/shard_map/ppermute | solution.py:374
  136.6 0.0 collective-permute-done.8.refs_3_
  136.6 0.1 update.1.refs_0_
  136.7 1.4 collective-permute-start.11
  138.1 3.1 %collective-permute-start.10 = (bf16[64,1024]{1,0:T(8,128)(2,1)S(1)}, bf16[64,1024]{1,0:T(8,128)(2,1)S(1)}, u32[]{:S(2)}, u32[]{:S(2)}) collective-permute-start(bf16[64,1024]{1,0:T(8,128)(2,1)S(1)} %update.1.refs_0_), channel_id=1, source_target_pairs={{0,2},{1,3},{2,0},{3,1},{4,6},{5,7},{6,4},{7,5},{8,10},{9,11},{10,... | collective-permute-start | bytes 393224 | tf_op jit(solution)/shard_map/ppermute | solution.py:374
  141.3 0.2 collective-permute-start.9
  141.4 2.7 %collective-permute-done.11.refs_3_ = bf16[64,1024]{1,0:T(8,128)(2,1)S(1)} collective-permute-done((bf16[64,1024]{1,0:T(8,128)(2,1)S(1)}, bf16[64,1024]{1,0:T(8,128)(2,1)S(1)}, u32[]{:S(2)}, u32[]{:S(2)}) %collective-permute-start.11) | collective-permute-done | bytes 131104 | tf_op jit(solution)/shard_map/ppermute | solution.py:374
  144.1 2.4 %collective-permute-done.10.refs_2_ = bf16[64,1024]{1,0:T(8,128)(2,1)S(1)} collective-permute-done((bf16[64,1024]{1,0:T(8,128)(2,1)S(1)}, bf16[64,1024]{1,0:T(8,128)(2,1)S(1)}, u32[]{:S(2)}, u32[]{:S(2)}) %collective-permute-start.10) | collective-permute-done | bytes 131104 | tf_op jit(solution)/shard_map/ppermute | solution.py:374
  146.5 0.1 collective-permute-done.9.refs_1_
  146.6 5.2 %cluster_sums.3 = bf16[16,16,1152]{2,1,0:T(8,128)(2,1)S(1)} custom-call(s32[1]{0:T(128)} %bitcast.y_ref, bf16[32,128,1024]{2,1,0:T(8,128)(2,1)S(1)} %get-tuple-element.15.source, bf16[64,1024]{1,0:T(8,128)(2,1)S(1)} %update.1.refs_0_, bf16[64,1024]{1,0:T(8,128)(2,1)S(1)} %collective-permute-done.9.refs_1_, ...), custom_call_target="tpu_custom_call" | custom-call | flops 4294967296 | bytes 9437184 | tf_op jit(solution)/shard_map/cluster_sums/pallas_call | solution.py:237
  151.7 15.4 %all_to_all.10.parts_ref = bf16[16,16,1152]{2,1,0:T(8,128)(2,1)S(1)} all-to-all(bf16[16,16,1152]{2,1,0:T(8,128)(2,1)S(1)} %cluster_sums.3), channel_id=1, replica_groups=mesh['x'=4,'core'=2,'z'=4,'y'=4] {'y','z'}, dimensions={0} | all-to-all | bytes 1179648 | tf_op jit(solution)/shard_map/all_to_all | solution.py:370
  167.1 0.8 finish.1
  (2 shorter events, 0.1 us)
Async XLA Ops:
  10.1 8.7 %copy-start = (bf16[4,16,1024]{2,1,0:T(8,128)(2,1)S(1)}, bf16[4,16,1024]{2,1,0:T(8,128)(2,1)}, u32[]{:S(2)}) copy-start(bf16[4,16,1024]{2,1,0:T(8,128)(2,1)} %refs_0_.1) | copy-start | bytes 393220
  10.1 108.2 %all-to-all-start = ((bf16[32,128,1024]{2,1,0:T(8,128)(2,1)}), bf16[32,128,1024]{2,1,0:T(8,128)(2,1)}, u32[]{:S(2)}, u32[]{:S(2)}) async-start(bf16[32,128,1024]{2,1,0:T(8,128)(2,1)} %scatter.1), calls=%async_computation | async-start | bytes 16777216 | tf_op jit(solution)/shard_map/all_to_all | solution.py:370
  18.8 7.8 %collective-permute-start.1 = (bf16[4,16,1024]{2,1,0:T(8,128)(2,1)S(1)}, bf16[4,16,1024]{2,1,0:T(8,128)(2,1)S(1)}, u32[]{:S(2)}, u32[]{:S(2)}) collective-permute-start(bf16[4,16,1024]{2,1,0:T(8,128)(2,1)S(1)} %copy-done), channel_id=1, source_target_pairs={{0,2},{1,3},{2,0},{3,1},{4,6},{5,7},{6,4},{7,5},{8,10},{9,11},{10,... | collective-permute-start | bytes 393224 | tf_op jit(solution)/shard_map/ppermute | solution.py:374
  22.0 7.0 %collective-permute-start = (bf16[4,16,1024]{2,1,0:T(8,128)(2,1)S(1)}, bf16[4,16,1024]{2,1,0:T(8,128)(2,1)S(1)}, u32[]{:S(2)}, u32[]{:S(2)}) collective-permute-start(bf16[4,16,1024]{2,1,0:T(8,128)(2,1)S(1)} %copy-done), channel_id=1, source_target_pairs={{0,3},{1,0},{2,1},{3,2},{4,7},{5,4},{6,5},{7,6},{8,11},{9,8},{10,9... | collective-permute-start | bytes 393224 | tf_op jit(solution)/shard_map/ppermute | solution.py:374
  23.1 6.2 %collective-permute-start.2 = (bf16[4,16,1024]{2,1,0:T(8,128)(2,1)S(1)}, bf16[4,16,1024]{2,1,0:T(8,128)(2,1)S(1)}, u32[]{:S(2)}, u32[]{:S(2)}) collective-permute-start(bf16[4,16,1024]{2,1,0:T(8,128)(2,1)S(1)} %copy-done), channel_id=1, source_target_pairs={{0,1},{1,2},{2,3},{3,0},{4,5},{5,6},{6,7},{7,4},{8,9},{9,10},{10,1... | collective-permute-start | bytes 393224 | tf_op jit(solution)/shard_map/ppermute | solution.py:374
  29.3 81.9 %collective-permute-start.3 = (bf16[4,16,1024]{2,1,0:T(8,128)(2,1)S(1)}, bf16[4,16,1024]{2,1,0:T(8,128)(2,1)S(1)}, u32[]{:S(2)}, u32[]{:S(2)}) collective-permute-start(bf16[4,16,1024]{2,1,0:T(8,128)(2,1)S(1)} %get-tuple-element.12), channel_id=1, source_target_pairs={{0,4},{4,8},{8,12},{12,0},{1,5},{5,9},{9,13},{13,1},{2,6},{6,10},{... | collective-permute-start | bytes 393224 | tf_op jit(solution)/shard_map/ppermute | solution.py:374
  30.9 87.4 %collective-permute-start.4 = (bf16[4,16,1024]{2,1,0:T(8,128)(2,1)S(1)}, bf16[4,16,1024]{2,1,0:T(8,128)(2,1)S(1)}, u32[]{:S(2)}, u32[]{:S(2)}) collective-permute-start(bf16[4,16,1024]{2,1,0:T(8,128)(2,1)S(1)} %get-tuple-element.13), channel_id=1, source_target_pairs={{0,8},{4,12},{8,0},{12,4},{1,9},{5,13},{9,1},{13,5},{2,10},{6,14},... | collective-permute-start | bytes 393224 | tf_op jit(solution)/shard_map/ppermute | solution.py:374
  33.6 84.7 %collective-permute-start.5 = (bf16[4,16,1024]{2,1,0:T(8,128)(2,1)S(1)}, bf16[4,16,1024]{2,1,0:T(8,128)(2,1)S(1)}, u32[]{:S(2)}, u32[]{:S(2)}) collective-permute-start(bf16[4,16,1024]{2,1,0:T(8,128)(2,1)S(1)} %get-tuple-element.14), channel_id=1, source_target_pairs={{0,12},{4,0},{8,4},{12,8},{1,13},{5,1},{9,5},{13,9},{2,14},{6,2},{... | collective-permute-start | bytes 393224 | tf_op jit(solution)/shard_map/ppermute | solution.py:374
  126.1 8.3 %collective-permute-start.6 = (bf16[64,1152]{1,0:T(8,128)(2,1)S(1)}, bf16[64,1152]{1,0:T(8,128)(2,1)S(1)}, u32[]{:S(2)}, u32[]{:S(2)}) collective-permute-start(bf16[64,1152]{1,0:T(8,128)(2,1)S(1)} %get-tuple-element.17), channel_id=1, source_target_pairs={{0,2},{1,3},{2,0},{3,1},{4,6},{5,7},{6,4},{7,5},{8,10},{9,11},{10,... | collective-permute-start | bytes 442376 | tf_op jit(solution)/shard_map/ppermute | solution.py:374
  129.4 7.2 %collective-permute-start.7 = (bf16[64,1152]{1,0:T(8,128)(2,1)S(1)}, bf16[64,1152]{1,0:T(8,128)(2,1)S(1)}, u32[]{:S(2)}, u32[]{:S(2)}) collective-permute-start(bf16[64,1152]{1,0:T(8,128)(2,1)S(1)} %get-tuple-element.18), channel_id=1, source_target_pairs={{0,1},{1,2},{2,3},{3,0},{4,5},{5,6},{6,7},{7,4},{8,9},{9,10},{10,1... | collective-permute-start | bytes 442376 | tf_op jit(solution)/shard_map/ppermute | solution.py:374
  130.0 6.5 %collective-permute-start.8 = (bf16[64,1152]{1,0:T(8,128)(2,1)S(1)}, bf16[64,1152]{1,0:T(8,128)(2,1)S(1)}, u32[]{:S(2)}, u32[]{:S(2)}) collective-permute-start(bf16[64,1152]{1,0:T(8,128)(2,1)S(1)} %get-tuple-element.19), channel_id=1, source_target_pairs={{0,3},{1,0},{2,1},{3,2},{4,7},{5,4},{6,5},{7,6},{8,11},{9,8},{10,9... | collective-permute-start | bytes 442376 | tf_op jit(solution)/shard_map/ppermute | solution.py:374
  136.7 7.4 %collective-permute-start.11 = (bf16[64,1024]{1,0:T(8,128)(2,1)S(1)}, bf16[64,1024]{1,0:T(8,128)(2,1)S(1)}, u32[]{:S(2)}, u32[]{:S(2)}) collective-permute-start(bf16[64,1024]{1,0:T(8,128)(2,1)S(1)} %update.1.refs_0_), channel_id=1, source_target_pairs={{0,1},{1,2},{2,3},{3,0},{4,5},{5,6},{6,7},{7,4},{8,9},{9,10},{10,1... | collective-permute-start | bytes 393224 | tf_op jit(solution)/shard_map/ppermute | solution.py:374
  138.1 8.4 %collective-permute-start.10 = (bf16[64,1024]{1,0:T(8,128)(2,1)S(1)}, bf16[64,1024]{1,0:T(8,128)(2,1)S(1)}, u32[]{:S(2)}, u32[]{:S(2)}) collective-permute-start(bf16[64,1024]{1,0:T(8,128)(2,1)S(1)} %update.1.refs_0_), channel_id=1, source_target_pairs={{0,2},{1,3},{2,0},{3,1},{4,6},{5,7},{6,4},{7,5},{8,10},{9,11},{10,... | collective-permute-start | bytes 393224 | tf_op jit(solution)/shard_map/ppermute | solution.py:374
  141.3 5.3 %collective-permute-start.9 = (bf16[64,1024]{1,0:T(8,128)(2,1)S(1)}, bf16[64,1024]{1,0:T(8,128)(2,1)S(1)}, u32[]{:S(2)}, u32[]{:S(2)}) collective-permute-start(bf16[64,1024]{1,0:T(8,128)(2,1)S(1)} %update.1.refs_0_), channel_id=1, source_target_pairs={{0,3},{1,0},{2,1},{3,2},{4,7},{5,4},{6,5},{7,6},{8,11},{9,8},{10,9... | collective-permute-start | bytes 393224 | tf_op jit(solution)/shard_map/ppermute | solution.py:374
